TPU v7x, 32 devices: a whole 2x2x4 slice. The times are simulated.
32 devices in a mesh: dom: 8 (over z, y), rep: 4 (over x, core).
Axes of the slice: x: 2, y: 2, z: 4, core: 2. Of those that a mesh axis runs over, the one named last changes fastest.
Arguments:
- features: bfloat16 [12288, 256], P('dom'), may hold values from -6 to 6
- tile_weights: bfloat16 [8, 4, 2, 88, 128, 128], P('dom', 'rep'), may hold values from 0 to 0.023071289
- tile_rows: int32 [8, 4, 2, 88], P('dom', 'rep'), may hold values from 0 to 11, as said below
- tile_cols: int32 [8, 4, 2, 88], P('dom', 'rep'), may hold values from 0 to 11, as said below
- tile_counts: int32 [8, 4, 2], P('dom', 'rep'), may hold values from 1 to 88, as said below
- weight_self: bfloat16 [256, 256], replicated, may hold values from -0.375 to 0.375
- weight_neigh: bfloat16 [256, 256], replicated, may hold values from -0.375 to 0.375
- cotangent: bfloat16 [12288, 256], P(('dom', 'rep')), may hold values from -0.053955078 to 0.053955078
Outputs:
- out: bfloat16 [12288, 256], P(('dom', 'rep'))
- grad_self: float32 [256, 256], replicated
- grad_neigh: float32 [256, 256], replicated
Inputs may be any that keep to these rules, and one draw needn't show every extreme that they name: For each p, r, s the first tile_counts[p, r, s] slots name distinct pairs (tile_rows, tile_cols); slots from tile_counts[p, r, s] on are unused. `tile_cols`: see tile_rows. `tile_counts`: some device fills all 88 slots of some column step.
All inputs are finite; a program needn't handle non-finite values.
Results may differ from a plain program's by a relative error of at most 0.0052.
Values may be sent and summed in bfloat16 or wider, within the bound.
No kernel may reach another device: no remote copies, remote signals or barrier semaphores. Data moves between devices by JAX's collectives and lax.ppermute only.
A program may use at most 128 MiB of HBM per device.

v0:
```python
import jax
import jax.numpy as jnp
from jax import lax
from jax.sharding import PartitionSpec as P


def passed_along(block, axis, distance):
    devices = range(lax.axis_size(axis))
    route = [((i - distance) % len(devices), i) for i in devices]
    return lax.ppermute(block, axis, route)


def step_terms(feature_block, weights_dev, rows_dev, cols_dev, counts_dev, column_step):
    weights_now = lax.dynamic_index_in_dim(weights_dev, column_step, 0, keepdims=False)
    row_index = lax.dynamic_index_in_dim(rows_dev, column_step, 0, keepdims=False)
    col_index = lax.dynamic_index_in_dim(cols_dev, column_step, 0, keepdims=False)
    live_total = lax.dynamic_index_in_dim(counts_dev, column_step, 0, keepdims=False)
    slot_total = weights_now.shape[0]
    tile_side = weights_now.shape[1]
    width = feature_block.shape[1]
    row_tiles = feature_block.shape[0] // tile_side
    flat_block = feature_block.reshape(row_tiles, tile_side * width)
    tile_ids = jnp.arange(row_tiles, dtype=jnp.int32)
    select = (col_index[:, None] == tile_ids[None, :]).astype(jnp.bfloat16)
    picked = jnp.dot(select, flat_block, preferred_element_type=jnp.float32).astype(jnp.bfloat16)
    picked = picked.reshape(slot_total, tile_side, width)
    product = jnp.einsum("kij,kjf->kif", weights_now, picked, preferred_element_type=jnp.float32)
    live_slots = jnp.arange(slot_total, dtype=jnp.int32) < live_total
    placing = ((row_index[None, :] == tile_ids[:, None]) & live_slots[None, :]).astype(jnp.float32)
    summed = jnp.dot(
        placing,
        product.reshape(slot_total, tile_side * width),
        precision=lax.Precision.HIGHEST,
        preferred_element_type=jnp.float32,
    )
    return summed.reshape(feature_block.shape[0], width)


def rotate(feature_block, steps_per_group, direction_sign):
    replica = lax.axis_index("rep")
    bit_total = (lax.axis_size("rep") - 1).bit_length()
    domain = lax.axis_size("dom")
    moves = []
    for bit_number in range(bit_total):
        moves.append((direction_sign * steps_per_group * (1 << bit_number) % domain, bit_number))
    for amount, bit_number in moves:
        shifted = passed_along(feature_block, "dom", amount)
        flag = replica >> bit_number & 1 == 1
        feature_block = jnp.where(flag, shifted, feature_block)
    return feature_block


def move_up(feature_block):
    return passed_along(feature_block, "dom", -1)


def move_down(feature_block):
    return passed_along(feature_block, "dom", 1)


def on_device(
    features, tile_weights, tile_rows, tile_cols, tile_counts, weight_self, weight_neigh, cotangent
):
    weights_dev = tile_weights[0, 0]
    rows_dev = tile_rows[0, 0]
    cols_dev = tile_cols[0, 0]
    counts_dev = tile_counts[0, 0]
    steps_per_group = weights_dev.shape[0]
    middle = steps_per_group // 2

    def contribution(feature_block, column_step):
        return step_terms(feature_block, weights_dev, rows_dev, cols_dev, counts_dev, column_step)

    empty = jnp.zeros(features.shape, jnp.float32)
    center = rotate(features, steps_per_group, -1)

    def turn_both(turn_index, carry):
        upper, lower, partial_value = carry
        partial_value = partial_value + contribution(upper, middle + turn_index)
        partial_value = partial_value + contribution(lower, middle - 1 - turn_index)
        return (move_up(upper), move_down(lower), partial_value)

    upper, lower, partial_value = lax.fori_loop(
        0, middle - 1, turn_both, (center, move_down(center), empty)
    )
    partial_value = partial_value + contribution(upper, 2 * middle - 1) + contribution(lower, 0)
    aggregate = lax.psum_scatter(partial_value, "rep", scatter_dimension=0, tiled=True).astype(
        jnp.bfloat16
    )
    quarter = features.shape[0] // lax.axis_size("rep")
    own_rows = lax.dynamic_slice_in_dim(features, lax.axis_index("rep") * quarter, quarter, 0)
    pre = jnp.dot(own_rows, weight_self, preferred_element_type=jnp.float32)
    pre = pre + jnp.dot(aggregate, weight_neigh, preferred_element_type=jnp.float32)
    output = jax.nn.silu(pre).astype(jnp.bfloat16)
    sigmoid = jax.nn.sigmoid(pre)
    slope = (cotangent.astype(jnp.float32) * sigmoid * (1.0 + pre * (1.0 - sigmoid))).astype(
        jnp.bfloat16
    )
    self_term = jnp.einsum("nf,ng->fg", own_rows, slope, preferred_element_type=jnp.float32)
    neigh_term = jnp.einsum("nf,ng->fg", aggregate, slope, preferred_element_type=jnp.float32)
    grad_self, grad_neigh = lax.psum((self_term, neigh_term), ("dom", "rep"))
    return (output, grad_self, grad_neigh)


def solution(mesh):
    return jax.shard_map(
        on_device,
        mesh=mesh,
        in_specs=(
            P("dom", None),
            P("dom", "rep", None, None, None, None),
            P("dom", "rep", None, None),
            P("dom", "rep", None, None),
            P("dom", "rep", None),
            P(),
            P(),
            P(("dom", "rep"), None),
        ),
        out_specs=(P(("dom", "rep"), None), P(), P()),
        check_vma=False,
    )
```

profile of v0, /device:TPU:0, one launch (start us, length us, event | category | flops | bytes accessed | tf_op | source)
XLA Modules:
  0.0 302.9 jit_solution(4750643534882592636)
XLA Ops:
  7.2 0.0 copy-start
  7.2 0.0 reduce-scatter.2.cloned.1.call-start
  7.2 5.1 %collective-permute-start = (bf16[1536,256]{1,0:T(8,128)(2,1)}, bf16[1536,256]{1,0:T(8,128)(2,1)S(1)}, u32[]{:S(2)}, u32[]{:S(2)}) collective-permute-start(bf16[1536,256]{1,0:T(8,128)(2,1)} %param.8), channel_id=1, source_target_pairs={{8,0},{12,4},{16,8},{20,12},{24,16},{28,20},{0,24},{4,28},{9,1},{1... | collective-permute-start | bytes 2359304 | tf_op jit(solution)/shard_map/ppermute | solution.py:10
  12.3 17.1 %collective-permute-done = bf16[1536,256]{1,0:T(8,128)(2,1)S(1)} collective-permute-done((bf16[1536,256]{1,0:T(8,128)(2,1)}, bf16[1536,256]{1,0:T(8,128)(2,1)S(1)}, u32[]{:S(2)}, u32[]{:S(2)}) %collective-permute-start) | collective-permute-done | bytes 786464 | tf_op jit(solution)/shard_map/ppermute | solution.py:10
  29.4 1.2 broadcast_select_fusion
  30.7 1.4 collective-permute-start.1
  32.1 1.3 fusion.24
  33.4 0.6 iota_compare_fusion.7
  34.1 0.7 iota_compare_fusion.6
  34.7 0.8 slice_bitcast_fusion
  35.5 0.8 slice_bitcast_fusion.1
  36.2 29.5 %collective-permute-done.1 = bf16[1536,256]{1,0:T(8,128)(2,1)S(1)} collective-permute-done((bf16[1536,256]{1,0:T(8,128)(2,1)S(1)}, bf16[1536,256]{1,0:T(8,128)(2,1)S(1)}, u32[]{:S(2)}, u32[]{:S(2)}) %collective-permute-start.1) | collective-permute-done | bytes 786464 | tf_op jit(solution)/shard_map/ppermute | solution.py:10
  65.8 0.1 broadcast_select_fusion.1
  65.8 0.5 reshape.55
  66.4 1.6 collective-permute-start.2
  68.0 0.0 slice-start
  68.0 1.7 convolution_convert_fusion.1
  69.6 0.0 slice-start.1
  69.7 1.5 copy.19
  71.2 0.0 slice-done
  71.2 0.0 slice-done.1
  71.2 5.4 %convolution_bitcast_fusion.1 = f32[88,128,256]{1,2,0:T(8,128)} fusion(bf16[88,128,256]{2,1,0:T(8,128)(2,1)S(1)} %bitcast.46, bf16[1,1,2,88,128,128]{5,4,3,2,1,0:T(8,128)(2,1)S(1)} %bitcast.49), kind=kOutput, calls=%fused_computation.4 | convolution fusion | flops 738197504 | bytes 20185088 | tf_op jit(solution)/shard_map/kij,kjf->kif/dot_general | solution.py:27
  76.6 12.2 %copy.20 = f32[11,8,128,256]{3,1,2,0:T(8,128)} copy(f32[11,8,128,256]{2,3,1,0:T(8,128)} %bitcast.42) | data formatting | bytes 23068672
  88.8 8.0 %fusion.14 = f32[12,32768]{1,0:T(8,128)} fusion(f32[88,32768]{1,0:T(8,128)} %bitcast.41, s32[88]{0:T(128)S(1)} %get-tuple-element.8, pred[88]{0:T(512)(128)(4,1)S(1)} %iota_compare_fusion.7), kind=kOutput, calls=%fused_computation.29 | convolution fusion | flops 415238208 | bytes 13107640 | tf_op jit(solution)/shard_map/dot_general | solution.py:30
  96.9 0.0 collective-permute-done.2
  96.9 1.6 reshape.58
  98.4 0.0 slice-start.2
  98.4 1.7 convolution_convert_fusion
  100.1 0.0 slice-start.3
  100.2 1.5 copy.21
  101.7 0.0 slice-done.2
  101.7 0.0 slice-done.3
  101.7 5.2 %convolution_bitcast_fusion = f32[88,128,256]{1,2,0:T(8,128)} fusion(bf16[88,128,256]{2,1,0:T(8,128)(2,1)S(1)} %bitcast.47, bf16[1,1,2,88,128,128]{5,4,3,2,1,0:T(8,128)(2,1)S(1)} %bitcast.51), kind=kOutput, calls=%fused_computation.3 | convolution fusion | flops 738197504 | bytes 20185088 | tf_op jit(solution)/shard_map/kij,kjf->kif/dot_general | solution.py:27
  106.9 12.2 %copy.22 = f32[11,8,128,256]{3,1,2,0:T(8,128)} copy(f32[11,8,128,256]{2,3,1,0:T(8,128)} %bitcast.43) | data formatting | bytes 23068672
  119.1 0.0 copy-start.1
  119.1 0.0 copy-start.2
  119.1 8.9 %convolution_add_fusion = f32[12,32768]{1,0:T(8,128)S(1)} fusion(f32[12,32768]{1,0:T(8,128)} %fusion.14, f32[88,32768]{1,0:T(8,128)} %bitcast.40, s32[88]{0:T(128)S(1)} %get-tuple-element.7, pred[88]{0:T(512)(128)(4,1)S(1)} %iota_compare_fusion.6), kind=kOutput, calls=%fused_computation.2 | convolution fusion | flops 415631424 | bytes 14680504 | tf_op jit(solution)/shard_map/dot_general | solution.py:30
  128.1 0.0 copy-start.3
  128.1 1.4 add.39
  129.4 0.0 reduce-scatter.2.cloned.1.call-update
  129.5 0.0 all-reduce.3.cloned.1.call-start
  129.5 0.0 copy-done.1
  129.5 0.0 copy-done.2
  129.5 0.2 fusion.6
  129.7 27.9 %reduce-scatter.2.cloned.1.call-done = f32[384,256]{1,0:T(8,128)} async-done(((f32[1536,256]{1,0:T(8,128)}), f32[384,256]{1,0:T(8,128)}) %reduce-scatter.2.cloned.1.call-update) | async-done | bytes 393232 | tf_op jit(solution)/shard_map/reduce_scatter | solution.py:87
  157.7 0.0 copy-done
  157.7 0.0 copy-done.3
  157.7 2.0 multiply_convert_fusion
  159.7 1.0 fusion.4
  160.7 2.0 fusion.8
  162.7 0.0 all-reduce.3.cloned.1.call-update
  162.7 130.1 %all-reduce.3.cloned.1.call-done = (f32[256,256]{1,0:T(8,128)}, f32[256,256]{1,0:T(8,128)}) async-done(((f32[256,256]{1,0:T(8,128)}, f32[256,256]{1,0:T(8,128)}), (f32[256,256]{1,0:T(8,128)}, f32[256,256]{1,0:T(8,128)})) %all-reduce.3.cloned.1.call-update) | async-done | bytes 524304 | tf_op jit(solution)/shard_map/psum | solution.py:101
  292.8 1.7 copy.27
  294.4 1.7 copy.28
  (2 shorter events, 0.0 us)
Async XLA Ops:
  7.2 150.5 %copy-start = (bf16[256,256]{1,0:T(8,128)(2,1)S(1)}, bf16[256,256]{1,0:T(8,128)(2,1)}, u32[]{:S(2)}) copy-start(bf16[256,256]{1,0:T(8,128)(2,1)} %param.14) | copy-start | bytes 393220
  7.2 150.5 %reduce-scatter.2.cloned.1.call-start = ((), (), s32[]{:S(2)}) async-start(), calls=%async_computation.1 | async-start | bytes 1966080 | tf_op jit(solution)/shard_map/reduce_scatter | solution.py:87
  7.2 22.2 %collective-permute-start = (bf16[1536,256]{1,0:T(8,128)(2,1)}, bf16[1536,256]{1,0:T(8,128)(2,1)S(1)}, u32[]{:S(2)}, u32[]{:S(2)}) collective-permute-start(bf16[1536,256]{1,0:T(8,128)(2,1)} %param.8), channel_id=1, source_target_pairs={{8,0},{12,4},{16,8},{20,12},{24,16},{28,20},{0,24},{4,28},{9,1},{1... | collective-permute-start | bytes 2359304 | tf_op jit(solution)/shard_map/ppermute | solution.py:10
  30.7 35.1 %collective-permute-start.1 = (bf16[1536,256]{1,0:T(8,128)(2,1)S(1)}, bf16[1536,256]{1,0:T(8,128)(2,1)S(1)}, u32[]{:S(2)}, u32[]{:S(2)}) collective-permute-start(bf16[1536,256]{1,0:T(8,128)(2,1)S(1)} %broadcast_select_fusion), channel_id=1, source_target_pairs={{16,0},{20,4},{24,8},{28,12},{0,16},{4,20},{8,24},{12,28},{17,1},{... | collective-permute-start | bytes 2359304 | tf_op jit(solution)/shard_map/ppermute | solution.py:10
  66.4 30.5 %collective-permute-start.2 = (bf16[1536,256]{1,0:T(8,128)(2,1)S(1)}, bf16[1536,256]{1,0:T(8,128)(2,1)}, u32[]{:S(2)}, u32[]{:S(2)}) collective-permute-start(bf16[1536,256]{1,0:T(8,128)(2,1)S(1)} %broadcast_select_fusion.1), channel_id=1, source_target_pairs={{28,0},{0,4},{4,8},{8,12},{12,16},{16,20},{20,24},{24,28},{29,1},{... | collective-permute-start | bytes 2359304 | tf_op jit(solution)/shard_map/ppermute | solution.py:10
  68.0 3.2 %slice-start = ((s8[5767168]{0:T(1024)(128)(4,1)}), s8[4194304]{0:T(1024)(128)(4,1)S(1)}, s32[]{:S(2)}) async-start(s8[5767168]{0:T(1024)(128)(4,1)} %bitcast.48), calls=%async_computation.3 | async-start | bytes 8388608
  69.6 1.6 slice-start.1
  98.4 3.3 %slice-start.2 = ((s8[5767168]{0:T(1024)(128)(4,1)}), s8[4194304]{0:T(1024)(128)(4,1)S(1)}, s32[]{:S(2)}) async-start(s8[5767168]{0:T(1024)(128)(4,1)} %bitcast.50), calls=%async_computation.5 | async-start | bytes 8388608
  100.1 1.6 slice-start.3
  119.1 10.4 %copy-start.1 = (bf16[1536,256]{1,0:T(8,128)(2,1)S(1)}, bf16[1536,256]{1,0:T(8,128)(2,1)}, u32[]{:S(2)}) copy-start(bf16[1536,256]{1,0:T(8,128)(2,1)} %param.8) | copy-start | bytes 2359300
  119.1 10.4 %copy-start.2 = (bf16[256,256]{1,0:T(8,128)(2,1)S(1)}, bf16[256,256]{1,0:T(8,128)(2,1)}, u32[]{:S(2)}) copy-start(bf16[256,256]{1,0:T(8,128)(2,1)} %param.13) | copy-start | bytes 393220
  128.1 29.6 %copy-start.3 = (bf16[384,256]{1,0:T(8,128)(2,1)S(1)}, bf16[384,256]{1,0:T(8,128)(2,1)}, u32[]{:S(2)}) copy-start(bf16[384,256]{1,0:T(8,128)(2,1)} %param.15) | copy-start | bytes 589828
  129.5 163.3 %all-reduce.3.cloned.1.call-start = ((), (), s32[]{:S(2)}) async-start(), calls=%async_computation.2 | async-start | bytes 1048576 | tf_op jit(solution)/shard_map/psum | solution.py:101
Sparse Core Ops, SparseCore 0:
  129.6 28.0 reduce-scatter.1
  164.6 128.0 all-reduce.2
where the time goes:
time: 304 us; the launch traced here: 303 us
  waiting for transfers between devices  205 us (67%)
  local copies, waits for them, and re-layouts  37.1 us (12%)
  matrix products  36.1 us (12%)
  between operations  14.2 us (5%)
  starting transfers between devices  8.18 us (3%)
    psum x1, waiting for transfers between devices, on_device(): grad_self, grad_neigh = lax.psum((self_term, neigh_term), ('dom', 'rep'))  130 us
    ppermute x3, waiting for transfers between devices, passed_along(): return lax.ppermute(block, axis, route)  46.6 us
    unnamed x22, local copies, waits for them, and re-layouts  30.9 us
    reduce_scatter x1, waiting for transfers between devices, on_device(): lax.psum_scatter(partial_value, 'rep', scatter_dimension=0, tiled=True)  27.9 us
    dot_general x2, matrix products, step_terms(): jnp.dot(placing, product.reshape(slot_total, tile_side * width), precisio...  17 us
    dot_general x2, matrix products, step_terms(): jnp.einsum('kij,kjf->kif', weights_now, picked, preferred_element_type=jn...  10.6 us
    ppermute x3, starting transfers between devices, passed_along(): return lax.ppermute(block, axis, route)  8.1 us
  transfers between devices with their start and end apart: 5, of which 4 were waited for; matrix products, arithmetic and copies ran while one was open for 11% of the time, Pallas kernels for 0%

commit v1 on v0

v1 whole, which is shorter than its diff:
```python
import functools

import jax
import jax.numpy as jnp
from jax import lax
from jax.experimental import pallas as pl
from jax.experimental.pallas import tpu as pltpu
from jax.sharding import PartitionSpec as P

AXES = ("dom", "rep")
F32, BF16 = jnp.float32, jnp.bfloat16
MIB = 1 << 20


def flat_permute(value, blocks, groups, source):
    route = []
    for p in range(blocks):
        for r in range(groups):
            q, g = source(p, r)
            route.append((q % blocks * groups + g % groups, p * groups + r))
    return lax.ppermute(value, AXES, route)


def rep_exchange(value, groups, bit):
    route = [(r, r ^ (1 << bit)) for r in range(groups)]
    return lax.ppermute(value, "rep", route)


def fetch_blocks(features, blocks, groups, steps):
    found = []
    for s in range(steps):
        flip = groups // 2 if s % 2 else 0

        def source(p, r, s=s, flip=flip):
            return p + r * steps + s - steps // 2, r ^ flip

        found.append(flat_permute(features, blocks, groups, source))
    return found


def densify_kernel(counts, rows, cols, weights, dense, zero_rows, sem):
    steps, _, tile, _ = weights.shape
    row_tiles = dense.shape[1] // tile
    zero_rows[...] = jnp.zeros_like(zero_rows)

    def clear(i):
        s, row = i // row_tiles, i % row_tiles
        return pltpu.make_async_copy(zero_rows, dense.at[s, pl.ds(row * tile, tile), :], sem)

    def place(s, k):
        row = pl.multiple_of(rows[s, k] * tile, tile)
        col = pl.multiple_of(cols[s, k] * tile, tile)
        return pltpu.make_async_copy(
            weights.at[s, k], dense.at[s, pl.ds(row, tile), pl.ds(col, tile)], sem
        )

    @pl.loop(0, steps * row_tiles)
    def _(i):
        clear(i).start()

    @pl.loop(0, steps * row_tiles)
    def _(i):
        clear(i).wait()

    for s in range(steps):

        @pl.loop(0, counts[s])
        def _(k, s=s):
            place(s, k).start()

    for s in range(steps):

        @pl.loop(0, counts[s])
        def _(k, s=s):
            place(s, k).wait()


def densify(weights, rows, cols, counts, nodes):
    steps, _, tile, _ = weights.shape
    smem = pl.BlockSpec(memory_space=pltpu.SMEM)
    hbm = pl.BlockSpec(memory_space=pl.ANY)
    return pl.pallas_call(
        densify_kernel,
        out_shape=jax.ShapeDtypeStruct((steps, nodes, nodes), BF16),
        in_specs=[smem, smem, smem, hbm],
        out_specs=hbm,
        scratch_shapes=[pltpu.VMEM((tile, nodes), BF16), pltpu.SemaphoreType.DMA],
        compiler_params=pltpu.CompilerParams(vmem_limit_bytes=4 * MIB),
        cost_estimate=pl.CostEstimate(
            flops=0, bytes_accessed=2 * weights.size * 2 + steps * nodes * nodes * 2, transcendentals=0
        ),
        name="densify",
    )(counts, rows, cols, weights)


def aggregate_kernel(half, order, dense, *refs):
    blocks, (send, keep) = refs[:-2], refs[-2:]
    i = pl.program_id(0)
    total = jnp.dot(dense[0], blocks[0][...], preferred_element_type=F32)
    for s in range(1, len(blocks)):
        total = total + jnp.dot(dense[s], blocks[s][...], preferred_element_type=F32)

    @pl.when(i < half)
    def _():
        send[0] = total

    @pl.when(i >= half)
    def _():
        keep[0] = total


def aggregate_parts(dense, blocks, groups, core):
    steps, nodes, _ = dense.shape
    width = blocks[0].shape[1]
    part, half = nodes // groups, groups // 2
    halves = jnp.arange(half, dtype=jnp.int32) * 2
    order = jnp.concatenate([halves + 1 - core, halves + core])
    whole = pl.BlockSpec((nodes, width), lambda i, order: (0, 0))
    shape = jax.ShapeDtypeStruct((half, part, width), F32)
    return pl.pallas_call(
        functools.partial(aggregate_kernel, half),
        out_shape=(shape, shape),
        grid_spec=pltpu.PrefetchScalarGridSpec(
            num_scalar_prefetch=1,
            grid=(groups,),
            in_specs=[pl.BlockSpec((steps, part, nodes), lambda i, order: (0, order[i], 0))]
            + [whole] * steps,
            out_specs=(
                pl.BlockSpec((1, part, width), lambda i, order: (jnp.minimum(i, half - 1), 0, 0)),
                pl.BlockSpec((1, part, width), lambda i, order: (jnp.maximum(i - half, 0), 0, 0)),
            ),
        ),
        compiler_params=pltpu.CompilerParams(vmem_limit_bytes=44 * MIB),
        cost_estimate=pl.CostEstimate(
            flops=2 * steps * nodes * nodes * width,
            bytes_accessed=dense.size * 2 + steps * nodes * width * 2 + nodes * width * 4,
            transcendentals=0,
        ),
        name="aggregate_parts",
    )(order, dense, *blocks)


def layer_kernel(
    place, features, kept, received, side, weight_self, weight_neigh, cotangent, out, grad_keep, grad_send
):
    own = features[...]
    summed = kept[0] + received[0] + side[...].astype(F32)
    aggregate = summed.astype(BF16)
    pre = jnp.dot(own, weight_self[...], preferred_element_type=F32)
    pre = pre + jnp.dot(aggregate, weight_neigh[...], preferred_element_type=F32)
    sigmoid = jax.nn.sigmoid(pre)
    out[...] = (pre * sigmoid).astype(BF16)
    slope = (cotangent[...].astype(F32) * sigmoid * (1.0 + pre * (1.0 - sigmoid))).astype(BF16)
    contract = (((0,), (0,)), ((), ()))
    grad_self = lax.dot_general(own, slope, contract, preferred_element_type=F32)
    grad_neigh = lax.dot_general(aggregate, slope, contract, preferred_element_type=F32)
    rows, lanes = grad_self.shape[0], grad_keep.shape[1]
    first = place[2] == 0
    for at in range(grad_self.shape[1] // lanes):
        a, b = (g[:, at * lanes : (at + 1) * lanes] for g in (grad_self, grad_neigh))
        grad_keep[at * rows : (at + 1) * rows, :] = jnp.where(first, a, b)
        grad_send[at * rows : (at + 1) * rows, :] = jnp.where(first, b, a)


def layer(place, features, kept, received, side, weight_self, weight_neigh, cotangent):
    part, width = side.shape
    lanes = width // 2
    square = pl.BlockSpec((width, width), lambda i, place: (0, 0))
    rows = pl.BlockSpec((part, width), lambda i, place: (0, 0))
    third = pl.BlockSpec((1, part, width), lambda i, place: (place[1], 0, 0))
    grads = pl.BlockSpec((width * width // lanes, lanes), lambda i, place: (0, 0))
    grad_shape = jax.ShapeDtypeStruct((width * width // lanes, lanes), F32)
    return pl.pallas_call(
        layer_kernel,
        out_shape=(jax.ShapeDtypeStruct((part, width), BF16), grad_shape, grad_shape),
        grid_spec=pltpu.PrefetchScalarGridSpec(
            num_scalar_prefetch=1,
            grid=(1,),
            in_specs=[
                pl.BlockSpec((part, width), lambda i, place: (place[0], 0)),
                third,
                third,
                rows,
                square,
                square,
                rows,
            ],
            out_specs=(rows, grads, grads),
        ),
        compiler_params=pltpu.CompilerParams(vmem_limit_bytes=16 * MIB),
        name="layer",
    )(place, features, kept, received, side, weight_self, weight_neigh, cotangent)


def unpack_kernel(place, mine, other, grad_self, grad_neigh):
    rows, lanes = grad_self.shape[0], mine.shape[1]
    first = place[2] == 0
    for at in range(grad_self.shape[1] // lanes):
        a = mine[at * rows : (at + 1) * rows, :].astype(F32)
        b = other[at * rows : (at + 1) * rows, :].astype(F32)
        grad_self[:, at * lanes : (at + 1) * lanes] = jnp.where(first, a, b)
        grad_neigh[:, at * lanes : (at + 1) * lanes] = jnp.where(first, b, a)


def unpack(place, mine, other, width):
    shape = jax.ShapeDtypeStruct((width, width), F32)
    vmem = pl.BlockSpec(memory_space=pltpu.VMEM)
    return pl.pallas_call(
        unpack_kernel,
        out_shape=(shape, shape),
        in_specs=[pl.BlockSpec(memory_space=pltpu.SMEM), vmem, vmem],
        out_specs=(vmem, vmem),
        name="unpack",
    )(place, mine, other)


def all_reduce_grads(place, keep, send, devices, groups, width):
    packed, lanes = keep.shape
    chunk = packed // devices
    chip = (keep + rep_exchange(send, groups, 0)).astype(BF16)
    terms = lax.all_to_all(chip, AXES, 0, 0, tiled=True)
    summed = terms.reshape(devices // 2, 2, chunk, lanes).astype(F32).sum(0).astype(BF16)
    spread = jnp.broadcast_to(summed[None], (devices // 2, 2, chunk, lanes)).reshape(packed, lanes)
    mine = lax.all_to_all(spread, AXES, 0, 0, tiled=True)
    other = rep_exchange(mine, groups, 0)
    return unpack(place, mine, other, width)


def on_device(
    features, tile_weights, tile_rows, tile_cols, tile_counts, weight_self, weight_neigh, cotangent
):
    blocks, groups = lax.axis_size("dom"), lax.axis_size("rep")
    steps = tile_weights.shape[2]
    nodes, width = features.shape
    rep = lax.axis_index("rep").astype(jnp.int32)
    core, side_at = rep % 2, rep // 2
    place = jnp.stack([rep, side_at, core])

    found = fetch_blocks(features, blocks, groups, steps)
    dense = densify(tile_weights[0, 0], tile_rows[0, 0], tile_cols[0, 0], tile_counts[0, 0], nodes)
    send, kept = aggregate_parts(dense, found, groups, core)
    received = rep_exchange(send, groups, 0)
    across = lax.dynamic_index_in_dim(kept, 1 - side_at, 0, keepdims=False)
    across = across + lax.dynamic_index_in_dim(received, 1 - side_at, 0, keepdims=False)
    side = rep_exchange(across.astype(BF16), groups, 1)
    out, grad_keep, grad_send = layer(
        place, features, kept, received, side, weight_self, weight_neigh, cotangent
    )
    grad_self, grad_neigh = all_reduce_grads(
        place, grad_keep, grad_send, blocks * groups, groups, width
    )
    return out, grad_self, grad_neigh


def solution(mesh):
    return jax.shard_map(
        on_device,
        mesh=mesh,
        in_specs=(
            P("dom", None),
            P("dom", "rep", None, None, None, None),
            P("dom", "rep", None, None),
            P("dom", "rep", None, None),
            P("dom", "rep", None),
            P(),
            P(),
            P(AXES, None),
        ),
        out_specs=(P(AXES, None), P(), P()),
        check_vma=False,
    )
```

time: 304 us -> 89.2 us (0.29)
  waiting for transfers between devices: 205 us -> 10.5 us
  matrix products: 36.1 us -> 0 us
  local copies, waits for them, and re-layouts: 37.1 us -> 9.88 us
  blocking collectives: 0 us -> 23.9 us
  Pallas kernels: 0 us -> 20.2 us
  starting transfers between devices: 8.18 us -> 23.4 us
  between operations: 14.2 us -> 0.7 us
    psum x1 -> x0, waiting for transfers between devices: 130 us -> none  [on_device(): grad_self, grad_neigh = lax.psum((self_term, neigh_term), ('dom', 'rep'))]
    dot_general x10 -> x0, matrix products: 36.1 us -> none  [the longest x2 17 us: step_terms(): jnp.dot(placing, product.reshape(slot_total, tile_side * width), precisio...]
    ppermute x3 -> x6, waiting for transfers between devices: 46.6 us -> 10.5 us  [the longest x4 9.91 us: rep_exchange(): return lax.ppermute(value, 'rep', route)]
    reduce_scatter x1 -> x0, waiting for transfers between devices: 27.9 us -> none  [on_device(): lax.psum_scatter(partial_value, 'rep', scatter_dimension=0, tiled=True)]
    all_to_all x0 -> x2, blocking collectives: none -> 23.9 us  [the longest x1 13.9 us: all_reduce_grads(): terms = lax.all_to_all(chip, AXES, 0, 0, tiled=True)]
    unnamed x22 -> x24, local copies, waits for them, and re-layouts: 30.9 us -> 9.86 us
    pallas_call x0 -> x4, Pallas kernels: none -> 20.2 us  [the longest x1 9.56 us: densify(): pl.pallas_call(densify_kernel, out_shape=jax.ShapeDtypeStruct((steps, nod...]
    ppermute x3 -> x6, starting transfers between devices: 8.1 us -> 23.4 us  [the longest x4 17.1 us: rep_exchange(): return lax.ppermute(value, 'rep', route)]
  transfers between devices with their start and end apart: 5 -> 6, of which waited for: 4 -> 5; matrix products, arithmetic and copies ran while one was open for 11% -> 0% of each run, Pallas kernels for 0% -> 11%
where the time goes in v1:
time: 89.2 us; the launch traced here: 88.9 us
  blocking collectives  23.9 us (27%)
  starting transfers between devices  23.4 us (26%)
  Pallas kernels  20.2 us (23%)
  waiting for transfers between devices  10.5 us (12%)
  local copies, waits for them, and re-layouts  9.88 us (11%)
    ppermute x4, starting transfers between devices, rep_exchange(): return lax.ppermute(value, 'rep', route)  17.1 us
    all_to_all x1, blocking collectives, all_reduce_grads(): terms = lax.all_to_all(chip, AXES, 0, 0, tiled=True)  13.9 us
    all_to_all x1, blocking collectives, all_reduce_grads(): mine = lax.all_to_all(spread, AXES, 0, 0, tiled=True)  10 us
    ppermute x4, waiting for transfers between devices, rep_exchange(): return lax.ppermute(value, 'rep', route)  9.91 us
    unnamed x24, local copies, waits for them, and re-layouts  9.86 us
    pallas_call x1, Pallas kernels, densify(): pl.pallas_call(densify_kernel, out_shape=jax.ShapeDtypeStruct((steps, nod...  9.56 us
    pallas_call x1, Pallas kernels, aggregate_parts(): pl.pallas_call(functools.partial(aggregate_kernel, half), out_shape=(shap...  7.26 us
    ppermute x2, starting transfers between devices, flat_permute(): return lax.ppermute(value, AXES, route)  6.31 us
  transfers between devices with their start and end apart: 6, of which 5 were waited for; matrix products, arithmetic and copies ran while one was open for 0% of the time, Pallas kernels for 11%

profile of v1, /device:TPU:0, one launch (start us, length us, event | category | flops | bytes accessed | tf_op | source)
XLA Modules:
  0.0 88.9 jit_solution(2762195375441614284)
XLA Ops:
  0.6 3.0 %collective-permute-start = (bf16[1536,256]{1,0:T(8,128)(2,1)}, bf16[1536,256]{1,0:T(8,128)(2,1)S(1)}, u32[]{:S(2)}, u32[]{:S(2)}) collective-permute-start(bf16[1536,256]{1,0:T(8,128)(2,1)} %features.1), channel_id=1, source_target_pairs={{28,0},{5,1},{14,2},{23,3},{0,4},{9,5},{18,6},{27,7},{4,8},{13,9},... | collective-permute-start | bytes 2359304 | tf_op jit(solution)/shard_map/ppermute | solution.py:21
  3.7 3.3 %collective-permute-start.1 = (bf16[1536,256]{1,0:T(8,128)(2,1)}, bf16[1536,256]{1,0:T(8,128)(2,1)S(1)}, u32[]{:S(2)}, u32[]{:S(2)}) collective-permute-start(bf16[1536,256]{1,0:T(8,128)(2,1)} %features.1), channel_id=1, source_target_pairs={{2,0},{11,1},{16,2},{25,3},{6,4},{15,5},{20,6},{29,7},{10,8},{19,9... | collective-permute-start | bytes 2359304 | tf_op jit(solution)/shard_map/ppermute | solution.py:21
  6.9 0.0 copy-start.1
  6.9 2.6 %copy-done.1 = bf16[1,1,2,88,128,128]{5,4,3,2,1,0:T(8,128)(2,1)S(1)} copy-done((bf16[1,1,2,88,128,128]{5,4,3,2,1,0:T(8,128)(2,1)S(1)}, bf16[1,1,2,88,128,128]{5,4,3,2,1,0:T(8,128)(2,1)}, u32[]{:S(2)}) %copy-start.1) | copy-done | bytes 5767192
  9.6 0.0 copy-start.7
  9.6 0.7 copy-done.7
  10.3 0.0 copy-start.8
  10.3 0.7 copy-done.8
  10.9 0.0 copy-start.9
  10.9 0.7 copy-done.9
  11.6 9.6 %densify.1.dense = bf16[2,1536,1536]{2,1,0:T(8,128)(2,1)S(1)} custom-call(s32[2]{0:T(128)S(1)} %bitcast.16, s32[2,88]{1,0:T(2,128)S(1)} %bitcast.14, s32[2,88]{1,0:T(2,128)S(1)} %bitcast.15, bf16[2,88,128,128]{3,2,1,0:T(8,128)(2,1)S(1)} %bitcast.13), custom_call_target="tpu_custom_call" | custom-call | bytes 20971520 | tf_op jit(solution)/shard_map/densify/pallas_call | solution.py:82
  21.2 0.0 copy-start
  21.2 3.6 %copy-done = bf16[2,1536,1536]{2,1,0:T(8,128)(2,1)} copy-done((bf16[2,1536,1536]{2,1,0:T(8,128)(2,1)}, bf16[2,1536,1536]{2,1,0:T(8,128)(2,1)S(1)}, u32[]{:S(2)}) %copy-start) | copy-done | bytes 9437208
  24.8 0.0 copy-start.2
  24.8 0.0 copy-start.3
  24.8 0.0 copy-start.4
  24.8 0.1 pad_add_fusion.1.order
  24.9 0.0 collective-permute-done.refs_0_
  24.9 0.6 collective-permute-done.1.refs_1_
  25.5 7.3 %aggregate_parts.1 = (f32[2,384,256]{2,1,0:T(8,128)}, f32[2,384,256]{2,1,0:T(8,128)S(1)}) custom-call(s32[4]{0:T(128)S(1)} %pad_add_fusion.1.order, bf16[2,1536,1536]{2,1,0:T(8,128)(2,1)} %copy-done, bf16[1536,256]{1,0:T(8,128)(2,1)S(1)} %collective-permute-done.refs_0_, bf16[1536,256]{1,0:T(8,128)(2,1)S(1)} %collective-permute-done.1.refs_1_), custom_call_target="tpu_custom_call" | custom-call | flops 2415919104 | bytes 12582912 | tf_op jit(solution)/shard_map/aggregate_parts/pallas_call | solution.py:120
  32.8 7.9 %collective-permute-start.2 = (f32[2,384,256]{2,1,0:T(8,128)}, f32[2,384,256]{2,1,0:T(8,128)S(1)}, u32[]{:S(2)}, u32[]{:S(2)}) collective-permute-start(f32[2,384,256]{2,1,0:T(8,128)} %get-tuple-element.11), channel_id=1, source_target_pairs={{0,1},{1,0},{2,3},{3,2},{4,5},{5,4},{6,7},{7,6},{8,9},{9,8},{10,11... | collective-permute-start | bytes 2359304 | tf_op jit(solution)/shard_map/ppermute | solution.py:26
  40.7 2.1 %collective-permute-done.2.received = f32[2,384,256]{2,1,0:T(8,128)S(1)} collective-permute-done((f32[2,384,256]{2,1,0:T(8,128)}, f32[2,384,256]{2,1,0:T(8,128)S(1)}, u32[]{:S(2)}, u32[]{:S(2)}) %collective-permute-start.2) | collective-permute-done | bytes 786464 | tf_op jit(solution)/shard_map/ppermute | solution.py:26
  42.8 0.1 fusion
  42.9 8.9 %collective-permute-start.3 = (bf16[384,256]{1,0:T(8,128)(2,1)S(1)}, bf16[384,256]{1,0:T(8,128)(2,1)S(1)}, u32[]{:S(2)}, u32[]{:S(2)}) collective-permute-start(bf16[384,256]{1,0:T(8,128)(2,1)S(1)} %fusion), channel_id=1, source_target_pairs={{0,2},{1,3},{2,0},{3,1},{4,6},{5,7},{6,4},{7,5},{8,10},{9,11},{10,... | collective-permute-start | bytes 589832 | tf_op jit(solution)/shard_map/ppermute | solution.py:26
  51.8 0.1 pad_add_fusion.place
  51.9 0.0 copy-start.6
  51.9 5.1 %collective-permute-done.3.side = bf16[384,256]{1,0:T(8,128)(2,1)S(1)} collective-permute-done((bf16[384,256]{1,0:T(8,128)(2,1)S(1)}, bf16[384,256]{1,0:T(8,128)(2,1)S(1)}, u32[]{:S(2)}, u32[]{:S(2)}) %collective-permute-start.3) | collective-permute-done | bytes 196640 | tf_op jit(solution)/shard_map/ppermute | solution.py:26
  57.0 0.0 copy-done.2
  57.0 0.0 copy-done.3
  57.0 0.0 copy-done.4
  57.0 0.0 copy-start.5
  57.1 0.9 %copy-done.5 = bf16[256,256]{1,0:T(8,128)(2,1)S(1)} copy-done((bf16[256,256]{1,0:T(8,128)(2,1)S(1)}, bf16[256,256]{1,0:T(8,128)(2,1)}, u32[]{:S(2)}) %copy-start.5) | copy-done | bytes 131096
  58.0 1.6 %layer.1 = (bf16[384,256]{1,0:T(8,128)(2,1)}, f32[512,128]{1,0:T(8,128)S(1)}, f32[512,128]{1,0:T(8,128)S(1)}) custom-call(s32[3]{0:T(128)S(1)} %pad_add_fusion.place, bf16[1536,256]{1,0:T(8,128)(2,1)S(1)} %copy-done.2, f32[2,384,256]{2,1,0:T(8,128)S(1)} %get-tuple-element.10.kept, f32[2,384,256]{2,1,0:T(8,128)S(1)} %collective-permute-done.2.received, ...), custom_call_target="tpu_custom_call" | custom-call | tf_op jit(solution)/shard_map/layer/pallas_call | solution.py:173
  59.6 0.0 collective-permute-start.4
  59.6 1.5 %collective-permute-done.4 = f32[512,128]{1,0:T(8,128)S(1)} collective-permute-done((f32[512,128]{1,0:T(8,128)S(1)}, f32[512,128]{1,0:T(8,128)S(1)}, u32[]{:S(2)}, u32[]{:S(2)}) %collective-permute-start.4) | collective-permute-done | bytes 262176 | tf_op jit(solution)/shard_map/ppermute | solution.py:26
  61.1 13.9 %all_to_all.20 = bf16[32,16,128]{2,1,0:T(8,128)(2,1)S(1)} all-to-all(bf16[32,16,128]{2,1,0:T(8,128)(2,1)S(1)} %bitcast.17), channel_id=1, replica_groups=mesh['dom'=8,'rep'=4] {'dom','rep'}, dimensions={0} | all-to-all | bytes 262144 | tf_op jit(solution)/shard_map/all_to_all | solution.py:221
  75.1 10.0 %all_to_all.21 = bf16[32,16,128]{2,1,0:T(8,128)(2,1)S(1)} all-to-all(bf16[32,16,128]{2,1,0:T(8,128)(2,1)S(1)} %bitcast.21), channel_id=1, replica_groups=mesh['dom'=8,'rep'=4] {'dom','rep'}, dimensions={0} | all-to-all | bytes 262144 | tf_op jit(solution)/shard_map/all_to_all | solution.py:224
  85.1 0.0 copy-start.10
  85.1 0.2 collective-permute-start.5
  85.3 1.1 %collective-permute-done.5.other = bf16[512,128]{1,0:T(8,128)(2,1)S(1)} collective-permute-done((bf16[512,128]{1,0:T(8,128)(2,1)S(1)}, bf16[512,128]{1,0:T(8,128)(2,1)S(1)}, u32[]{:S(2)}, u32[]{:S(2)}) %collective-permute-start.5) | collective-permute-done | bytes 131104 | tf_op jit(solution)/shard_map/ppermute | solution.py:26
  86.5 0.0 copy-done.6
  86.5 0.0 copy-done.10
  86.5 0.0 copy-start.11
  86.5 0.6 copy-done.11
  87.1 1.8 %unpack.1 = (f32[256,256]{1,0:T(8,128)}, f32[256,256]{1,0:T(8,128)}) custom-call(s32[3]{0:T(128)} %copy-done.6, bf16[512,128]{1,0:T(8,128)(2,1)} %bitcast.19, bf16[512,128]{1,0:T(8,128)(2,1)} %copy-done.11), custom_call_target="tpu_custom_call" | custom-call | tf_op jit(solution)/shard_map/unpack/pallas_call | solution.py:208
  (4 shorter events, 0.1 us)
Async XLA Ops:
  0.6 24.3 %collective-permute-start = (bf16[1536,256]{1,0:T(8,128)(2,1)}, bf16[1536,256]{1,0:T(8,128)(2,1)S(1)}, u32[]{:S(2)}, u32[]{:S(2)}) collective-permute-start(bf16[1536,256]{1,0:T(8,128)(2,1)} %features.1), channel_id=1, source_target_pairs={{28,0},{5,1},{14,2},{23,3},{0,4},{9,5},{18,6},{27,7},{4,8},{13,9},... | collective-permute-start | bytes 2359304 | tf_op jit(solution)/shard_map/ppermute | solution.py:21
  3.7 21.9 %collective-permute-start.1 = (bf16[1536,256]{1,0:T(8,128)(2,1)}, bf16[1536,256]{1,0:T(8,128)(2,1)S(1)}, u32[]{:S(2)}, u32[]{:S(2)}) collective-permute-start(bf16[1536,256]{1,0:T(8,128)(2,1)} %features.1), channel_id=1, source_target_pairs={{2,0},{11,1},{16,2},{25,3},{6,4},{15,5},{20,6},{29,7},{10,8},{19,9... | collective-permute-start | bytes 2359304 | tf_op jit(solution)/shard_map/ppermute | solution.py:21
  6.9 2.6 %copy-start.1 = (bf16[1,1,2,88,128,128]{5,4,3,2,1,0:T(8,128)(2,1)S(1)}, bf16[1,1,2,88,128,128]{5,4,3,2,1,0:T(8,128)(2,1)}, u32[]{:S(2)}) copy-start(bf16[1,1,2,88,128,128]{5,4,3,2,1,0:T(8,128)(2,1)} %param.9) | copy-start | bytes 17301508
  9.6 0.7 copy-start.7
  10.3 0.7 copy-start.8
  10.9 0.7 copy-start.9
  21.2 3.7 %copy-start = (bf16[2,1536,1536]{2,1,0:T(8,128)(2,1)}, bf16[2,1536,1536]{2,1,0:T(8,128)(2,1)S(1)}, u32[]{:S(2)}) copy-start(bf16[2,1536,1536]{2,1,0:T(8,128)(2,1)S(1)} %densify.1.dense) | copy-start | bytes 28311556
  24.8 32.2 %copy-start.2 = (bf16[1536,256]{1,0:T(8,128)(2,1)S(1)}, bf16[1536,256]{1,0:T(8,128)(2,1)}, u32[]{:S(2)}) copy-start(bf16[1536,256]{1,0:T(8,128)(2,1)} %features.1) | copy-start | bytes 2359300
  24.8 32.2 %copy-start.3 = (bf16[384,256]{1,0:T(8,128)(2,1)S(1)}, bf16[384,256]{1,0:T(8,128)(2,1)}, u32[]{:S(2)}) copy-start(bf16[384,256]{1,0:T(8,128)(2,1)} %cotangent.1) | copy-start | bytes 589828
  24.8 32.2 %copy-start.4 = (bf16[256,256]{1,0:T(8,128)(2,1)S(1)}, bf16[256,256]{1,0:T(8,128)(2,1)}, u32[]{:S(2)}) copy-start(bf16[256,256]{1,0:T(8,128)(2,1)} %weight_self.1) | copy-start | bytes 393220
  32.8 10.0 %collective-permute-start.2 = (f32[2,384,256]{2,1,0:T(8,128)}, f32[2,384,256]{2,1,0:T(8,128)S(1)}, u32[]{:S(2)}, u32[]{:S(2)}) collective-permute-start(f32[2,384,256]{2,1,0:T(8,128)} %get-tuple-element.11), channel_id=1, source_target_pairs={{0,1},{1,0},{2,3},{3,2},{4,5},{5,4},{6,7},{7,6},{8,9},{9,8},{10,11... | collective-permute-start | bytes 2359304 | tf_op jit(solution)/shard_map/ppermute | solution.py:26
  42.9 14.1 %collective-permute-start.3 = (bf16[384,256]{1,0:T(8,128)(2,1)S(1)}, bf16[384,256]{1,0:T(8,128)(2,1)S(1)}, u32[]{:S(2)}, u32[]{:S(2)}) collective-permute-start(bf16[384,256]{1,0:T(8,128)(2,1)S(1)} %fusion), channel_id=1, source_target_pairs={{0,2},{1,3},{2,0},{3,1},{4,6},{5,7},{6,4},{7,5},{8,10},{9,11},{10,... | collective-permute-start | bytes 589832 | tf_op jit(solution)/shard_map/ppermute | solution.py:26
  51.9 34.6 %copy-start.6 = (s32[3]{0:T(128)}, s32[3]{0:T(128)S(1)}, u32[]{:S(2)}) copy-start(s32[3]{0:T(128)S(1)} %pad_add_fusion.place) | copy-start | bytes 40
  57.0 0.9 %copy-start.5 = (bf16[256,256]{1,0:T(8,128)(2,1)S(1)}, bf16[256,256]{1,0:T(8,128)(2,1)}, u32[]{:S(2)}) copy-start(bf16[256,256]{1,0:T(8,128)(2,1)} %weight_neigh.1) | copy-start | bytes 393220
  59.6 1.5 %collective-permute-start.4 = (f32[512,128]{1,0:T(8,128)S(1)}, f32[512,128]{1,0:T(8,128)S(1)}, u32[]{:S(2)}, u32[]{:S(2)}) collective-permute-start(f32[512,128]{1,0:T(8,128)S(1)} %get-tuple-element.14), channel_id=1, source_target_pairs={{0,1},{1,0},{2,3},{3,2},{4,5},{5,4},{6,7},{7,6},{8,9},{9,8},{10,11... | collective-permute-start | bytes 786440 | tf_op jit(solution)/shard_map/ppermute | solution.py:26
  85.1 1.4 %copy-start.10 = (bf16[32,16,128]{2,1,0:T(8,128)(2,1)}, bf16[32,16,128]{2,1,0:T(8,128)(2,1)S(1)}, u32[]{:S(2)}) copy-start(bf16[32,16,128]{2,1,0:T(8,128)(2,1)S(1)} %all_to_all.21) | copy-start | bytes 393220
  85.1 1.3 %collective-permute-start.5 = (bf16[512,128]{1,0:T(8,128)(2,1)S(1)}, bf16[512,128]{1,0:T(8,128)(2,1)S(1)}, u32[]{:S(2)}, u32[]{:S(2)}) collective-permute-start(bf16[512,128]{1,0:T(8,128)(2,1)S(1)} %bitcast.18), channel_id=1, source_target_pairs={{0,1},{1,0},{2,3},{3,2},{4,5},{5,4},{6,7},{7,6},{8,9},{9,8},{10,11... | collective-permute-start | bytes 393224 | tf_op jit(solution)/shard_map/ppermute | solution.py:26
  86.5 0.6 copy-start.11

commit v2 on v1

v2 whole, which is shorter than its diff:
```python
import functools

import jax
import jax.numpy as jnp
from jax import lax
from jax.experimental import pallas as pl
from jax.experimental.pallas import tpu as pltpu
from jax.sharding import PartitionSpec as P

AXES = ("dom", "rep")
F32, BF16 = jnp.float32, jnp.bfloat16
MIB = 1 << 20


def flat_permute(value, blocks, groups, source):
    route = []
    for p in range(blocks):
        for r in range(groups):
            q, g = source(p, r)
            route.append((q % blocks * groups + g % groups, p * groups + r))
    return lax.ppermute(value, AXES, route)


def rep_exchange(value, groups, bit):
    route = [(r, r ^ (1 << bit)) for r in range(groups)]
    return lax.ppermute(value, "rep", route)


def fetch_blocks(features, blocks, groups, steps):
    found = []
    for s in range(steps):
        flip = groups // 2 if s % 2 else 0

        def source(p, r, s=s, flip=flip):
            return p + r * steps + s - steps // 2, r ^ flip

        found.append(flat_permute(features, blocks, groups, source))
    return found


def densify_kernel(place, counts, rows, cols, weights, send, mid, own, zero_rows, sem):
    steps, _, tile, _ = weights.shape
    nodes = zero_rows.shape[1]
    per_part = own.shape[1] // tile
    zero_rows[...] = jnp.zeros_like(zero_rows)

    def clear(ref, i):
        per_step = ref.shape[1] // tile
        s, row = i // per_step, i % per_step
        return pltpu.make_async_copy(zero_rows, ref.at[s, pl.ds(row * tile, tile), :], sem)

    def put(ref, s, k, row):
        row = pl.multiple_of(row * tile, tile)
        col = pl.multiple_of(cols[s, k] * tile, tile)
        return pltpu.make_async_copy(
            weights.at[s, k], ref.at[s, pl.ds(row, tile), pl.ds(col, tile)], sem
        )

    for ref in (send, mid, own):

        @pl.loop(0, steps * (ref.shape[1] // tile))
        def _(i, ref=ref):
            clear(ref, i).start()

    for ref in (send, mid, own):

        @pl.loop(0, steps * (ref.shape[1] // tile))
        def _(i, ref=ref):
            clear(ref, i).wait()

    for s in range(steps):

        @pl.loop(0, counts[s])
        def _(k, s=s):
            part, row = rows[s, k] // per_part, rows[s, k] % per_part
            sent = part % 2 != place[2]
            kept = jnp.logical_and(jnp.logical_not(sent), part // 2 == place[1])

            @pl.when(sent)
            def _():
                put(send, s, k, part // 2 * per_part + row).start()

            @pl.when(kept)
            def _():
                put(own, s, k, row).start()

            @pl.when(jnp.logical_not(jnp.logical_or(sent, kept)))
            def _():
                put(mid, s, k, row).start()

    for s in range(steps):

        @pl.loop(0, counts[s])
        def _(k, s=s):
            put(own, s, 0, 0).wait()


def densify(place, weights, rows, cols, counts, nodes, groups):
    steps, _, tile, _ = weights.shape
    part = nodes // groups
    smem = pl.BlockSpec(memory_space=pltpu.SMEM)
    hbm = pl.BlockSpec(memory_space=pl.ANY)
    return pl.pallas_call(
        densify_kernel,
        out_shape=tuple(
            jax.ShapeDtypeStruct((steps, n * part, nodes), BF16) for n in (groups // 2, 1, 1)
        ),
        in_specs=[smem, smem, smem, smem, hbm],
        out_specs=(hbm, hbm, hbm),
        scratch_shapes=[pltpu.VMEM((tile, nodes), BF16), pltpu.SemaphoreType.DMA],
        compiler_params=pltpu.CompilerParams(vmem_limit_bytes=4 * MIB),
        cost_estimate=pl.CostEstimate(
            flops=0, bytes_accessed=2 * weights.size * 2 + steps * nodes * nodes * 2, transcendentals=0
        ),
        name="densify",
    )(place, counts, rows, cols, weights)


def block_product(dense, found):
    total = jnp.dot(dense[0], found[0][...], preferred_element_type=F32)
    for s in range(1, len(found)):
        total = total + jnp.dot(dense[s], found[s][...], preferred_element_type=F32)
    return total


def rows_kernel(found_total, place, dense, *refs):
    refs[-1][...] = block_product(dense, refs[:found_total])


def own_kernel(place, features, received, weight_self, dense, *refs):
    found, (own, projected) = refs[:-2], refs[-2:]
    part = own.shape[0]
    own[...] = block_product(dense, found) + received[pl.ds(pl.multiple_of(place[1] * part, part), part), :]
    mine = features[pl.ds(pl.multiple_of(place[0] * part, part), part), :]
    projected[...] = jnp.dot(mine, weight_self[...], preferred_element_type=F32)


def product_call(kernel, place, out_shape, others, dense, found, name):
    vmem = pl.BlockSpec(memory_space=pltpu.VMEM)
    operands = (*others, dense, *found)
    outs = jax.tree.leaves(out_shape)
    held = sum(v.size * v.dtype.itemsize for v in (*operands, *outs))
    width = found[0].shape[1]
    rows = sum(v.size // width for v in outs[:1])
    return pl.pallas_call(
        kernel,
        out_shape=out_shape,
        in_specs=[pl.BlockSpec(memory_space=pltpu.SMEM)] + [vmem] * len(operands),
        out_specs=jax.tree.map(lambda _: vmem, out_shape),
        compiler_params=pltpu.CompilerParams(vmem_limit_bytes=held + 8 * MIB),
        cost_estimate=pl.CostEstimate(
            flops=2 * rows * dense.shape[0] * dense.shape[1] * width,
            bytes_accessed=rows * dense.shape[0] * dense.shape[1] * 2,
            transcendentals=0,
        ),
        name=name,
    )(place, *operands)


def layer_kernel(
    place, features, own, side, projected, weight_neigh, cotangent, out, grad_keep, grad_send
):
    part = own.shape[0]
    mine = features[pl.ds(pl.multiple_of(place[0] * part, part), part), :]
    aggregate = (own[...] + side[...].astype(F32)).astype(BF16)
    pre = projected[...] + jnp.dot(aggregate, weight_neigh[...], preferred_element_type=F32)
    sigmoid = jax.nn.sigmoid(pre)
    out[...] = (pre * sigmoid).astype(BF16)
    slope = (cotangent[...].astype(F32) * sigmoid * (1.0 + pre * (1.0 - sigmoid))).astype(BF16)
    contract = (((0,), (0,)), ((), ()))
    grad_self = lax.dot_general(mine, slope, contract, preferred_element_type=F32)
    grad_neigh = lax.dot_general(aggregate, slope, contract, preferred_element_type=F32)
    first = place[2] == 0
    grad_keep[...] = jnp.where(first, grad_self, grad_neigh)
    grad_send[...] = jnp.where(first, grad_neigh, grad_self)


def layer(place, features, own, side, projected, weight_neigh, cotangent):
    part, width = side.shape
    vmem = pl.BlockSpec(memory_space=pltpu.VMEM)
    grad = jax.ShapeDtypeStruct((width, width), F32)
    return pl.pallas_call(
        layer_kernel,
        out_shape=(jax.ShapeDtypeStruct((part, width), BF16), grad, grad),
        in_specs=[pl.BlockSpec(memory_space=pltpu.SMEM)] + [vmem] * 6,
        out_specs=(vmem, vmem, vmem),
        compiler_params=pltpu.CompilerParams(vmem_limit_bytes=16 * MIB),
        name="layer",
    )(place, features, own, side, projected, weight_neigh, cotangent)


def all_reduce_grads(core, keep, send, devices, groups):
    rows, width = keep.shape
    chunk = rows // devices
    chip = (keep + rep_exchange(send, groups, 0)).astype(BF16)
    terms = lax.all_to_all(chip, AXES, 0, 0, tiled=True)
    summed = terms.reshape(devices // 2, 2, chunk, width).astype(F32).sum(0).astype(BF16)
    spread = jnp.broadcast_to(summed[None], (devices // 2, 2, chunk, width)).reshape(rows, width)
    mine = lax.all_to_all(spread, AXES, 0, 0, tiled=True)
    other = rep_exchange(mine, groups, 0)
    first = core == 0
    grad_self = jnp.where(first, mine, other).astype(F32)
    grad_neigh = jnp.where(first, other, mine).astype(F32)
    return grad_self, grad_neigh


def on_device(
    features, tile_weights, tile_rows, tile_cols, tile_counts, weight_self, weight_neigh, cotangent
):
    blocks, groups = lax.axis_size("dom"), lax.axis_size("rep")
    steps = tile_weights.shape[2]
    nodes, width = features.shape
    rep = lax.axis_index("rep").astype(jnp.int32)
    core, side_at = rep % 2, rep // 2
    place = jnp.stack([rep, side_at, core])

    found = fetch_blocks(features, blocks, groups, steps)
    dense_send, dense_mid, dense_own = densify(
        place, tile_weights[0, 0], tile_rows[0, 0], tile_cols[0, 0], tile_counts[0, 0], nodes, groups
    )
    part = nodes // groups
    rows = functools.partial(rows_kernel, steps)
    quarter = jax.ShapeDtypeStruct((part, width), F32)
    halves = jax.ShapeDtypeStruct((nodes // 2, width), F32)
    send = product_call(
        rows, place, halves, (), dense_send, found, "send_rows"
    )
    received = rep_exchange(send, groups, 0)
    mid = product_call(
        rows, place, quarter, (), dense_mid, found, "mid_rows"
    )
    across = mid + lax.dynamic_slice_in_dim(received, (1 - side_at) * part, part, 0)
    side = rep_exchange(across.astype(BF16), groups, 1)
    own, projected = product_call(
        own_kernel, place, (quarter, quarter), (features, received, weight_self), dense_own, found, "own_rows"
    )
    out, grad_keep, grad_send = layer(
        place, features, own, side, projected, weight_neigh, cotangent
    )
    grad_self, grad_neigh = all_reduce_grads(core, grad_keep, grad_send, blocks * groups, groups)
    return out, grad_self, grad_neigh


def solution(mesh):
    return jax.shard_map(
        on_device,
        mesh=mesh,
        in_specs=(
            P("dom", None),
            P("dom", "rep", None, None, None, None),
            P("dom", "rep", None, None),
            P("dom", "rep", None, None),
            P("dom", "rep", None),
            P(),
            P(),
            P(AXES, None),
        ),
        out_specs=(P(AXES, None), P(), P()),
        check_vma=False,
    )
```

time: 89.2 us -> 82.3 us (0.923)
  starting transfers between devices: 23.4 us -> 15.6 us
  waiting for transfers between devices: 10.5 us -> 15.8 us
  Pallas kernels: 20.2 us -> 17.2 us
  blocking collectives: 23.9 us -> 22.5 us
    ppermute x2, waiting for transfers between devices: 0.64 us -> 8.98 us  [flat_permute(): return lax.ppermute(value, AXES, route)]
    ppermute x4, starting transfers between devices: 17.1 us -> 9.03 us  [rep_exchange(): return lax.ppermute(value, 'rep', route)]
    ppermute x4, waiting for transfers between devices: 9.91 us -> 6.85 us  [rep_exchange(): return lax.ppermute(value, 'rep', route)]
    pallas_call x3 -> x4, Pallas kernels: 18.6 us -> 15.6 us  [the longest x1 10.1 us: densify(): pl.pallas_call(densify_kernel, out_shape=tuple((jax.ShapeDtypeStruct((ste...]
    all_to_all x1, blocking collectives: 13.9 us -> 12.5 us  [all_reduce_grads(): terms = lax.all_to_all(chip, AXES, 0, 0, tiled=True)]
  transfers between devices with their start and end apart: 6 -> 6, of which waited for: 5 -> 4; matrix products, arithmetic and copies ran while one was open for 0% -> 0% of each run, Pallas kernels for 11% -> 16%
where the time goes in v2:
time: 82.3 us; the launch traced here: 82.1 us
  blocking collectives  22.5 us (27%)
  Pallas kernels  17.2 us (21%)
  waiting for transfers between devices  15.8 us (19%)
  starting transfers between devices  15.6 us (19%)
  local copies, waits for them, and re-layouts  9.33 us (11%)
  other arithmetic  1.02 us (1%)
    all_to_all x1, blocking collectives, all_reduce_grads(): terms = lax.all_to_all(chip, AXES, 0, 0, tiled=True)  12.5 us
    pallas_call x1, Pallas kernels, densify(): pl.pallas_call(densify_kernel, out_shape=tuple((jax.ShapeDtypeStruct((ste...  10.1 us
    all_to_all x1, blocking collectives, all_reduce_grads(): mine = lax.all_to_all(spread, AXES, 0, 0, tiled=True)  10 us
    unnamed x24, local copies, waits for them, and re-layouts  9.32 us
    ppermute x4, starting transfers between devices, rep_exchange(): return lax.ppermute(value, 'rep', route)  9.03 us
    ppermute x2, waiting for transfers between devices, flat_permute(): return lax.ppermute(value, AXES, route)  8.98 us
    ppermute x4, waiting for transfers between devices, rep_exchange(): return lax.ppermute(value, 'rep', route)  6.85 us
    ppermute x2, starting transfers between devices, flat_permute(): return lax.ppermute(value, AXES, route)  6.54 us
  transfers between devices with their start and end apart: 6, of which 4 were waited for; matrix products, arithmetic and copies ran while one was open for 0% of the time, Pallas kernels for 16%

profile of v2, /device:TPU:0, one launch (start us, length us, event | category | flops | bytes accessed | tf_op | source)
XLA Modules:
  0.0 82.1 jit_solution(13474843218494445648)
XLA Ops:
  0.6 5.0 %collective-permute-start.1 = (bf16[1536,256]{1,0:T(8,128)(2,1)}, bf16[1536,256]{1,0:T(8,128)(2,1)S(1)}, u32[]{:S(2)}, u32[]{:S(2)}) collective-permute-start(bf16[1536,256]{1,0:T(8,128)(2,1)} %features.3), channel_id=1, source_target_pairs={{2,0},{11,1},{16,2},{25,3},{6,4},{15,5},{20,6},{29,7},{10,8},{19,9... | collective-permute-start | bytes 2359304 | tf_op jit(solution)/shard_map/ppermute | solution.py:21
  5.6 1.5 %collective-permute-start = (bf16[1536,256]{1,0:T(8,128)(2,1)}, bf16[1536,256]{1,0:T(8,128)(2,1)S(1)}, u32[]{:S(2)}, u32[]{:S(2)}) collective-permute-start(bf16[1536,256]{1,0:T(8,128)(2,1)} %features.3), channel_id=1, source_target_pairs={{28,0},{5,1},{14,2},{23,3},{0,4},{9,5},{18,6},{27,7},{4,8},{13,9},... | collective-permute-start | bytes 2359304 | tf_op jit(solution)/shard_map/ppermute | solution.py:21
  7.2 0.1 pad_add_fusion.place
  7.2 0.0 copy-start
  7.2 2.6 %copy-done = bf16[1,1,2,88,128,128]{5,4,3,2,1,0:T(8,128)(2,1)S(1)} copy-done((bf16[1,1,2,88,128,128]{5,4,3,2,1,0:T(8,128)(2,1)S(1)}, bf16[1,1,2,88,128,128]{5,4,3,2,1,0:T(8,128)(2,1)}, u32[]{:S(2)}) %copy-start) | copy-done | bytes 5767192
  9.9 0.0 copy-start.9
  9.9 0.7 copy-done.9
  10.6 0.0 copy-start.10
  10.6 0.7 copy-done.10
  11.2 0.0 copy-start.11
  11.2 0.7 copy-done.11
  11.9 10.1 %densify.1 = (bf16[2,768,1536]{2,1,0:T(8,128)(2,1)S(1)}, bf16[2,384,1536]{2,1,0:T(8,128)(2,1)S(1)}, bf16[2,384,1536]{2,1,0:T(8,128)(2,1)S(1)}) custom-call(s32[3]{0:T(128)S(1)} %pad_add_fusion.place, s32[2]{0:T(128)S(1)} %bitcast.17, s32[2,88]{1,0:T(2,128)S(1)} %bitcast.15, s32[2,88]{1,0:T(2,128)S(1)} %bitcast.16, bf16[2,88,128,128]{3,2,1,0:T(8,128)(2,1)S(1)} %bitcast.14), custom_call_target="tpu_custom_call" | custom-call | bytes 20971520 | tf_op jit(solution)/shard_map/densify/pallas_call | solution.py:103
  22.0 0.0 copy-start.2
  22.0 1.4 %copy-done.2 = bf16[2,384,1536]{2,1,0:T(8,128)(2,1)} copy-done((bf16[2,384,1536]{2,1,0:T(8,128)(2,1)}, bf16[2,384,1536]{2,1,0:T(8,128)(2,1)S(1)}, u32[]{:S(2)}) %copy-start.2) | copy-done | bytes 2359320
  23.4 0.0 copy-start.4
  23.4 1.4 %copy-done.4 = bf16[2,384,1536]{2,1,0:T(8,128)(2,1)} copy-done((bf16[2,384,1536]{2,1,0:T(8,128)(2,1)}, bf16[2,384,1536]{2,1,0:T(8,128)(2,1)S(1)}, u32[]{:S(2)}) %copy-start.4) | copy-done | bytes 2359320
  24.8 0.0 collective-permute-done.1.refs_1_
  24.8 9.0 %collective-permute-done.refs_0_ = bf16[1536,256]{1,0:T(8,128)(2,1)S(1)} collective-permute-done((bf16[1536,256]{1,0:T(8,128)(2,1)}, bf16[1536,256]{1,0:T(8,128)(2,1)S(1)}, u32[]{:S(2)}, u32[]{:S(2)}) %collective-permute-start) | collective-permute-done | bytes 786464 | tf_op jit(solution)/shard_map/ppermute | solution.py:21
  33.8 0.0 copy-start.1
  33.8 0.0 copy-start.7
  33.8 2.8 %send_rows.1 = f32[768,256]{1,0:T(8,128)} custom-call(s32[3]{0:T(128)S(1)} %pad_add_fusion.place, bf16[2,768,1536]{2,1,0:T(8,128)(2,1)S(1)} %get-tuple-element.11.dense, bf16[1536,256]{1,0:T(8,128)(2,1)S(1)} %collective-permute-done.refs_0_, bf16[1536,256]{1,0:T(8,128)(2,1)S(1)} %collective-permute-done.1.refs_1_), custom_call_target="tpu_custom_call" | custom-call | flops 603979776 | bytes 2359296 | tf_op jit(solution)/shard_map/send_rows/pallas_call | solution.py:145
  36.7 0.0 collective-permute-start.2
  36.7 0.0 copy-start.3
  36.7 0.0 copy-start.5
  36.7 1.8 %copy-done.5 = bf16[2,384,1536]{2,1,0:T(8,128)(2,1)S(1)} copy-done((bf16[2,384,1536]{2,1,0:T(8,128)(2,1)S(1)}, bf16[2,384,1536]{2,1,0:T(8,128)(2,1)}, u32[]{:S(2)}) %copy-start.5) | copy-done | bytes 2359320
  38.5 0.0 copy-start.6
  38.5 0.0 copy-start.8
  38.5 1.3 %mid_rows.1 = f32[384,256]{1,0:T(8,128)S(1)} custom-call(s32[3]{0:T(128)S(1)} %pad_add_fusion.place, bf16[2,384,1536]{2,1,0:T(8,128)(2,1)S(1)} %copy-done.5, bf16[1536,256]{1,0:T(8,128)(2,1)S(1)} %collective-permute-done.refs_0_, bf16[1536,256]{1,0:T(8,128)(2,1)S(1)} %collective-permute-done.1.refs_1_), custom_call_target="tpu_custom_call" | custom-call | flops 150994944 | bytes 589824 | tf_op jit(solution)/shard_map/mid_rows/pallas_call | solution.py:145
  39.8 0.0 collective-permute-done.2.received
  39.8 0.1 add_convert_fusion
  39.9 8.8 %collective-permute-start.3 = (bf16[384,256]{1,0:T(8,128)(2,1)S(1)}, bf16[384,256]{1,0:T(8,128)(2,1)S(1)}, u32[]{:S(2)}, u32[]{:S(2)}) collective-permute-start(bf16[384,256]{1,0:T(8,128)(2,1)S(1)} %add_convert_fusion), channel_id=1, source_target_pairs={{0,2},{1,3},{2,0},{3,1},{4,6},{5,7},{6,4},{7,5},{8,10},{9,11},{10,... | collective-permute-start | bytes 589832 | tf_op jit(solution)/shard_map/ppermute | solution.py:26
  48.7 0.0 copy-done.1
  48.7 0.0 copy-done.7
  48.7 0.0 copy-done.3
  48.7 1.4 %own_rows.1 = (f32[384,256]{1,0:T(8,128)S(1)}, f32[384,256]{1,0:T(8,128)S(1)}) custom-call(s32[3]{0:T(128)S(1)} %pad_add_fusion.place, bf16[1536,256]{1,0:T(8,128)(2,1)S(1)} %copy-done.1, f32[768,256]{1,0:T(8,128)S(1)} %collective-permute-done.2.received, bf16[256,256]{1,0:T(8,128)(2,1)S(1)} %copy-done.7, bf16[2,384,1536]{2,1,0:T(8,128)(2,1)S(1)} %copy-done.3, ...), custom_call_target="tpu_custom_call" | custom-call | flops 150994944 | bytes 589824 | tf_op jit(solution)/shard_map/own_rows/pallas_call | solution.py:145
  50.1 4.2 %collective-permute-done.3.side = bf16[384,256]{1,0:T(8,128)(2,1)S(1)} collective-permute-done((bf16[384,256]{1,0:T(8,128)(2,1)S(1)}, bf16[384,256]{1,0:T(8,128)(2,1)S(1)}, u32[]{:S(2)}, u32[]{:S(2)}) %collective-permute-start.3) | collective-permute-done | bytes 196640 | tf_op jit(solution)/shard_map/ppermute | solution.py:26
  54.3 0.0 copy-done.6
  54.3 0.0 copy-done.8
  54.3 1.6 %layer.1 = (bf16[384,256]{1,0:T(8,128)(2,1)}, f32[256,256]{1,0:T(8,128)S(1)}, f32[256,256]{1,0:T(8,128)S(1)}) custom-call(s32[3]{0:T(128)S(1)} %pad_add_fusion.place, bf16[1536,256]{1,0:T(8,128)(2,1)S(1)} %copy-done.1, f32[384,256]{1,0:T(8,128)S(1)} %get-tuple-element.13.own, bf16[384,256]{1,0:T(8,128)(2,1)S(1)} %collective-permute-done.3.side, ...), custom_call_target="tpu_custom_call" | custom-call | tf_op jit(solution)/shard_map/layer/pallas_call | solution.py:182
  55.8 0.0 collective-permute-start.4
  55.8 1.5 %collective-permute-done.4 = f32[256,256]{1,0:T(8,128)S(1)} collective-permute-done((f32[256,256]{1,0:T(8,128)S(1)}, f32[256,256]{1,0:T(8,128)S(1)}, u32[]{:S(2)}, u32[]{:S(2)}) %collective-permute-start.4) | collective-permute-done | bytes 262176 | tf_op jit(solution)/shard_map/ppermute | solution.py:26
  57.4 12.5 %all_to_all.21 = bf16[32,8,256]{2,1,0:T(8,128)(2,1)S(1)} all-to-all(bf16[32,8,256]{2,1,0:T(8,128)(2,1)S(1)} %fusion), channel_id=1, replica_groups=mesh['dom'=8,'rep'=4] {'dom','rep'}, dimensions={0} | all-to-all | bytes 262144 | tf_op jit(solution)/shard_map/all_to_all | solution.py:196
  69.9 10.0 %all_to_all.22 = bf16[32,8,256]{2,1,0:T(8,128)(2,1)S(1)} all-to-all(bf16[32,8,256]{2,1,0:T(8,128)(2,1)S(1)} %bitcast.19), channel_id=1, replica_groups=mesh['dom'=8,'rep'=4] {'dom','rep'}, dimensions={0} | all-to-all | bytes 262144 | tf_op jit(solution)/shard_map/all_to_all | solution.py:199
  79.9 0.2 collective-permute-start.5
  80.1 1.1 %collective-permute-done.5 = bf16[256,256]{1,0:T(8,128)(2,1)S(1)} collective-permute-done((bf16[256,256]{1,0:T(8,128)(2,1)S(1)}, bf16[256,256]{1,0:T(8,128)(2,1)S(1)}, u32[]{:S(2)}, u32[]{:S(2)}) %collective-permute-start.5) | collective-permute-done | bytes 131104 | tf_op jit(solution)/shard_map/ppermute | solution.py:26
  81.2 0.8 %select_convert_fusion = (f32[256,256]{1,0:T(8,128)}, f32[256,256]{1,0:T(8,128)}) fusion(bf16[256,256]{1,0:T(8,128)(2,1)S(1)} %collective-permute-done.5, pred[]{:T(512)S(6)} %eq.5, bf16[32,8,256]{2,1,0:T(8,128)(2,1)S(1)} %all_to_all.22), kind=kLoop, calls=%fused_computation.3 | loop fusion | flops 262144 | bytes 786433 | tf_op jit(solution)/shard_map/convert_element_type | solution.py:203
  (3 shorter events, 0.1 us)
Async XLA Ops:
  0.6 24.2 %collective-permute-start.1 = (bf16[1536,256]{1,0:T(8,128)(2,1)}, bf16[1536,256]{1,0:T(8,128)(2,1)S(1)}, u32[]{:S(2)}, u32[]{:S(2)}) collective-permute-start(bf16[1536,256]{1,0:T(8,128)(2,1)} %features.3), channel_id=1, source_target_pairs={{2,0},{11,1},{16,2},{25,3},{6,4},{15,5},{20,6},{29,7},{10,8},{19,9... | collective-permute-start | bytes 2359304 | tf_op jit(solution)/shard_map/ppermute | solution.py:21
  5.6 28.2 %collective-permute-start = (bf16[1536,256]{1,0:T(8,128)(2,1)}, bf16[1536,256]{1,0:T(8,128)(2,1)S(1)}, u32[]{:S(2)}, u32[]{:S(2)}) collective-permute-start(bf16[1536,256]{1,0:T(8,128)(2,1)} %features.3), channel_id=1, source_target_pairs={{28,0},{5,1},{14,2},{23,3},{0,4},{9,5},{18,6},{27,7},{4,8},{13,9},... | collective-permute-start | bytes 2359304 | tf_op jit(solution)/shard_map/ppermute | solution.py:21
  7.2 2.6 %copy-start = (bf16[1,1,2,88,128,128]{5,4,3,2,1,0:T(8,128)(2,1)S(1)}, bf16[1,1,2,88,128,128]{5,4,3,2,1,0:T(8,128)(2,1)}, u32[]{:S(2)}) copy-start(bf16[1,1,2,88,128,128]{5,4,3,2,1,0:T(8,128)(2,1)} %param.9) | copy-start | bytes 17301508
  9.9 0.7 copy-start.9
  10.6 0.7 copy-start.10
  11.2 0.7 copy-start.11
  22.0 1.4 %copy-start.2 = (bf16[2,384,1536]{2,1,0:T(8,128)(2,1)}, bf16[2,384,1536]{2,1,0:T(8,128)(2,1)S(1)}, u32[]{:S(2)}) copy-start(bf16[2,384,1536]{2,1,0:T(8,128)(2,1)S(1)} %get-tuple-element.12.dense) | copy-start | bytes 7077892
  23.4 1.4 %copy-start.4 = (bf16[2,384,1536]{2,1,0:T(8,128)(2,1)}, bf16[2,384,1536]{2,1,0:T(8,128)(2,1)S(1)}, u32[]{:S(2)}) copy-start(bf16[2,384,1536]{2,1,0:T(8,128)(2,1)S(1)} %get-tuple-element.14.dense) | copy-start | bytes 7077892
  33.8 14.9 %copy-start.1 = (bf16[1536,256]{1,0:T(8,128)(2,1)S(1)}, bf16[1536,256]{1,0:T(8,128)(2,1)}, u32[]{:S(2)}) copy-start(bf16[1536,256]{1,0:T(8,128)(2,1)} %features.3) | copy-start | bytes 2359300
  33.8 14.9 %copy-start.7 = (bf16[256,256]{1,0:T(8,128)(2,1)S(1)}, bf16[256,256]{1,0:T(8,128)(2,1)}, u32[]{:S(2)}) copy-start(bf16[256,256]{1,0:T(8,128)(2,1)} %weight_self.1) | copy-start | bytes 393220
  36.7 3.1 %collective-permute-start.2 = (f32[768,256]{1,0:T(8,128)}, f32[768,256]{1,0:T(8,128)S(1)}, u32[]{:S(2)}, u32[]{:S(2)}) collective-permute-start(f32[768,256]{1,0:T(8,128)} %send_rows.1), channel_id=1, source_target_pairs={{0,1},{1,0},{2,3},{3,2},{4,5},{5,4},{6,7},{7,6},{8,9},{9,8},{10,11... | collective-permute-start | bytes 2359304 | tf_op jit(solution)/shard_map/ppermute | solution.py:26
  36.7 12.0 %copy-start.3 = (bf16[2,384,1536]{2,1,0:T(8,128)(2,1)S(1)}, bf16[2,384,1536]{2,1,0:T(8,128)(2,1)}, u32[]{:S(2)}) copy-start(bf16[2,384,1536]{2,1,0:T(8,128)(2,1)} %copy-done.2) | copy-start | bytes 7077892
  36.7 1.8 %copy-start.5 = (bf16[2,384,1536]{2,1,0:T(8,128)(2,1)S(1)}, bf16[2,384,1536]{2,1,0:T(8,128)(2,1)}, u32[]{:S(2)}) copy-start(bf16[2,384,1536]{2,1,0:T(8,128)(2,1)} %copy-done.4) | copy-start | bytes 7077892
  38.5 15.8 %copy-start.6 = (bf16[384,256]{1,0:T(8,128)(2,1)S(1)}, bf16[384,256]{1,0:T(8,128)(2,1)}, u32[]{:S(2)}) copy-start(bf16[384,256]{1,0:T(8,128)(2,1)} %cotangent.1) | copy-start | bytes 589828
  38.5 15.8 %copy-start.8 = (bf16[256,256]{1,0:T(8,128)(2,1)S(1)}, bf16[256,256]{1,0:T(8,128)(2,1)}, u32[]{:S(2)}) copy-start(bf16[256,256]{1,0:T(8,128)(2,1)} %weight_neigh.1) | copy-start | bytes 393220
  39.9 14.4 %collective-permute-start.3 = (bf16[384,256]{1,0:T(8,128)(2,1)S(1)}, bf16[384,256]{1,0:T(8,128)(2,1)S(1)}, u32[]{:S(2)}, u32[]{:S(2)}) collective-permute-start(bf16[384,256]{1,0:T(8,128)(2,1)S(1)} %add_convert_fusion), channel_id=1, source_target_pairs={{0,2},{1,3},{2,0},{3,1},{4,6},{5,7},{6,4},{7,5},{8,10},{9,11},{10,... | collective-permute-start | bytes 589832 | tf_op jit(solution)/shard_map/ppermute | solution.py:26
  55.8 1.5 %collective-permute-start.4 = (f32[256,256]{1,0:T(8,128)S(1)}, f32[256,256]{1,0:T(8,128)S(1)}, u32[]{:S(2)}, u32[]{:S(2)}) collective-permute-start(f32[256,256]{1,0:T(8,128)S(1)} %get-tuple-element.18), channel_id=1, source_target_pairs={{0,1},{1,0},{2,3},{3,2},{4,5},{5,4},{6,7},{7,6},{8,9},{9,8},{10,11... | collective-permute-start | bytes 786440 | tf_op jit(solution)/shard_map/ppermute | solution.py:26
  79.9 1.3 %collective-permute-start.5 = (bf16[256,256]{1,0:T(8,128)(2,1)S(1)}, bf16[256,256]{1,0:T(8,128)(2,1)S(1)}, u32[]{:S(2)}, u32[]{:S(2)}) collective-permute-start(bf16[256,256]{1,0:T(8,128)(2,1)S(1)} %bitcast.20), channel_id=1, source_target_pairs={{0,1},{1,0},{2,3},{3,2},{4,5},{5,4},{6,7},{7,6},{8,9},{9,8},{10,11... | collective-permute-start | bytes 393224 | tf_op jit(solution)/shard_map/ppermute | solution.py:26

commit v3 on v2

v3 whole, which is shorter than its diff:
```python
import functools

import jax
import jax.numpy as jnp
from jax import lax
from jax.experimental import pallas as pl
from jax.experimental.pallas import tpu as pltpu
from jax.sharding import PartitionSpec as P

AXES = ("dom", "rep")
F32, BF16 = jnp.float32, jnp.bfloat16
MIB = 1 << 20
SHIFT = 16


def position():
    rep = lax.axis_index("rep").astype(jnp.int32)
    return rep, rep // 2, rep % 2


def flat_permute(value, blocks, groups, source):
    route = []
    for p in range(blocks):
        for r in range(groups):
            at = source(p, r)
            if at is not None:
                route.append((at[0] % blocks * groups + at[1] % groups, p * groups + r))
    return lax.ppermute(value, AXES, route)


def rep_exchange(value, groups, bit):
    route = [(r, r ^ (1 << bit)) for r in range(groups)]
    return lax.ppermute(value, "rep", route)


def fetch_blocks(features, blocks, groups, steps):
    found = []
    for s in range(steps):
        flip = groups // 2 if s % 2 else 0

        def source(p, r, s=s, flip=flip):
            ahead = r * steps + s - steps // 2
            return (p + ahead, r ^ flip) if ahead or steps > 2 else None

        found.append(flat_permute(features, blocks, groups, source))
    return found


def densify_kernel(pieces, table, weights, *refs):
    outs, (zero_rows, sem) = refs[:-2], refs[-2:]
    tile = weights.shape[2]
    slots = weights.shape[1]
    filled = [
        (outs[at].at[i] if len(outs[at].shape) == 3 else outs[at], s, first)
        for at, i, s, first in pieces
    ]
    zero_rows[...] = jnp.zeros_like(zero_rows)

    def clear(ref, i):
        return pltpu.make_async_copy(zero_rows, ref.at[pl.ds(i * tile, tile), :], sem)

    for ref, _, _ in filled:

        @pl.loop(0, ref.shape[0] // tile)
        def _(i, ref=ref):
            clear(ref, i).start()

    for ref, _, _ in filled:

        @pl.loop(0, ref.shape[0] // tile)
        def _(i, ref=ref):
            clear(ref, i).wait()

    started = jnp.int32(0)
    for ref, s, first in filled:
        held = ref.shape[0] // tile
        whole = held * tile == zero_rows.shape[1]

        def place_slot(k, total, ref=ref, s=s, first=first, held=held, whole=whole):
            spot = table[s, k]
            row, col = (spot >> SHIFT) - first, spot & ((1 << SHIFT) - 1)

            def start():
                pltpu.make_async_copy(
                    weights.at[s, k],
                    ref.at[
                        pl.ds(pl.multiple_of(row * tile, tile), tile),
                        pl.ds(pl.multiple_of(col * tile, tile), tile),
                    ],
                    sem,
                ).start()

            if whole:
                start()
                return total + 1
            inside = jnp.logical_and(row >= 0, row < held)
            pl.when(inside)(start)
            return total + inside.astype(jnp.int32)

        started = lax.fori_loop(0, table[s, slots], place_slot, started)

    largest = 1
    while largest * 2 <= slots:
        largest *= 2

    def wait(tiles):
        some = weights.at[0, pl.ds(0, tiles)]
        pltpu.make_async_copy(some, some, sem).wait()

    @pl.loop(0, started // largest)
    def _(_):
        wait(largest)

    amount = largest // 2
    while amount:

        @pl.when(started & amount != 0)
        def _(amount=amount):
            wait(amount)

        amount //= 2


def densify(limit, table, weights, pieces, out_shape, name):
    tile = weights.shape[2]
    nodes = out_shape[0].shape[-1]
    hbm = pl.BlockSpec(memory_space=pl.ANY)
    size = sum(v.size for v in out_shape)
    return pl.pallas_call(
        functools.partial(densify_kernel, pieces),
        out_shape=out_shape,
        in_specs=[pl.BlockSpec(memory_space=pltpu.SMEM), hbm],
        out_specs=(hbm,) * len(out_shape),
        scratch_shapes=[pltpu.VMEM((tile, nodes), BF16), pltpu.SemaphoreType.DMA],
        compiler_params=pltpu.CompilerParams(vmem_limit_bytes=limit),
        cost_estimate=pl.CostEstimate(flops=0, bytes_accessed=6 * size, transcendentals=0),
        name=name,
    )(table, weights)


def spot_table(rows, cols, counts, order, part_tiles):
    part = rows // part_tiles
    row = rows % part_tiles
    for g, at in enumerate(order):
        row = row + jnp.where(part == g, at * part_tiles, 0)
    return jnp.concatenate([(row << SHIFT) + cols, counts[:, None]], axis=1)


def early_kernel(features, dense, *refs):
    found, outs = refs[:-3], refs[-3:]

    def run(blocks):
        at = 0
        for out in outs:
            rows = slice(at, at + out.shape[0])
            total = jnp.dot(dense[0, rows, :], blocks[0][...], preferred_element_type=F32)
            for s in range(1, len(blocks)):
                total = total + jnp.dot(dense[s, rows, :], blocks[s][...], preferred_element_type=F32)
            out[...] = total
            at += out.shape[0]

    if len(found) > 1:
        run(found)
        return
    rep, _, _ = position()
    pl.when(rep == 0)(lambda: run([features]))
    pl.when(rep != 0)(lambda: run(found))


def rows_kernel(begun, dense, block, out):
    out[...] = begun[...] + jnp.dot(dense[...], block[...], preferred_element_type=F32)


def mid_kernel(begun, dense, block, received, out):
    part = out.shape[0]
    _, side_at, _ = position()
    total = begun[...] + jnp.dot(dense[...], block[...], preferred_element_type=F32)
    total = total + received[pl.ds(pl.multiple_of((1 - side_at) * part, part), part), :]
    out[...] = total.astype(out.dtype)


def own_kernel(features, received, weight_self, begun, dense, block, own, projected):
    part = own.shape[0]
    rep, side_at, _ = position()
    own[...] = (
        begun[...]
        + jnp.dot(dense[...], block[...], preferred_element_type=F32)
        + received[pl.ds(pl.multiple_of(side_at * part, part), part), :]
    )
    mine = features[pl.ds(pl.multiple_of(rep * part, part), part), :]
    projected[...] = jnp.dot(mine, weight_self[...], preferred_element_type=F32)


def vmem_call(limit, kernel, out_shape, operands, name, flops=0):
    vmem = pl.BlockSpec(memory_space=pltpu.VMEM)
    held = sum(v.size * v.dtype.itemsize for v in (*operands, *jax.tree.leaves(out_shape)))
    return pl.pallas_call(
        kernel,
        out_shape=out_shape,
        in_specs=[vmem] * len(operands),
        out_specs=jax.tree.map(lambda _: vmem, out_shape),
        compiler_params=pltpu.CompilerParams(vmem_limit_bytes=limit),
        cost_estimate=pl.CostEstimate(flops=flops, bytes_accessed=held, transcendentals=0),
        name=name,
    )(*operands)


def layer_kernel(
    features, own, side, projected, weight_neigh, cotangent, out, grad_keep, grad_send
):
    part = own.shape[0]
    rep, _, core = position()
    mine = features[pl.ds(pl.multiple_of(rep * part, part), part), :]
    aggregate = (own[...] + side[...].astype(F32)).astype(BF16)
    pre = projected[...] + jnp.dot(aggregate, weight_neigh[...], preferred_element_type=F32)
    sigmoid = jax.nn.sigmoid(pre)
    out[...] = (pre * sigmoid).astype(BF16)
    slope = (cotangent[...].astype(F32) * sigmoid * (1.0 + pre * (1.0 - sigmoid))).astype(BF16)
    contract = (((0,), (0,)), ((), ()))
    grad_self = lax.dot_general(mine, slope, contract, preferred_element_type=F32)
    grad_neigh = lax.dot_general(aggregate, slope, contract, preferred_element_type=F32)
    first = core == 0
    grad_keep[...] = jnp.where(first, grad_self, grad_neigh)
    grad_send[...] = jnp.where(first, grad_neigh, grad_self)


def all_reduce_grads(core, keep, send, devices, groups):
    rows, width = keep.shape
    chunk = rows // devices
    chip = (keep + rep_exchange(send, groups, 0)).astype(BF16)
    terms = lax.all_to_all(chip, AXES, 0, 0, tiled=True)
    summed = terms.reshape(devices // 2, 2, chunk, width).astype(F32).sum(0).astype(BF16)
    spread = jnp.broadcast_to(summed[None], (devices // 2, 2, chunk, width)).reshape(rows, width)
    mine = lax.all_to_all(spread, AXES, 0, 0, tiled=True)
    other = rep_exchange(mine, groups, 0)
    first = core == 0
    grad_self = jnp.where(first, mine, other).astype(F32)
    grad_neigh = jnp.where(first, other, mine).astype(F32)
    return grad_self, grad_neigh


def on_device(
    features, tile_weights, tile_rows, tile_cols, tile_counts, weight_self, weight_neigh, cotangent
):
    blocks, groups = lax.axis_size("dom"), lax.axis_size("rep")
    steps = tile_weights.shape[2]
    nodes, width = features.shape
    rep, side_at, core = position()
    half = groups // 2
    others = [half + (jnp.int32(g // 2) == side_at) for g in range(groups)]
    order = [jnp.where(core == g % 2, others[g], g // 2) for g in range(groups)]
    part = nodes // groups
    part_tiles = part // tile_weights.shape[-1]
    table = spot_table(tile_rows[0, 0], tile_cols[0, 0], tile_counts[0, 0], order, part_tiles)
    weights = tile_weights[0, 0]
    limit = 2 * ((steps - 1) * nodes + (steps + 1) * width) * nodes + 4 * nodes * width + 8 * MIB
    row_parts = lambda n: jax.ShapeDtypeStruct((n * part, nodes), BF16)
    later = jax.ShapeDtypeStruct((steps - 1, nodes, nodes), BF16)
    send_piece = ((0, 0, 0, 0),)
    rest_pieces = tuple((0, s - 1, s, 0) for s in range(1, steps)) + (
        (1, 0, 0, half * part_tiles),
        (2, 0, 0, (half + 1) * part_tiles),
    )

    late_found, *early_found = fetch_blocks(features, blocks, groups, steps)
    (dense_send,) = densify(limit, table, weights, send_piece, (row_parts(half),), "densify_send")
    early, dense_mid, dense_own = densify(
        limit, table, weights, rest_pieces, (later, row_parts(1), row_parts(1)), "densify_rest"
    )
    quarter = jax.ShapeDtypeStruct((part, width), F32)
    halves = jax.ShapeDtypeStruct((nodes // 2, width), F32)
    square = jax.ShapeDtypeStruct((width, width), F32)
    per_row = 2 * nodes * width
    begun_send, begun_mid, begun_own = vmem_call(
        limit,
        early_kernel,
        (halves, quarter, quarter),
        (features, early, *early_found),
        "early_rows",
        (steps - 1) * nodes * per_row,
    )
    send = vmem_call(
        limit, rows_kernel, halves, (begun_send, dense_send, late_found), "send_rows", nodes // 2 * per_row
    )
    received = rep_exchange(send, groups, 0)
    across = vmem_call(
        limit,
        mid_kernel,
        jax.ShapeDtypeStruct((part, width), BF16),
        (begun_mid, dense_mid, late_found, received),
        "mid_rows",
        part * per_row,
    )
    side = rep_exchange(across, groups, 1)
    own, projected = vmem_call(
        limit,
        own_kernel,
        (quarter, quarter),
        (features, received, weight_self, begun_own, dense_own, late_found),
        "own_rows",
        part * per_row,
    )
    out, grad_keep, grad_send = vmem_call(
        limit,
        layer_kernel,
        (jax.ShapeDtypeStruct((part, width), BF16), square, square),
        (features, own, side, projected, weight_neigh, cotangent),
        "layer",
        6 * part * width * width,
    )
    grad_self, grad_neigh = all_reduce_grads(core, grad_keep, grad_send, blocks * groups, groups)
    return out, grad_self, grad_neigh


def solution(mesh):
    return jax.shard_map(
        on_device,
        mesh=mesh,
        in_specs=(
            P("dom", None),
            P("dom", "rep", None, None, None, None),
            P("dom", "rep", None, None),
            P("dom", "rep", None, None),
            P("dom", "rep", None),
            P(),
            P(),
            P(AXES, None),
        ),
        out_specs=(P(AXES, None), P(), P()),
        check_vma=False,
    )
```

time: 82.3 us -> 81.1 us (0.985)
  local copies, waits for them, and re-layouts: 9.33 us -> 3.41 us
  starting transfers between devices: 15.6 us -> 19 us
  waiting for transfers between devices: 15.8 us -> 18.3 us
  blocking collectives: 22.5 us -> 21.4 us
    unnamed x24 -> x10, local copies, waits for them, and re-layouts: 9.32 us -> 2.66 us
    ppermute x4, waiting for transfers between devices: 6.85 us -> 9.6 us  [rep_exchange(): return lax.ppermute(value, 'rep', route)]
    ppermute x2, starting transfers between devices: 6.54 us -> 8.49 us  [flat_permute(): return lax.ppermute(value, AXES, route)]
    ppermute x4, starting transfers between devices: 9.03 us -> 10.5 us  [rep_exchange(): return lax.ppermute(value, 'rep', route)]
    all_to_all x1, blocking collectives: 12.5 us -> 11.4 us  [all_reduce_grads(): terms = lax.all_to_all(chip, AXES, 0, 0, tiled=True)]
    pallas_call x5 -> x7, Pallas kernels: 17.2 us -> 16.4 us  [the longest x2 12.2 us: densify(): pl.pallas_call(functools.partial(densify_kernel, pieces), out_shape=out_s...]
  transfers between devices with their start and end apart: 6 -> 6, of which waited for: 4 -> 6; matrix products, arithmetic and copies ran while one was open for 0% -> 2% of each run, Pallas kernels for 16% -> 17%
where the time goes in v3:
time: 81.1 us; the launch traced here: 80.9 us
  blocking collectives  21.4 us (26%)
  starting transfers between devices  19 us (23%)
  waiting for transfers between devices  18.3 us (23%)
  Pallas kernels  16.4 us (20%)
  local copies, waits for them, and re-layouts  3.41 us (4%)
  other arithmetic  1.68 us (2%)
    pallas_call x2, Pallas kernels, densify(): pl.pallas_call(functools.partial(densify_kernel, pieces), out_shape=out_s...  12.2 us
    all_to_all x1, blocking collectives, all_reduce_grads(): terms = lax.all_to_all(chip, AXES, 0, 0, tiled=True)  11.4 us
    ppermute x4, starting transfers between devices, rep_exchange(): return lax.ppermute(value, 'rep', route)  10.5 us
    all_to_all x1, blocking collectives, all_reduce_grads(): mine = lax.all_to_all(spread, AXES, 0, 0, tiled=True)  10 us
    ppermute x4, waiting for transfers between devices, rep_exchange(): return lax.ppermute(value, 'rep', route)  9.6 us
    ppermute x2, waiting for transfers between devices, flat_permute(): return lax.ppermute(value, AXES, route)  8.72 us
    ppermute x2, starting transfers between devices, flat_permute(): return lax.ppermute(value, AXES, route)  8.49 us
    pallas_call x5, Pallas kernels, vmem_call(): pl.pallas_call(kernel, out_shape=out_shape, in_specs=[vmem] * len(operand...  4.17 us
  transfers between devices with their start and end apart: 6, of which 6 were waited for; matrix products, arithmetic and copies ran while one was open for 2% of the time, Pallas kernels for 17%

profile of v3, /device:TPU:0, one launch (start us, length us, event | category | flops | bytes accessed | tf_op | source)
XLA Modules:
  0.0 80.9 jit_solution(4733885978547255790)
XLA Ops:
  0.6 6.9 %collective-permute-start = (bf16[1536,256]{1,0:T(8,128)(2,1)}, bf16[1536,256]{1,0:T(8,128)(2,1)S(1)}, u32[]{:S(2)}, u32[]{:S(2)}) collective-permute-start(bf16[1536,256]{1,0:T(8,128)(2,1)} %features.5), channel_id=1, source_target_pairs={{11,1},{16,2},{25,3},{15,5},{20,6},{29,7},{19,9},{24,10},{1,11},{2... | collective-permute-start | bytes 2359304 | tf_op jit(solution)/shard_map/ppermute | solution.py:28
  7.6 1.6 %collective-permute-start.1 = (bf16[1536,256]{1,0:T(8,128)(2,1)}, bf16[1536,256]{1,0:T(8,128)(2,1)S(1)}, u32[]{:S(2)}, u32[]{:S(2)}) collective-permute-start(bf16[1536,256]{1,0:T(8,128)(2,1)} %features.5), channel_id=1, source_target_pairs={{28,0},{5,1},{14,2},{23,3},{0,4},{9,5},{18,6},{27,7},{4,8},{13,9},... | collective-permute-start | bytes 2359304 | tf_op jit(solution)/shard_map/ppermute | solution.py:28
  9.1 0.7 copy.11
  9.9 0.7 fusion.7
  10.6 0.1 pad_add_fusion.table
  10.7 0.0 copy-start
  10.7 2.6 %copy-done = bf16[1,1,2,88,128,128]{5,4,3,2,1,0:T(8,128)(2,1)S(1)} copy-done((bf16[1,1,2,88,128,128]{5,4,3,2,1,0:T(8,128)(2,1)S(1)}, bf16[1,1,2,88,128,128]{5,4,3,2,1,0:T(8,128)(2,1)}, u32[]{:S(2)}) %copy-start) | copy-done | bytes 5767192
  13.3 8.8 %densify_rest.1 = (bf16[1,1536,1536]{2,1,0:T(8,128)(2,1)S(1)}, bf16[384,1536]{1,0:T(8,128)(2,1)S(1)}, bf16[384,1536]{1,0:T(8,128)(2,1)S(1)}) custom-call(s32[2,89]{1,0:T(2,128)S(1)} %pad_add_fusion.table, bf16[2,88,128,128]{3,2,1,0:T(8,128)(2,1)S(1)} %bitcast.32), custom_call_target="tpu_custom_call" | custom-call | bytes 21233664 | tf_op jit(solution)/shard_map/densify_rest/pallas_call | solution.py:129
  22.2 0.0 copy-start.1
  22.2 3.4 %densify_send.1.dense = bf16[768,1536]{1,0:T(8,128)(2,1)S(1)} custom-call(s32[2,89]{1,0:T(2,128)S(1)} %pad_add_fusion.table, bf16[2,88,128,128]{3,2,1,0:T(8,128)(2,1)S(1)} %bitcast.33), custom_call_target="tpu_custom_call" | custom-call | bytes 7077888 | tf_op jit(solution)/shard_map/densify_send/pallas_call | solution.py:129
  25.6 0.3 collective-permute-done.refs_0_
  25.9 0.0 copy-done.1
  25.9 1.4 %early_rows.1 = (f32[768,256]{1,0:T(8,128)S(1)}, f32[384,256]{1,0:T(8,128)S(1)}, f32[384,256]{1,0:T(8,128)S(1)}) custom-call(bf16[1536,256]{1,0:T(8,128)(2,1)S(1)} %copy-done.1, bf16[1,1536,1536]{2,1,0:T(8,128)(2,1)S(1)} %get-tuple-element.14.dense, bf16[1536,256]{1,0:T(8,128)(2,1)S(1)} %collective-permute-done.refs_0_), custom_call_target="tpu_custom_call" | custom-call | flops 1207959552 | bytes 7864320 | tf_op jit(solution)/shard_map/early_rows/pallas_call | solution.py:197
  27.2 8.4 %collective-permute-done.1.block = bf16[1536,256]{1,0:T(8,128)(2,1)S(1)} collective-permute-done((bf16[1536,256]{1,0:T(8,128)(2,1)}, bf16[1536,256]{1,0:T(8,128)(2,1)S(1)}, u32[]{:S(2)}, u32[]{:S(2)}) %collective-permute-start.1) | collective-permute-done | bytes 786464 | tf_op jit(solution)/shard_map/ppermute | solution.py:28
  35.7 0.8 send_rows.1
  36.5 0.0 copy-start.3
  36.5 0.1 collective-permute-start.2
  36.5 2.3 %collective-permute-done.2.received = f32[768,256]{1,0:T(8,128)S(1)} collective-permute-done((f32[768,256]{1,0:T(8,128)S(1)}, f32[768,256]{1,0:T(8,128)S(1)}, u32[]{:S(2)}, u32[]{:S(2)}) %collective-permute-start.2) | collective-permute-done | bytes 786464 | tf_op jit(solution)/shard_map/ppermute | solution.py:33
  38.8 0.5 mid_rows.1
  39.3 0.0 copy-start.2
  39.3 0.0 copy-start.4
  39.3 10.2 %collective-permute-start.3 = (bf16[384,256]{1,0:T(8,128)(2,1)S(1)}, bf16[384,256]{1,0:T(8,128)(2,1)S(1)}, u32[]{:S(2)}, u32[]{:S(2)}) collective-permute-start(bf16[384,256]{1,0:T(8,128)(2,1)S(1)} %mid_rows.1), channel_id=1, source_target_pairs={{0,2},{1,3},{2,0},{3,1},{4,6},{5,7},{6,4},{7,5},{8,10},{9,11},{10,... | collective-permute-start | bytes 589832 | tf_op jit(solution)/shard_map/ppermute | solution.py:33
  49.5 0.0 copy-done.3
  49.5 0.5 own_rows.1
  50.1 4.7 %collective-permute-done.3.side = bf16[384,256]{1,0:T(8,128)(2,1)S(1)} collective-permute-done((bf16[384,256]{1,0:T(8,128)(2,1)S(1)}, bf16[384,256]{1,0:T(8,128)(2,1)S(1)}, u32[]{:S(2)}, u32[]{:S(2)}) %collective-permute-start.3) | collective-permute-done | bytes 196640 | tf_op jit(solution)/shard_map/ppermute | solution.py:33
  54.7 0.0 copy-done.2
  54.7 0.0 copy-done.4
  54.7 1.0 %layer.1 = (bf16[384,256]{1,0:T(8,128)(2,1)}, f32[256,256]{1,0:T(8,128)S(1)}, f32[256,256]{1,0:T(8,128)S(1)}) custom-call(bf16[1536,256]{1,0:T(8,128)(2,1)S(1)} %copy-done.1, f32[384,256]{1,0:T(8,128)S(1)} %get-tuple-element.18.own, bf16[384,256]{1,0:T(8,128)(2,1)S(1)} %collective-permute-done.3.side, f32[384,256]{1,0:T(8,128)S(1)} %get-tuple-element.21.projected, ...), custom_call_target="tpu_custom_call" | custom-call | flops 150994944 | bytes 2818048 | tf_op jit(solution)/shard_map/layer/pallas_call | solution.py:197
  55.7 0.0 collective-permute-start.4
  55.7 1.5 %collective-permute-done.4 = f32[256,256]{1,0:T(8,128)S(1)} collective-permute-done((f32[256,256]{1,0:T(8,128)S(1)}, f32[256,256]{1,0:T(8,128)S(1)}, u32[]{:S(2)}, u32[]{:S(2)}) %collective-permute-start.4) | collective-permute-done | bytes 262176 | tf_op jit(solution)/shard_map/ppermute | solution.py:33
  57.3 11.4 %all_to_all.21 = bf16[32,8,256]{2,1,0:T(8,128)(2,1)S(1)} all-to-all(bf16[32,8,256]{2,1,0:T(8,128)(2,1)S(1)} %fusion), channel_id=1, replica_groups=mesh['dom'=8,'rep'=4] {'dom','rep'}, dimensions={0} | all-to-all | bytes 262144 | tf_op jit(solution)/shard_map/all_to_all | solution.py:231
  68.7 10.0 %all_to_all.22 = bf16[32,8,256]{2,1,0:T(8,128)(2,1)S(1)} all-to-all(bf16[32,8,256]{2,1,0:T(8,128)(2,1)S(1)} %bitcast.35), channel_id=1, replica_groups=mesh['dom'=8,'rep'=4] {'dom','rep'}, dimensions={0} | all-to-all | bytes 262144 | tf_op jit(solution)/shard_map/all_to_all | solution.py:234
  78.7 0.2 collective-permute-start.5
  79.0 1.1 %collective-permute-done.5 = bf16[256,256]{1,0:T(8,128)(2,1)S(1)} collective-permute-done((bf16[256,256]{1,0:T(8,128)(2,1)S(1)}, bf16[256,256]{1,0:T(8,128)(2,1)S(1)}, u32[]{:S(2)}, u32[]{:S(2)}) %collective-permute-start.5) | collective-permute-done | bytes 131104 | tf_op jit(solution)/shard_map/ppermute | solution.py:33
  80.1 0.8 %select_convert_fusion = (f32[256,256]{1,0:T(8,128)}, f32[256,256]{1,0:T(8,128)}) fusion(bf16[256,256]{1,0:T(8,128)(2,1)S(1)} %collective-permute-done.5, pred[]{:T(512)S(6)} %eq.40, bf16[32,8,256]{2,1,0:T(8,128)(2,1)S(1)} %all_to_all.22), kind=kLoop, calls=%fused_computation.2 | loop fusion | flops 262144 | bytes 786433 | tf_op jit(solution)/shard_map/convert_element_type | solution.py:238
  (3 shorter events, 0.1 us)
Async XLA Ops:
  0.6 25.2 %collective-permute-start = (bf16[1536,256]{1,0:T(8,128)(2,1)}, bf16[1536,256]{1,0:T(8,128)(2,1)S(1)}, u32[]{:S(2)}, u32[]{:S(2)}) collective-permute-start(bf16[1536,256]{1,0:T(8,128)(2,1)} %features.5), channel_id=1, source_target_pairs={{11,1},{16,2},{25,3},{15,5},{20,6},{29,7},{19,9},{24,10},{1,11},{2... | collective-permute-start | bytes 2359304 | tf_op jit(solution)/shard_map/ppermute | solution.py:28
  7.6 28.1 %collective-permute-start.1 = (bf16[1536,256]{1,0:T(8,128)(2,1)}, bf16[1536,256]{1,0:T(8,128)(2,1)S(1)}, u32[]{:S(2)}, u32[]{:S(2)}) collective-permute-start(bf16[1536,256]{1,0:T(8,128)(2,1)} %features.5), channel_id=1, source_target_pairs={{28,0},{5,1},{14,2},{23,3},{0,4},{9,5},{18,6},{27,7},{4,8},{13,9},... | collective-permute-start | bytes 2359304 | tf_op jit(solution)/shard_map/ppermute | solution.py:28
  10.7 2.6 %copy-start = (bf16[1,1,2,88,128,128]{5,4,3,2,1,0:T(8,128)(2,1)S(1)}, bf16[1,1,2,88,128,128]{5,4,3,2,1,0:T(8,128)(2,1)}, u32[]{:S(2)}) copy-start(bf16[1,1,2,88,128,128]{5,4,3,2,1,0:T(8,128)(2,1)} %param.9) | copy-start | bytes 17301508
  22.2 3.7 %copy-start.1 = (bf16[1536,256]{1,0:T(8,128)(2,1)S(1)}, bf16[1536,256]{1,0:T(8,128)(2,1)}, u32[]{:S(2)}) copy-start(bf16[1536,256]{1,0:T(8,128)(2,1)} %features.5) | copy-start | bytes 2359300
  36.5 13.1 %copy-start.3 = (bf16[256,256]{1,0:T(8,128)(2,1)S(1)}, bf16[256,256]{1,0:T(8,128)(2,1)}, u32[]{:S(2)}) copy-start(bf16[256,256]{1,0:T(8,128)(2,1)} %weight_self.1) | copy-start | bytes 393220
  36.5 2.4 %collective-permute-start.2 = (f32[768,256]{1,0:T(8,128)S(1)}, f32[768,256]{1,0:T(8,128)S(1)}, u32[]{:S(2)}, u32[]{:S(2)}) collective-permute-start(f32[768,256]{1,0:T(8,128)S(1)} %send_rows.1), channel_id=1, source_target_pairs={{0,1},{1,0},{2,3},{3,2},{4,5},{5,4},{6,7},{7,6},{8,9},{9,8},{10,11... | collective-permute-start | bytes 2359304 | tf_op jit(solution)/shard_map/ppermute | solution.py:33
  39.3 15.4 %copy-start.2 = (bf16[384,256]{1,0:T(8,128)(2,1)S(1)}, bf16[384,256]{1,0:T(8,128)(2,1)}, u32[]{:S(2)}) copy-start(bf16[384,256]{1,0:T(8,128)(2,1)} %cotangent.1) | copy-start | bytes 589828
  39.3 15.4 %copy-start.4 = (bf16[256,256]{1,0:T(8,128)(2,1)S(1)}, bf16[256,256]{1,0:T(8,128)(2,1)}, u32[]{:S(2)}) copy-start(bf16[256,256]{1,0:T(8,128)(2,1)} %weight_neigh.1) | copy-start | bytes 393220
  39.3 15.4 %collective-permute-start.3 = (bf16[384,256]{1,0:T(8,128)(2,1)S(1)}, bf16[384,256]{1,0:T(8,128)(2,1)S(1)}, u32[]{:S(2)}, u32[]{:S(2)}) collective-permute-start(bf16[384,256]{1,0:T(8,128)(2,1)S(1)} %mid_rows.1), channel_id=1, source_target_pairs={{0,2},{1,3},{2,0},{3,1},{4,6},{5,7},{6,4},{7,5},{8,10},{9,11},{10,... | collective-permute-start | bytes 589832 | tf_op jit(solution)/shard_map/ppermute | solution.py:33
  55.7 1.5 %collective-permute-start.4 = (f32[256,256]{1,0:T(8,128)S(1)}, f32[256,256]{1,0:T(8,128)S(1)}, u32[]{:S(2)}, u32[]{:S(2)}) collective-permute-start(f32[256,256]{1,0:T(8,128)S(1)} %get-tuple-element.24), channel_id=1, source_target_pairs={{0,1},{1,0},{2,3},{3,2},{4,5},{5,4},{6,7},{7,6},{8,9},{9,8},{10,11... | collective-permute-start | bytes 786440 | tf_op jit(solution)/shard_map/ppermute | solution.py:33
  78.7 1.3 %collective-permute-start.5 = (bf16[256,256]{1,0:T(8,128)(2,1)S(1)}, bf16[256,256]{1,0:T(8,128)(2,1)S(1)}, u32[]{:S(2)}, u32[]{:S(2)}) collective-permute-start(bf16[256,256]{1,0:T(8,128)(2,1)S(1)} %bitcast.36), channel_id=1, source_target_pairs={{0,1},{1,0},{2,3},{3,2},{4,5},{5,4},{6,7},{7,6},{8,9},{9,8},{10,11... | collective-permute-start | bytes 393224 | tf_op jit(solution)/shard_map/ppermute | solution.py:33

commit v4 on v3

--- a/solution.py
+++ b/solution.py
@@ -39,11 +39,36 @@
         flip = groups // 2 if s % 2 else 0
 
         def source(p, r, s=s, flip=flip):
-            ahead = r * steps + s - steps // 2
-            return (p + ahead, r ^ flip) if ahead or steps > 2 else None
+            return p + r * steps + s - steps // 2, r ^ flip
 
         found.append(flat_permute(features, blocks, groups, source))
     return found
+
+
+class Routes:
+    def __init__(self, blocks, groups):
+        self.blocks, self.half, self.last = blocks, groups // 2, groups - 1
+
+    def ahead(self, p, r):
+        if r == self.half:
+            q = (p + 2 * r) % self.blocks
+            return q, self.half if q // 2 % 2 else 0
+        return (p + 2 * r - 1, 1) if r == 1 - p % 2 else None
+
+    def passed(self, p, r):
+        if p % 2 and r == self.half:
+            return p - 1, r
+        if p % 2 == 0 and r == self.last:
+            return p + 1, r - 1
+        return None
+
+    def later(self, p, r):
+        return (p + 2 * r, self.last + 1 - r) if r not in (0, self.half) else None
+
+    def first(self, p, r):
+        if self.passed(p, r) or r == 1 - p % 2:
+            return None
+        return p + 2 * r - 1, self.half if r in (0, self.last) else 1
 
 
 def densify_kernel(pieces, table, weights, *refs):
@@ -146,10 +171,29 @@
     return jnp.concatenate([(row << SHIFT) + cols, counts[:, None]], axis=1)
 
 
-def early_kernel(features, dense, *refs):
-    found, outs = refs[:-3], refs[-3:]
-
-    def run(blocks):
+def either(at, blocks, run):
+    if len(blocks) == 1:
+        run(blocks[0])
+        return
+    for i, block in enumerate(blocks):
+        pl.when(at == i)(functools.partial(run, block))
+
+
+def pick_early():
+    rep, _, _ = position()
+    return jnp.where(rep == 0, 0, jnp.where(rep == lax.axis_size("rep") // 2, 1, 2))
+
+
+def pick_late():
+    rep, _, _ = position()
+    odd = lax.axis_index("dom").astype(jnp.int32) % 2
+    return jnp.where(rep == 1 - odd, 2, jnp.where(rep == lax.axis_size("rep") // 2 + 1 - odd, 1, 0))
+
+
+def early_kernel(dense, *refs):
+    found, outs = refs[:-4], refs[-4:]
+
+    def run(*blocks):
         at = 0
         for out in outs:
             rows = slice(at, at + out.shape[0])
@@ -159,34 +203,41 @@
             out[...] = total
             at += out.shape[0]
 
-    if len(found) > 1:
-        run(found)
-        return
+    if dense.shape[0] > 1:
+        run(*found)
+    else:
+        either(pick_early(), found, run)
+
+
+def rows_kernel(begun, dense, *refs):
+    found, out = refs[:-1], refs[-1]
+
+    def run(block):
+        out[...] = begun[...] + jnp.dot(dense[...], block[...], preferred_element_type=F32)
+
+    either(pick_late(), found, run)
+
+
+def mid_kernel(received, begun, dense, *refs):
+    found, out = refs[:-1], refs[-1]
+
+    def run(block):
+        total = begun[...] + jnp.dot(dense[...], block[...], preferred_element_type=F32)
+        out[...] = (total + received[...]).astype(out.dtype)
+
+    either(pick_late(), found, run)
+
+
+def own_kernel(features, received, weight_self, begun, dense, *refs):
+    found, (own, projected) = refs[:-2], refs[-2:]
+    part = own.shape[0]
     rep, _, _ = position()
-    pl.when(rep == 0)(lambda: run([features]))
-    pl.when(rep != 0)(lambda: run(found))
-
-
-def rows_kernel(begun, dense, block, out):
-    out[...] = begun[...] + jnp.dot(dense[...], block[...], preferred_element_type=F32)
-
-
-def mid_kernel(begun, dense, block, received, out):
-    part = out.shape[0]
-    _, side_at, _ = position()
-    total = begun[...] + jnp.dot(dense[...], block[...], preferred_element_type=F32)
-    total = total + received[pl.ds(pl.multiple_of((1 - side_at) * part, part), part), :]
-    out[...] = total.astype(out.dtype)
-
-
-def own_kernel(features, received, weight_self, begun, dense, block, own, projected):
-    part = own.shape[0]
-    rep, side_at, _ = position()
-    own[...] = (
-        begun[...]
-        + jnp.dot(dense[...], block[...], preferred_element_type=F32)
-        + received[pl.ds(pl.multiple_of(side_at * part, part), part), :]
-    )
+
+    def run(block):
+        total = begun[...] + jnp.dot(dense[...], block[...], preferred_element_type=F32)
+        own[...] = total + received[...]
+
+    either(pick_late(), found, run)
     mine = features[pl.ds(pl.multiple_of(rep * part, part), part), :]
     projected[...] = jnp.dot(mine, weight_self[...], preferred_element_type=F32)
 
@@ -247,47 +298,60 @@
     nodes, width = features.shape
     rep, side_at, core = position()
     half = groups // 2
-    others = [half + (jnp.int32(g // 2) == side_at) for g in range(groups)]
-    order = [jnp.where(core == g % 2, others[g], g // 2) for g in range(groups)]
+    order = [
+        jnp.where(core == g % 2, half, 0) + jnp.where(side_at == g // 2, 1, 0) for g in range(groups)
+    ]
     part = nodes // groups
     part_tiles = part // tile_weights.shape[-1]
     table = spot_table(tile_rows[0, 0], tile_cols[0, 0], tile_counts[0, 0], order, part_tiles)
     weights = tile_weights[0, 0]
     limit = 2 * ((steps - 1) * nodes + (steps + 1) * width) * nodes + 4 * nodes * width + 8 * MIB
-    row_parts = lambda n: jax.ShapeDtypeStruct((n * part, nodes), BF16)
+    row_parts = jax.ShapeDtypeStruct((part, nodes), BF16)
     later = jax.ShapeDtypeStruct((steps - 1, nodes, nodes), BF16)
-    send_piece = ((0, 0, 0, 0),)
+    send_pieces = ((0, 0, 0, 0), (1, 0, 0, part_tiles))
     rest_pieces = tuple((0, s - 1, s, 0) for s in range(1, steps)) + (
         (1, 0, 0, half * part_tiles),
         (2, 0, 0, (half + 1) * part_tiles),
     )
 
-    late_found, *early_found = fetch_blocks(features, blocks, groups, steps)
-    (dense_send,) = densify(limit, table, weights, send_piece, (row_parts(half),), "densify_send")
+    special = steps == 2 and groups == 4 and blocks == steps * groups
+    routes = Routes(blocks, groups)
+    move = lambda value, source: flat_permute(value, blocks, groups, source)
+    waited = features
+    if special:
+        ahead = move(features, routes.ahead)
+    dense_send = densify(limit, table, weights, send_pieces, (row_parts,) * half, "densify_send")
+    if special:
+        waited, dense_send = lax.optimization_barrier((features, dense_send))
+        early_found = (features, ahead, move(waited, routes.later))
+        late_found = (move(waited, routes.first), move(ahead, routes.passed), ahead)
+    else:
+        late, *early_found = fetch_blocks(features, blocks, groups, steps)
+        late_found = (late,)
     early, dense_mid, dense_own = densify(
-        limit, table, weights, rest_pieces, (later, row_parts(1), row_parts(1)), "densify_rest"
+        limit, table, weights, rest_pieces, (later, row_parts, row_parts), "densify_rest"
     )
     quarter = jax.ShapeDtypeStruct((part, width), F32)
-    halves = jax.ShapeDtypeStruct((nodes // 2, width), F32)
     square = jax.ShapeDtypeStruct((width, width), F32)
     per_row = 2 * nodes * width
-    begun_send, begun_mid, begun_own = vmem_call(
+    *begun_send, begun_mid, begun_own = vmem_call(
         limit,
         early_kernel,
-        (halves, quarter, quarter),
-        (features, early, *early_found),
+        (quarter,) * groups,
+        (early, *early_found),
         "early_rows",
         (steps - 1) * nodes * per_row,
     )
-    send = vmem_call(
-        limit, rows_kernel, halves, (begun_send, dense_send, late_found), "send_rows", nodes // 2 * per_row
-    )
-    received = rep_exchange(send, groups, 0)
+    send = [
+        vmem_call(limit, rows_kernel, quarter, (begun, dense, *late_found), name, part * per_row)
+        for begun, dense, name in zip(begun_send, dense_send, ("send_other_side", "send_this_side"))
+    ]
+    received = [rep_exchange(rows, groups, 0) for rows in send]
     across = vmem_call(
         limit,
         mid_kernel,
         jax.ShapeDtypeStruct((part, width), BF16),
-        (begun_mid, dense_mid, late_found, received),
+        (received[0], begun_mid, dense_mid, *late_found),
         "mid_rows",
         part * per_row,
     )
@@ -296,7 +360,7 @@
         limit,
         own_kernel,
         (quarter, quarter),
-        (features, received, weight_self, begun_own, dense_own, late_found),
+        (features, received[1], weight_self, begun_own, dense_own, *late_found),
         "own_rows",
         part * per_row,
     )

time: 81.1 us -> 79 us (0.974)
  starting transfers between devices: 19 us -> 14.1 us
  waiting for transfers between devices: 18.3 us -> 22.9 us
  Pallas kernels: 16.4 us -> 12.2 us
  blocking collectives: 21.4 us -> 23.9 us
    ppermute x2 -> x4, waiting for transfers between devices: 8.72 us -> 14.8 us  [flat_permute(): return lax.ppermute(value, AXES, route)]
    ppermute x4 -> x5, starting transfers between devices: 10.5 us -> 4.46 us  [rep_exchange(): return lax.ppermute(value, 'rep', route)]
    pallas_call x2, Pallas kernels: 12.2 us -> 7.65 us  [densify(): pl.pallas_call(functools.partial(densify_kernel, pieces), out_shape=out_s...]
    all_to_all x1, blocking collectives: 11.4 us -> 13.9 us  [all_reduce_grads(): terms = lax.all_to_all(chip, AXES, 0, 0, tiled=True)]
    ppermute x4 -> x5, waiting for transfers between devices: 9.6 us -> 8.04 us  [rep_exchange(): return lax.ppermute(value, 'rep', route)]
    ppermute x2 -> x4, starting transfers between devices: 8.49 us -> 9.62 us  [flat_permute(): return lax.ppermute(value, AXES, route)]
    pallas_call x5 -> x6, Pallas kernels: 4.17 us -> 4.56 us  [vmem_call(): pl.pallas_call(kernel, out_shape=out_shape, in_specs=[vmem] * len(operand...]
  transfers between devices with their start and end apart: 6 -> 9, of which waited for: 6 -> 6; matrix products, arithmetic and copies ran while one was open for 2% -> 2% of each run, Pallas kernels for 17% -> 14%
where the time goes in v4:
time: 79 us
  blocking collectives  23.9 us (30%)
  waiting for transfers between devices  22.9 us (29%)
  starting transfers between devices  14.1 us (18%)
  Pallas kernels  12.2 us (15%)
  local copies, waits for them, and re-layouts  3.4 us (4%)
  other arithmetic  1.68 us (2%)
  between operations  0.82 us (1%)
    ppermute x4, waiting for transfers between devices, flat_permute(): return lax.ppermute(value, AXES, route)  14.8 us
    all_to_all x1, blocking collectives, all_reduce_grads(): terms = lax.all_to_all(chip, AXES, 0, 0, tiled=True)  13.9 us
    all_to_all x1, blocking collectives, all_reduce_grads(): mine = lax.all_to_all(spread, AXES, 0, 0, tiled=True)  10 us
    ppermute x4, starting transfers between devices, flat_permute(): return lax.ppermute(value, AXES, route)  9.62 us
    ppermute x5, waiting for transfers between devices, rep_exchange(): return lax.ppermute(value, 'rep', route)  8.04 us
    pallas_call x2, Pallas kernels, densify(): pl.pallas_call(functools.partial(densify_kernel, pieces), out_shape=out_s...  7.65 us
    pallas_call x6, Pallas kernels, vmem_call(): pl.pallas_call(kernel, out_shape=out_shape, in_specs=[vmem] * len(operand...  4.56 us
    ppermute x5, starting transfers between devices, rep_exchange(): return lax.ppermute(value, 'rep', route)  4.46 us
  transfers between devices with their start and end apart: 9, of which 6 were waited for; matrix products, arithmetic and copies ran while one was open for 2% of the time, Pallas kernels for 14%

profile of v4, /device:TPU:0, one launch (start us, length us, event | category | flops | bytes accessed | tf_op | source)
XLA Modules:
  0.0 79.0 jit_solution(9222831309243260194)
XLA Ops:
  0.6 6.9 %collective-permute-start = (bf16[1536,256]{1,0:T(8,128)(2,1)}, bf16[1536,256]{1,0:T(8,128)(2,1)S(1)}, u32[]{:S(2)}, u32[]{:S(2)}) collective-permute-start(bf16[1536,256]{1,0:T(8,128)(2,1)} %features.3), channel_id=1, source_target_pairs={{5,1},{16,2},{1,4},{20,6},{13,9},{26,10},{9,12},{30,14},{21,17},{0... | collective-permute-start | bytes 2359304 | tf_op jit(solution)/shard_map/ppermute | solution.py:28
  7.6 0.7 copy.11
  8.3 0.7 fusion.7
  9.1 0.1 pad_add_fusion.table
  9.1 0.0 copy-start
  9.1 2.6 %copy-done = bf16[1,1,2,88,128,128]{5,4,3,2,1,0:T(8,128)(2,1)S(1)} copy-done((bf16[1,1,2,88,128,128]{5,4,3,2,1,0:T(8,128)(2,1)S(1)}, bf16[1,1,2,88,128,128]{5,4,3,2,1,0:T(8,128)(2,1)}, u32[]{:S(2)}) %copy-start) | copy-done | bytes 5767192
  11.8 0.0 copy-start.1
  11.8 2.5 %densify_send.1 = (bf16[384,1536]{1,0:T(8,128)(2,1)S(1)}, bf16[384,1536]{1,0:T(8,128)(2,1)S(1)}) custom-call(s32[2,89]{1,0:T(2,128)S(1)} %pad_add_fusion.table, bf16[2,88,128,128]{3,2,1,0:T(8,128)(2,1)S(1)} %bitcast.32), custom_call_target="tpu_custom_call" | custom-call | bytes 7077888 | tf_op jit(solution)/shard_map/densify_send/pallas_call | solution.py:154
  14.3 0.0 copy-done.1
  14.3 0.7 collective-permute-start.1
  15.0 1.3 %collective-permute-start.2 = (bf16[1536,256]{1,0:T(8,128)(2,1)S(1)}, bf16[1536,256]{1,0:T(8,128)(2,1)S(1)}, u32[]{:S(2)}, u32[]{:S(2)}) collective-permute-start(bf16[1536,256]{1,0:T(8,128)(2,1)S(1)} %copy-done.1), channel_id=1, source_target_pairs={{30,0},{13,2},{9,5},{26,7},{6,8},{21,10},{17,13},{2,15},{14,16},{2... | collective-permute-start | bytes 2359304 | tf_op jit(solution)/shard_map/ppermute | solution.py:28
  16.3 2.0 %collective-permute-done.refs_1_.refs_2_ = bf16[1536,256]{1,0:T(8,128)(2,1)S(1)} collective-permute-done((bf16[1536,256]{1,0:T(8,128)(2,1)}, bf16[1536,256]{1,0:T(8,128)(2,1)S(1)}, u32[]{:S(2)}, u32[]{:S(2)}) %collective-permute-start) | collective-permute-done | bytes 786464 | tf_op jit(solution)/shard_map/ppermute | solution.py:28
  18.4 0.7 collective-permute-start.3
  19.1 5.2 %densify_rest.1 = (bf16[1,1536,1536]{2,1,0:T(8,128)(2,1)S(1)}, bf16[384,1536]{1,0:T(8,128)(2,1)S(1)}, bf16[384,1536]{1,0:T(8,128)(2,1)S(1)}) custom-call(s32[2,89]{1,0:T(2,128)S(1)} %pad_add_fusion.table, bf16[2,88,128,128]{3,2,1,0:T(8,128)(2,1)S(1)} %bitcast.33), custom_call_target="tpu_custom_call" | custom-call | bytes 21233664 | tf_op jit(solution)/shard_map/densify_rest/pallas_call | solution.py:154
  24.2 0.0 collective-permute-done.1.refs_2_
  24.2 1.4 %early_rows.1 = (f32[384,256]{1,0:T(8,128)S(1)}, f32[384,256]{1,0:T(8,128)S(1)}, f32[384,256]{1,0:T(8,128)S(1)}, f32[384,256]{1,0:T(8,128)S(1)}) custom-call(bf16[1,1536,1536]{2,1,0:T(8,128)(2,1)S(1)} %get-tuple-element.20.dense, bf16[1536,256]{1,0:T(8,128)(2,1)S(1)} %copy-done.1, bf16[1536,256]{1,0:T(8,128)(2,1)S(1)} %collective-permute-done.refs_1_.refs_2_, ...), custom_call_target="tpu_custom_call" | custom-call | flops 1207959552 | bytes 8650752 | tf_op jit(solution)/shard_map/early_rows/pallas_call | solution.py:248
  25.6 12.8 %collective-permute-done.2.refs_0_ = bf16[1536,256]{1,0:T(8,128)(2,1)S(1)} collective-permute-done((bf16[1536,256]{1,0:T(8,128)(2,1)S(1)}, bf16[1536,256]{1,0:T(8,128)(2,1)S(1)}, u32[]{:S(2)}, u32[]{:S(2)}) %collective-permute-start.2) | collective-permute-done | bytes 786464 | tf_op jit(solution)/shard_map/ppermute | solution.py:28
  38.4 0.0 collective-permute-done.3.refs_1_
  38.4 0.5 send_other_side.1
  38.9 0.1 collective-permute-start.5
  39.0 0.5 send_this_side.1
  39.5 0.5 collective-permute-start.4
  40.0 0.7 collective-permute-done.5.received
  40.7 0.0 copy-start.3
  40.7 0.5 mid_rows.1
  41.2 3.6 %collective-permute-start.6 = (bf16[384,256]{1,0:T(8,128)(2,1)S(1)}, bf16[384,256]{1,0:T(8,128)(2,1)S(1)}, u32[]{:S(2)}, u32[]{:S(2)}) collective-permute-start(bf16[384,256]{1,0:T(8,128)(2,1)S(1)} %mid_rows.1), channel_id=1, source_target_pairs={{0,2},{1,3},{2,0},{3,1},{4,6},{5,7},{6,4},{7,5},{8,10},{9,11},{10,... | collective-permute-start | bytes 589832 | tf_op jit(solution)/shard_map/ppermute | solution.py:33
  44.8 0.0 collective-permute-done.4.received
  44.8 0.0 copy-done.3
  44.8 0.0 copy-start.2
  44.8 0.0 copy-start.4
  44.8 0.7 own_rows.1
  45.5 4.7 %collective-permute-done.6.side = bf16[384,256]{1,0:T(8,128)(2,1)S(1)} collective-permute-done((bf16[384,256]{1,0:T(8,128)(2,1)S(1)}, bf16[384,256]{1,0:T(8,128)(2,1)S(1)}, u32[]{:S(2)}, u32[]{:S(2)}) %collective-permute-start.6) | collective-permute-done | bytes 196640 | tf_op jit(solution)/shard_map/ppermute | solution.py:33
  50.2 0.0 copy-done.2
  50.2 0.0 copy-done.4
  50.2 1.0 %layer.1 = (bf16[384,256]{1,0:T(8,128)(2,1)}, f32[256,256]{1,0:T(8,128)S(1)}, f32[256,256]{1,0:T(8,128)S(1)}) custom-call(bf16[1536,256]{1,0:T(8,128)(2,1)S(1)} %copy-done.1, f32[384,256]{1,0:T(8,128)S(1)} %get-tuple-element.28.own, bf16[384,256]{1,0:T(8,128)(2,1)S(1)} %collective-permute-done.6.side, f32[384,256]{1,0:T(8,128)S(1)} %get-tuple-element.33.projected, ...), custom_call_target="tpu_custom_call" | custom-call | flops 150994944 | bytes 2818048 | tf_op jit(solution)/shard_map/layer/pallas_call | solution.py:248
  51.3 0.0 collective-permute-start.7
  51.3 1.5 %collective-permute-done.7 = f32[256,256]{1,0:T(8,128)S(1)} collective-permute-done((f32[256,256]{1,0:T(8,128)S(1)}, f32[256,256]{1,0:T(8,128)S(1)}, u32[]{:S(2)}, u32[]{:S(2)}) %collective-permute-start.7) | collective-permute-done | bytes 262176 | tf_op jit(solution)/shard_map/ppermute | solution.py:33
  52.8 13.9 %all_to_all.21 = bf16[32,8,256]{2,1,0:T(8,128)(2,1)S(1)} all-to-all(bf16[32,8,256]{2,1,0:T(8,128)(2,1)S(1)} %fusion), channel_id=1, replica_groups=mesh['dom'=8,'rep'=4] {'dom','rep'}, dimensions={0} | all-to-all | bytes 262144 | tf_op jit(solution)/shard_map/all_to_all | solution.py:282
  66.8 10.0 %all_to_all.22 = bf16[32,8,256]{2,1,0:T(8,128)(2,1)S(1)} all-to-all(bf16[32,8,256]{2,1,0:T(8,128)(2,1)S(1)} %bitcast.35), channel_id=1, replica_groups=mesh['dom'=8,'rep'=4] {'dom','rep'}, dimensions={0} | all-to-all | bytes 262144 | tf_op jit(solution)/shard_map/all_to_all | solution.py:285
  76.8 0.2 collective-permute-start.8
  77.0 1.1 %collective-permute-done.8 = bf16[256,256]{1,0:T(8,128)(2,1)S(1)} collective-permute-done((bf16[256,256]{1,0:T(8,128)(2,1)S(1)}, bf16[256,256]{1,0:T(8,128)(2,1)S(1)}, u32[]{:S(2)}, u32[]{:S(2)}) %collective-permute-start.8) | collective-permute-done | bytes 131104 | tf_op jit(solution)/shard_map/ppermute | solution.py:33
  78.1 0.8 %select_convert_fusion = (f32[256,256]{1,0:T(8,128)}, f32[256,256]{1,0:T(8,128)}) fusion(bf16[256,256]{1,0:T(8,128)(2,1)S(1)} %collective-permute-done.8, pred[]{:T(512)S(6)} %eq.40, bf16[32,8,256]{2,1,0:T(8,128)(2,1)S(1)} %all_to_all.22), kind=kLoop, calls=%fused_computation.2 | loop fusion | flops 262144 | bytes 786433 | tf_op jit(solution)/shard_map/convert_element_type | solution.py:289
  (3 shorter events, 0.1 us)
Async XLA Ops:
  0.6 17.7 %collective-permute-start = (bf16[1536,256]{1,0:T(8,128)(2,1)}, bf16[1536,256]{1,0:T(8,128)(2,1)S(1)}, u32[]{:S(2)}, u32[]{:S(2)}) collective-permute-start(bf16[1536,256]{1,0:T(8,128)(2,1)} %features.3), channel_id=1, source_target_pairs={{5,1},{16,2},{1,4},{20,6},{13,9},{26,10},{9,12},{30,14},{21,17},{0... | collective-permute-start | bytes 2359304 | tf_op jit(solution)/shard_map/ppermute | solution.py:28
  9.1 2.6 %copy-start = (bf16[1,1,2,88,128,128]{5,4,3,2,1,0:T(8,128)(2,1)S(1)}, bf16[1,1,2,88,128,128]{5,4,3,2,1,0:T(8,128)(2,1)}, u32[]{:S(2)}) copy-start(bf16[1,1,2,88,128,128]{5,4,3,2,1,0:T(8,128)(2,1)} %param.9) | copy-start | bytes 17301508
  11.8 2.5 %copy-start.1 = (bf16[1536,256]{1,0:T(8,128)(2,1)S(1)}, bf16[1536,256]{1,0:T(8,128)(2,1)}, u32[]{:S(2)}) copy-start(bf16[1536,256]{1,0:T(8,128)(2,1)} %features.3) | copy-start | bytes 2359300
  14.3 9.9 %collective-permute-start.1 = (bf16[1536,256]{1,0:T(8,128)(2,1)S(1)}, bf16[1536,256]{1,0:T(8,128)(2,1)S(1)}, u32[]{:S(2)}, u32[]{:S(2)}) collective-permute-start(bf16[1536,256]{1,0:T(8,128)(2,1)S(1)} %copy-done.1), channel_id=1, source_target_pairs={{11,1},{25,3},{15,5},{29,7},{19,9},{1,11},{23,13},{5,15},{27,17},{... | collective-permute-start | bytes 2359304 | tf_op jit(solution)/shard_map/ppermute | solution.py:28
  15.0 23.4 %collective-permute-start.2 = (bf16[1536,256]{1,0:T(8,128)(2,1)S(1)}, bf16[1536,256]{1,0:T(8,128)(2,1)S(1)}, u32[]{:S(2)}, u32[]{:S(2)}) collective-permute-start(bf16[1536,256]{1,0:T(8,128)(2,1)S(1)} %copy-done.1), channel_id=1, source_target_pairs={{30,0},{13,2},{9,5},{26,7},{6,8},{21,10},{17,13},{2,15},{14,16},{2... | collective-permute-start | bytes 2359304 | tf_op jit(solution)/shard_map/ppermute | solution.py:28
  18.4 20.1 %collective-permute-start.3 = (bf16[1536,256]{1,0:T(8,128)(2,1)S(1)}, bf16[1536,256]{1,0:T(8,128)(2,1)S(1)}, u32[]{:S(2)}, u32[]{:S(2)}) collective-permute-start(bf16[1536,256]{1,0:T(8,128)(2,1)S(1)} %collective-permute-done.refs_1_.refs_2_), channel_id=1, source_target_pairs={{6,3},{2,6},{14,11},{10,14},{22,19},{18,22},{30,27},{26,30}} | collective-permute-start | bytes 2359304 | tf_op jit(solution)/shard_map/ppermute | solution.py:28
  38.9 1.8 %collective-permute-start.5 = (f32[384,256]{1,0:T(8,128)S(1)}, f32[384,256]{1,0:T(8,128)S(1)}, u32[]{:S(2)}, u32[]{:S(2)}) collective-permute-start(f32[384,256]{1,0:T(8,128)S(1)} %send_other_side.1), channel_id=1, source_target_pairs={{0,1},{1,0},{2,3},{3,2},{4,5},{5,4},{6,7},{7,6},{8,9},{9,8},{10,11... | collective-permute-start | bytes 1179656 | tf_op jit(solution)/shard_map/ppermute | solution.py:33
  39.5 5.3 %collective-permute-start.4 = (f32[384,256]{1,0:T(8,128)S(1)}, f32[384,256]{1,0:T(8,128)S(1)}, u32[]{:S(2)}, u32[]{:S(2)}) collective-permute-start(f32[384,256]{1,0:T(8,128)S(1)} %send_this_side.1), channel_id=1, source_target_pairs={{0,1},{1,0},{2,3},{3,2},{4,5},{5,4},{6,7},{7,6},{8,9},{9,8},{10,11... | collective-permute-start | bytes 1179656 | tf_op jit(solution)/shard_map/ppermute | solution.py:33
  40.7 4.1 %copy-start.3 = (bf16[256,256]{1,0:T(8,128)(2,1)S(1)}, bf16[256,256]{1,0:T(8,128)(2,1)}, u32[]{:S(2)}) copy-start(bf16[256,256]{1,0:T(8,128)(2,1)} %weight_self.1) | copy-start | bytes 393220
  41.2 9.1 %collective-permute-start.6 = (bf16[384,256]{1,0:T(8,128)(2,1)S(1)}, bf16[384,256]{1,0:T(8,128)(2,1)S(1)}, u32[]{:S(2)}, u32[]{:S(2)}) collective-permute-start(bf16[384,256]{1,0:T(8,128)(2,1)S(1)} %mid_rows.1), channel_id=1, source_target_pairs={{0,2},{1,3},{2,0},{3,1},{4,6},{5,7},{6,4},{7,5},{8,10},{9,11},{10,... | collective-permute-start | bytes 589832 | tf_op jit(solution)/shard_map/ppermute | solution.py:33
  44.8 5.4 %copy-start.2 = (bf16[384,256]{1,0:T(8,128)(2,1)S(1)}, bf16[384,256]{1,0:T(8,128)(2,1)}, u32[]{:S(2)}) copy-start(bf16[384,256]{1,0:T(8,128)(2,1)} %cotangent.1) | copy-start | bytes 589828
  44.8 5.4 %copy-start.4 = (bf16[256,256]{1,0:T(8,128)(2,1)S(1)}, bf16[256,256]{1,0:T(8,128)(2,1)}, u32[]{:S(2)}) copy-start(bf16[256,256]{1,0:T(8,128)(2,1)} %weight_neigh.1) | copy-start | bytes 393220
  51.3 1.5 %collective-permute-start.7 = (f32[256,256]{1,0:T(8,128)S(1)}, f32[256,256]{1,0:T(8,128)S(1)}, u32[]{:S(2)}, u32[]{:S(2)}) collective-permute-start(f32[256,256]{1,0:T(8,128)S(1)} %get-tuple-element.36), channel_id=1, source_target_pairs={{0,1},{1,0},{2,3},{3,2},{4,5},{5,4},{6,7},{7,6},{8,9},{9,8},{10,11... | collective-permute-start | bytes 786440 | tf_op jit(solution)/shard_map/ppermute | solution.py:33
  76.8 1.3 %collective-permute-start.8 = (bf16[256,256]{1,0:T(8,128)(2,1)S(1)}, bf16[256,256]{1,0:T(8,128)(2,1)S(1)}, u32[]{:S(2)}, u32[]{:S(2)}) collective-permute-start(bf16[256,256]{1,0:T(8,128)(2,1)S(1)} %bitcast.36), channel_id=1, source_target_pairs={{0,1},{1,0},{2,3},{3,2},{4,5},{5,4},{6,7},{7,6},{8,9},{9,8},{10,11... | collective-permute-start | bytes 393224 | tf_op jit(solution)/shard_map/ppermute | solution.py:33

commit v5 on v4

--- a/solution.py
+++ b/solution.py
@@ -62,13 +62,17 @@
             return p + 1, r - 1
         return None
 
-    def later(self, p, r):
-        return (p + 2 * r, self.last + 1 - r) if r not in (0, self.half) else None
-
-    def first(self, p, r):
-        if self.passed(p, r) or r == 1 - p % 2:
-            return None
-        return p + 2 * r - 1, self.half if r in (0, self.last) else 1
+    def second(self, p, r):
+        if r == 1:
+            return p + 2 * r, self.last
+        return (p + 2 * r - 1, 1) if r == self.last and p % 2 else None
+
+    def third(self, p, r):
+        if r == self.last:
+            return p + 2 * r, self.last
+        if p % 2:
+            return (p + 2 * r - 1, 1) if r == 1 else None
+        return None if r == 1 else (p + 2 * r - 1, 0 if r else 1)
 
 
 def densify_kernel(pieces, table, weights, *refs):
@@ -181,13 +185,16 @@
 
 def pick_early():
     rep, _, _ = position()
-    return jnp.where(rep == 0, 0, jnp.where(rep == lax.axis_size("rep") // 2, 1, 2))
+    half = lax.axis_size("rep") // 2
+    return jnp.where(rep == 0, 0, jnp.where(rep == half, 1, jnp.where(rep == 1, 2, 3)))
 
 
 def pick_late():
     rep, _, _ = position()
     odd = lax.axis_index("dom").astype(jnp.int32) % 2
-    return jnp.where(rep == 1 - odd, 2, jnp.where(rep == lax.axis_size("rep") // 2 + 1 - odd, 1, 0))
+    half = lax.axis_size("rep") // 2
+    others = jnp.where(jnp.logical_and(rep == half + 1, odd == 1), 2, 3)
+    return jnp.where(rep == 1 - odd, 0, jnp.where(rep == half + 1 - odd, 1, others))
 
 
 def early_kernel(dense, *refs):
@@ -323,8 +330,9 @@
     dense_send = densify(limit, table, weights, send_pieces, (row_parts,) * half, "densify_send")
     if special:
         waited, dense_send = lax.optimization_barrier((features, dense_send))
-        early_found = (features, ahead, move(waited, routes.later))
-        late_found = (move(waited, routes.first), move(ahead, routes.passed), ahead)
+        second, third = move(waited, routes.second), move(waited, routes.third)
+        early_found = (features, ahead, second, third)
+        late_found = (ahead, move(ahead, routes.passed), second, third)
     else:
         late, *early_found = fetch_blocks(features, blocks, groups, steps)
         late_found = (late,)

time: 79 us -> 77.8 us (0.985)
  starting transfers between devices: 14.1 us -> 11.2 us
  waiting for transfers between devices: 22.9 us -> 24.1 us
  blocking collectives: 23.9 us -> 23 us
  Pallas kernels: 12.2 us -> 13 us
    ppermute x5, starting transfers between devices: 4.46 us -> 1.58 us  [rep_exchange(): return lax.ppermute(value, 'rep', route)]
    all_to_all x1, blocking collectives: 13.9 us -> 13 us  [all_reduce_grads(): terms = lax.all_to_all(chip, AXES, 0, 0, tiled=True)]
    ppermute x5, waiting for transfers between devices: 8.04 us -> 8.87 us  [rep_exchange(): return lax.ppermute(value, 'rep', route)]
    pallas_call x2, Pallas kernels: 7.65 us -> 8.45 us  [densify(): pl.pallas_call(functools.partial(densify_kernel, pieces), out_shape=out_s...]
  transfers between devices with their start and end apart: 9 -> 9, of which waited for: 6 -> 6; matrix products, arithmetic and copies ran while one was open for 2% -> 2% of each run, Pallas kernels for 14% -> 15%
where the time goes in v5:
time: 77.8 us; the launch traced here: 77.2 us
  waiting for transfers between devices  24.1 us (31%)
  blocking collectives  23 us (30%)
  Pallas kernels  13 us (17%)
  starting transfers between devices  11.2 us (14%)
  local copies, waits for them, and re-layouts  3.4 us (4%)
  other arithmetic  1.68 us (2%)
  between operations  0.82 us (1%)
    ppermute x4, waiting for transfers between devices, flat_permute(): return lax.ppermute(value, AXES, route)  15.2 us
    all_to_all x1, blocking collectives, all_reduce_grads(): terms = lax.all_to_all(chip, AXES, 0, 0, tiled=True)  13 us
    all_to_all x1, blocking collectives, all_reduce_grads(): mine = lax.all_to_all(spread, AXES, 0, 0, tiled=True)  10 us
    ppermute x4, starting transfers between devices, flat_permute(): return lax.ppermute(value, AXES, route)  9.62 us
    ppermute x5, waiting for transfers between devices, rep_exchange(): return lax.ppermute(value, 'rep', route)  8.87 us
    pallas_call x2, Pallas kernels, densify(): pl.pallas_call(functools.partial(densify_kernel, pieces), out_shape=out_s...  8.45 us
    pallas_call x6, Pallas kernels, vmem_call(): pl.pallas_call(kernel, out_shape=out_shape, in_specs=[vmem] * len(operand...  4.59 us
    unnamed x10, local copies, waits for them, and re-layouts  2.65 us
  transfers between devices with their start and end apart: 9, of which 6 were waited for; matrix products, arithmetic and copies ran while one was open for 2% of the time, Pallas kernels for 15%

profile of v5, /device:TPU:0, one launch (start us, length us, event | category | flops | bytes accessed | tf_op | source)
XLA Modules:
  0.0 77.2 jit_solution(11737669295548383948)
XLA Ops:
  0.6 6.9 %collective-permute-start = (bf16[1536,256]{1,0:T(8,128)(2,1)}, bf16[1536,256]{1,0:T(8,128)(2,1)S(1)}, u32[]{:S(2)}, u32[]{:S(2)}) collective-permute-start(bf16[1536,256]{1,0:T(8,128)(2,1)} %features.3), channel_id=1, source_target_pairs={{5,1},{16,2},{1,4},{20,6},{13,9},{26,10},{9,12},{30,14},{21,17},{0... | collective-permute-start | bytes 2359304 | tf_op jit(solution)/shard_map/ppermute | solution.py:28
  7.6 0.7 copy.11
  8.3 0.7 fusion.7
  9.1 0.1 pad_add_fusion.table
  9.1 0.0 copy-start
  9.1 2.6 %copy-done = bf16[1,1,2,88,128,128]{5,4,3,2,1,0:T(8,128)(2,1)S(1)} copy-done((bf16[1,1,2,88,128,128]{5,4,3,2,1,0:T(8,128)(2,1)S(1)}, bf16[1,1,2,88,128,128]{5,4,3,2,1,0:T(8,128)(2,1)}, u32[]{:S(2)}) %copy-start) | copy-done | bytes 5767192
  11.8 0.0 copy-start.1
  11.8 2.7 %densify_send.1 = (bf16[384,1536]{1,0:T(8,128)(2,1)S(1)}, bf16[384,1536]{1,0:T(8,128)(2,1)S(1)}) custom-call(s32[2,89]{1,0:T(2,128)S(1)} %pad_add_fusion.table, bf16[2,88,128,128]{3,2,1,0:T(8,128)(2,1)S(1)} %bitcast.32), custom_call_target="tpu_custom_call" | custom-call | bytes 7077888 | tf_op jit(solution)/shard_map/densify_send/pallas_call | solution.py:158
  14.5 0.0 copy-done.1
  14.5 0.7 collective-permute-start.1
  15.3 1.3 %collective-permute-start.2 = (bf16[1536,256]{1,0:T(8,128)(2,1)S(1)}, bf16[1536,256]{1,0:T(8,128)(2,1)S(1)}, u32[]{:S(2)}, u32[]{:S(2)}) collective-permute-start(bf16[1536,256]{1,0:T(8,128)(2,1)S(1)} %copy-done.1), channel_id=1, source_target_pairs={{29,0},{12,2},{27,3},{9,5},{31,7},{5,8},{20,10},{3,11},{17,13},{7,... | collective-permute-start | bytes 2359304 | tf_op jit(solution)/shard_map/ppermute | solution.py:28
  16.6 1.3 %collective-permute-done.refs_1_.refs_0_ = bf16[1536,256]{1,0:T(8,128)(2,1)S(1)} collective-permute-done((bf16[1536,256]{1,0:T(8,128)(2,1)}, bf16[1536,256]{1,0:T(8,128)(2,1)S(1)}, u32[]{:S(2)}, u32[]{:S(2)}) %collective-permute-start) | collective-permute-done | bytes 786464 | tf_op jit(solution)/shard_map/ppermute | solution.py:28
  17.8 0.7 collective-permute-start.3
  18.5 5.7 %densify_rest.1 = (bf16[1,1536,1536]{2,1,0:T(8,128)(2,1)S(1)}, bf16[384,1536]{1,0:T(8,128)(2,1)S(1)}, bf16[384,1536]{1,0:T(8,128)(2,1)S(1)}) custom-call(s32[2,89]{1,0:T(2,128)S(1)} %pad_add_fusion.table, bf16[2,88,128,128]{3,2,1,0:T(8,128)(2,1)S(1)} %bitcast.33), custom_call_target="tpu_custom_call" | custom-call | bytes 21233664 | tf_op jit(solution)/shard_map/densify_rest/pallas_call | solution.py:158
  24.2 0.0 collective-permute-done.1.refs_2_
  24.2 13.9 %collective-permute-done.2.refs_3_ = bf16[1536,256]{1,0:T(8,128)(2,1)S(1)} collective-permute-done((bf16[1536,256]{1,0:T(8,128)(2,1)S(1)}, bf16[1536,256]{1,0:T(8,128)(2,1)S(1)}, u32[]{:S(2)}, u32[]{:S(2)}) %collective-permute-start.2) | collective-permute-done | bytes 786464 | tf_op jit(solution)/shard_map/ppermute | solution.py:28
  38.2 1.4 %early_rows.1 = (f32[384,256]{1,0:T(8,128)S(1)}, f32[384,256]{1,0:T(8,128)S(1)}, f32[384,256]{1,0:T(8,128)S(1)}, f32[384,256]{1,0:T(8,128)S(1)}) custom-call(bf16[1,1536,1536]{2,1,0:T(8,128)(2,1)S(1)} %get-tuple-element.20.dense, bf16[1536,256]{1,0:T(8,128)(2,1)S(1)} %copy-done.1, bf16[1536,256]{1,0:T(8,128)(2,1)S(1)} %collective-permute-done.refs_1_.refs_0_, ...), custom_call_target="tpu_custom_call" | custom-call | flops 1207959552 | bytes 9437184 | tf_op jit(solution)/shard_map/early_rows/pallas_call | solution.py:255
  39.6 0.0 collective-permute-done.3.refs_1_
  39.6 0.5 send_other_side.1
  40.1 0.1 collective-permute-start.5
  40.2 0.5 send_this_side.1
  40.7 0.5 collective-permute-start.4
  41.2 0.7 collective-permute-done.5.received
  41.9 0.0 copy-start.3
  41.9 0.5 mid_rows.1
  42.4 0.7 collective-permute-start.6
  43.1 0.0 collective-permute-done.4.received
  43.1 0.0 copy-done.3
  43.1 0.0 copy-start.2
  43.1 0.0 copy-start.4
  43.1 0.7 own_rows.1
  43.8 5.5 %collective-permute-done.6.side = bf16[384,256]{1,0:T(8,128)(2,1)S(1)} collective-permute-done((bf16[384,256]{1,0:T(8,128)(2,1)S(1)}, bf16[384,256]{1,0:T(8,128)(2,1)S(1)}, u32[]{:S(2)}, u32[]{:S(2)}) %collective-permute-start.6) | collective-permute-done | bytes 196640 | tf_op jit(solution)/shard_map/ppermute | solution.py:33
  49.4 0.0 copy-done.2
  49.4 0.0 copy-done.4
  49.4 1.0 %layer.1 = (bf16[384,256]{1,0:T(8,128)(2,1)}, f32[256,256]{1,0:T(8,128)S(1)}, f32[256,256]{1,0:T(8,128)S(1)}) custom-call(bf16[1536,256]{1,0:T(8,128)(2,1)S(1)} %copy-done.1, f32[384,256]{1,0:T(8,128)S(1)} %get-tuple-element.28.own, bf16[384,256]{1,0:T(8,128)(2,1)S(1)} %collective-permute-done.6.side, f32[384,256]{1,0:T(8,128)S(1)} %get-tuple-element.33.projected, ...), custom_call_target="tpu_custom_call" | custom-call | flops 150994944 | bytes 2818048 | tf_op jit(solution)/shard_map/layer/pallas_call | solution.py:255
  50.4 0.0 collective-permute-start.7
  50.4 1.5 %collective-permute-done.7 = f32[256,256]{1,0:T(8,128)S(1)} collective-permute-done((f32[256,256]{1,0:T(8,128)S(1)}, f32[256,256]{1,0:T(8,128)S(1)}, u32[]{:S(2)}, u32[]{:S(2)}) %collective-permute-start.7) | collective-permute-done | bytes 262176 | tf_op jit(solution)/shard_map/ppermute | solution.py:33
  52.0 13.0 %all_to_all.21 = bf16[32,8,256]{2,1,0:T(8,128)(2,1)S(1)} all-to-all(bf16[32,8,256]{2,1,0:T(8,128)(2,1)S(1)} %fusion), channel_id=1, replica_groups=mesh['dom'=8,'rep'=4] {'dom','rep'}, dimensions={0} | all-to-all | bytes 262144 | tf_op jit(solution)/shard_map/all_to_all | solution.py:289
  65.0 10.0 %all_to_all.22 = bf16[32,8,256]{2,1,0:T(8,128)(2,1)S(1)} all-to-all(bf16[32,8,256]{2,1,0:T(8,128)(2,1)S(1)} %bitcast.35), channel_id=1, replica_groups=mesh['dom'=8,'rep'=4] {'dom','rep'}, dimensions={0} | all-to-all | bytes 262144 | tf_op jit(solution)/shard_map/all_to_all | solution.py:292
  75.1 0.2 collective-permute-start.8
  75.3 1.1 %collective-permute-done.8 = bf16[256,256]{1,0:T(8,128)(2,1)S(1)} collective-permute-done((bf16[256,256]{1,0:T(8,128)(2,1)S(1)}, bf16[256,256]{1,0:T(8,128)(2,1)S(1)}, u32[]{:S(2)}, u32[]{:S(2)}) %collective-permute-start.8) | collective-permute-done | bytes 131104 | tf_op jit(solution)/shard_map/ppermute | solution.py:33
  76.4 0.8 %select_convert_fusion = (f32[256,256]{1,0:T(8,128)}, f32[256,256]{1,0:T(8,128)}) fusion(bf16[256,256]{1,0:T(8,128)(2,1)S(1)} %collective-permute-done.8, pred[]{:T(512)S(6)} %eq.40, bf16[32,8,256]{2,1,0:T(8,128)(2,1)S(1)} %all_to_all.22), kind=kLoop, calls=%fused_computation.2 | loop fusion | flops 262144 | bytes 786433 | tf_op jit(solution)/shard_map/convert_element_type | solution.py:296
  (3 shorter events, 0.1 us)
Async XLA Ops:
  0.6 17.2 %collective-permute-start = (bf16[1536,256]{1,0:T(8,128)(2,1)}, bf16[1536,256]{1,0:T(8,128)(2,1)S(1)}, u32[]{:S(2)}, u32[]{:S(2)}) collective-permute-start(bf16[1536,256]{1,0:T(8,128)(2,1)} %features.3), channel_id=1, source_target_pairs={{5,1},{16,2},{1,4},{20,6},{13,9},{26,10},{9,12},{30,14},{21,17},{0... | collective-permute-start | bytes 2359304 | tf_op jit(solution)/shard_map/ppermute | solution.py:28
  9.1 2.6 %copy-start = (bf16[1,1,2,88,128,128]{5,4,3,2,1,0:T(8,128)(2,1)S(1)}, bf16[1,1,2,88,128,128]{5,4,3,2,1,0:T(8,128)(2,1)}, u32[]{:S(2)}) copy-start(bf16[1,1,2,88,128,128]{5,4,3,2,1,0:T(8,128)(2,1)} %param.9) | copy-start | bytes 17301508
  11.8 2.8 %copy-start.1 = (bf16[1536,256]{1,0:T(8,128)(2,1)S(1)}, bf16[1536,256]{1,0:T(8,128)(2,1)}, u32[]{:S(2)}) copy-start(bf16[1536,256]{1,0:T(8,128)(2,1)} %features.3) | copy-start | bytes 2359300
  14.5 9.7 %collective-permute-start.1 = (bf16[1536,256]{1,0:T(8,128)(2,1)S(1)}, bf16[1536,256]{1,0:T(8,128)(2,1)S(1)}, u32[]{:S(2)}, u32[]{:S(2)}) collective-permute-start(bf16[1536,256]{1,0:T(8,128)(2,1)S(1)} %copy-done.1), channel_id=1, source_target_pairs={{11,1},{15,5},{25,7},{19,9},{23,13},{1,15},{27,17},{31,21},{9,23},... | collective-permute-start | bytes 2359304 | tf_op jit(solution)/shard_map/ppermute | solution.py:28
  15.3 22.9 %collective-permute-start.2 = (bf16[1536,256]{1,0:T(8,128)(2,1)S(1)}, bf16[1536,256]{1,0:T(8,128)(2,1)S(1)}, u32[]{:S(2)}, u32[]{:S(2)}) collective-permute-start(bf16[1536,256]{1,0:T(8,128)(2,1)S(1)} %copy-done.1), channel_id=1, source_target_pairs={{29,0},{12,2},{27,3},{9,5},{31,7},{5,8},{20,10},{3,11},{17,13},{7,... | collective-permute-start | bytes 2359304 | tf_op jit(solution)/shard_map/ppermute | solution.py:28
  17.8 21.8 %collective-permute-start.3 = (bf16[1536,256]{1,0:T(8,128)(2,1)S(1)}, bf16[1536,256]{1,0:T(8,128)(2,1)S(1)}, u32[]{:S(2)}, u32[]{:S(2)}) collective-permute-start(bf16[1536,256]{1,0:T(8,128)(2,1)S(1)} %collective-permute-done.refs_1_.refs_0_), channel_id=1, source_target_pairs={{6,3},{2,6},{14,11},{10,14},{22,19},{18,22},{30,27},{26,30}} | collective-permute-start | bytes 2359304 | tf_op jit(solution)/shard_map/ppermute | solution.py:28
  40.1 1.8 %collective-permute-start.5 = (f32[384,256]{1,0:T(8,128)S(1)}, f32[384,256]{1,0:T(8,128)S(1)}, u32[]{:S(2)}, u32[]{:S(2)}) collective-permute-start(f32[384,256]{1,0:T(8,128)S(1)} %send_other_side.1), channel_id=1, source_target_pairs={{0,1},{1,0},{2,3},{3,2},{4,5},{5,4},{6,7},{7,6},{8,9},{9,8},{10,11... | collective-permute-start | bytes 1179656 | tf_op jit(solution)/shard_map/ppermute | solution.py:33
  40.7 2.4 %collective-permute-start.4 = (f32[384,256]{1,0:T(8,128)S(1)}, f32[384,256]{1,0:T(8,128)S(1)}, u32[]{:S(2)}, u32[]{:S(2)}) collective-permute-start(f32[384,256]{1,0:T(8,128)S(1)} %send_this_side.1), channel_id=1, source_target_pairs={{0,1},{1,0},{2,3},{3,2},{4,5},{5,4},{6,7},{7,6},{8,9},{9,8},{10,11... | collective-permute-start | bytes 1179656 | tf_op jit(solution)/shard_map/ppermute | solution.py:33
  41.9 1.2 %copy-start.3 = (bf16[256,256]{1,0:T(8,128)(2,1)S(1)}, bf16[256,256]{1,0:T(8,128)(2,1)}, u32[]{:S(2)}) copy-start(bf16[256,256]{1,0:T(8,128)(2,1)} %weight_self.1) | copy-start | bytes 393220
  42.4 7.0 %collective-permute-start.6 = (bf16[384,256]{1,0:T(8,128)(2,1)S(1)}, bf16[384,256]{1,0:T(8,128)(2,1)S(1)}, u32[]{:S(2)}, u32[]{:S(2)}) collective-permute-start(bf16[384,256]{1,0:T(8,128)(2,1)S(1)} %mid_rows.1), channel_id=1, source_target_pairs={{0,2},{1,3},{2,0},{3,1},{4,6},{5,7},{6,4},{7,5},{8,10},{9,11},{10,... | collective-permute-start | bytes 589832 | tf_op jit(solution)/shard_map/ppermute | solution.py:33
  43.1 6.3 %copy-start.2 = (bf16[384,256]{1,0:T(8,128)(2,1)S(1)}, bf16[384,256]{1,0:T(8,128)(2,1)}, u32[]{:S(2)}) copy-start(bf16[384,256]{1,0:T(8,128)(2,1)} %cotangent.1) | copy-start | bytes 589828
  43.1 6.3 %copy-start.4 = (bf16[256,256]{1,0:T(8,128)(2,1)S(1)}, bf16[256,256]{1,0:T(8,128)(2,1)}, u32[]{:S(2)}) copy-start(bf16[256,256]{1,0:T(8,128)(2,1)} %weight_neigh.1) | copy-start | bytes 393220
  50.4 1.5 %collective-permute-start.7 = (f32[256,256]{1,0:T(8,128)S(1)}, f32[256,256]{1,0:T(8,128)S(1)}, u32[]{:S(2)}, u32[]{:S(2)}) collective-permute-start(f32[256,256]{1,0:T(8,128)S(1)} %get-tuple-element.36), channel_id=1, source_target_pairs={{0,1},{1,0},{2,3},{3,2},{4,5},{5,4},{6,7},{7,6},{8,9},{9,8},{10,11... | collective-permute-start | bytes 786440 | tf_op jit(solution)/shard_map/ppermute | solution.py:33
  75.1 1.3 %collective-permute-start.8 = (bf16[256,256]{1,0:T(8,128)(2,1)S(1)}, bf16[256,256]{1,0:T(8,128)(2,1)S(1)}, u32[]{:S(2)}, u32[]{:S(2)}) collective-permute-start(bf16[256,256]{1,0:T(8,128)(2,1)S(1)} %bitcast.36), channel_id=1, source_target_pairs={{0,1},{1,0},{2,3},{3,2},{4,5},{5,4},{6,7},{7,6},{8,9},{9,8},{10,11... | collective-permute-start | bytes 393224 | tf_op jit(solution)/shard_map/ppermute | solution.py:33

commit v6 on v5

--- a/solution.py
+++ b/solution.py
@@ -52,7 +52,7 @@
     def ahead(self, p, r):
         if r == self.half:
             q = (p + 2 * r) % self.blocks
-            return q, self.half if q // 2 % 2 else 0
+            return q, 0 if q // 2 % 2 else self.half
         return (p + 2 * r - 1, 1) if r == 1 - p % 2 else None
 
     def passed(self, p, r):
@@ -65,14 +65,14 @@
     def second(self, p, r):
         if r == 1:
             return p + 2 * r, self.last
-        return (p + 2 * r - 1, 1) if r == self.last and p % 2 else None
+        return (p + 2 * r - 1, 0) if r == self.last and p % 2 else None
 
     def third(self, p, r):
         if r == self.last:
             return p + 2 * r, self.last
         if p % 2:
             return (p + 2 * r - 1, 1) if r == 1 else None
-        return None if r == 1 else (p + 2 * r - 1, 0 if r else 1)
+        return None if r == 1 else (p + 2 * r - 1, 1 if r else 0)
 
 
 def densify_kernel(pieces, table, weights, *refs):

time: 77.8 us -> 76.2 us (0.979)
  waiting for transfers between devices: 24.1 us -> 21.8 us
  blocking collectives: 23 us -> 21.4 us
  starting transfers between devices: 11.2 us -> 12.5 us
  Pallas kernels: 13 us -> 13.9 us
    ppermute x5, starting transfers between devices: 1.58 us -> 3.45 us  [rep_exchange(): return lax.ppermute(value, 'rep', route)]
    all_to_all x1, blocking collectives: 13 us -> 11.4 us  [all_reduce_grads(): terms = lax.all_to_all(chip, AXES, 0, 0, tiled=True)]
    ppermute x4, waiting for transfers between devices: 15.2 us -> 14 us  [flat_permute(): return lax.ppermute(value, AXES, route)]
    ppermute x5, waiting for transfers between devices: 8.87 us -> 7.8 us  [rep_exchange(): return lax.ppermute(value, 'rep', route)]
    pallas_call x2, Pallas kernels: 8.45 us -> 9.28 us  [densify(): pl.pallas_call(functools.partial(densify_kernel, pieces), out_shape=out_s...]
  transfers between devices with their start and end apart: 9 -> 9, of which waited for: 6 -> 6; matrix products, arithmetic and copies ran while one was open for 2% -> 2% of each run, Pallas kernels for 15% -> 16%
where the time goes in v6:
time: 76.2 us; the launch traced here: 75.4 us
  waiting for transfers between devices  21.8 us (29%)
  blocking collectives  21.4 us (28%)
  Pallas kernels  13.9 us (18%)
  starting transfers between devices  12.5 us (16%)
  local copies, waits for them, and re-layouts  3.4 us (4%)
  other arithmetic  1.68 us (2%)
  between operations  0.82 us (1%)
    ppermute x4, waiting for transfers between devices, flat_permute(): return lax.ppermute(value, AXES, route)  14 us
    all_to_all x1, blocking collectives, all_reduce_grads(): terms = lax.all_to_all(chip, AXES, 0, 0, tiled=True)  11.4 us
    all_to_all x1, blocking collectives, all_reduce_grads(): mine = lax.all_to_all(spread, AXES, 0, 0, tiled=True)  10 us
    pallas_call x2, Pallas kernels, densify(): pl.pallas_call(functools.partial(densify_kernel, pieces), out_shape=out_s...  9.28 us
    ppermute x4, starting transfers between devices, flat_permute(): return lax.ppermute(value, AXES, route)  9.01 us
    ppermute x5, waiting for transfers between devices, rep_exchange(): return lax.ppermute(value, 'rep', route)  7.8 us
    pallas_call x6, Pallas kernels, vmem_call(): pl.pallas_call(kernel, out_shape=out_shape, in_specs=[vmem] * len(operand...  4.6 us
    ppermute x5, starting transfers between devices, rep_exchange(): return lax.ppermute(value, 'rep', route)  3.45 us
  transfers between devices with their start and end apart: 9, of which 6 were waited for; matrix products, arithmetic and copies ran while one was open for 2% of the time, Pallas kernels for 16%

profile of v6, /device:TPU:0, one launch (start us, length us, event | category | flops | bytes accessed | tf_op | source)
XLA Modules:
  0.0 75.4 jit_solution(2261800590827938506)
XLA Ops:
  0.6 0.7 collective-permute-start
  1.4 0.7 copy.11
  2.1 0.7 fusion.7
  2.9 0.1 pad_add_fusion.table
  2.9 0.0 copy-start
  2.9 2.6 %copy-done = bf16[1,1,2,88,128,128]{5,4,3,2,1,0:T(8,128)(2,1)S(1)} copy-done((bf16[1,1,2,88,128,128]{5,4,3,2,1,0:T(8,128)(2,1)S(1)}, bf16[1,1,2,88,128,128]{5,4,3,2,1,0:T(8,128)(2,1)}, u32[]{:S(2)}) %copy-start) | copy-done | bytes 5767192
  5.6 0.0 copy-start.1
  5.6 3.1 %densify_send.1 = (bf16[384,1536]{1,0:T(8,128)(2,1)S(1)}, bf16[384,1536]{1,0:T(8,128)(2,1)S(1)}) custom-call(s32[2,89]{1,0:T(2,128)S(1)} %pad_add_fusion.table, bf16[2,88,128,128]{3,2,1,0:T(8,128)(2,1)S(1)} %bitcast.32), custom_call_target="tpu_custom_call" | custom-call | bytes 7077888 | tf_op jit(solution)/shard_map/densify_send/pallas_call | solution.py:158
  8.7 0.0 copy-done.1
  8.7 6.3 %collective-permute-start.1 = (bf16[1536,256]{1,0:T(8,128)(2,1)S(1)}, bf16[1536,256]{1,0:T(8,128)(2,1)S(1)}, u32[]{:S(2)}, u32[]{:S(2)}) collective-permute-start(bf16[1536,256]{1,0:T(8,128)(2,1)S(1)} %copy-done.1), channel_id=1, source_target_pairs={{11,1},{15,5},{24,7},{19,9},{23,13},{0,15},{27,17},{31,21},{8,23},... | collective-permute-start | bytes 2359304 | tf_op jit(solution)/shard_map/ppermute | solution.py:28
  15.0 1.3 %collective-permute-start.2 = (bf16[1536,256]{1,0:T(8,128)(2,1)S(1)}, bf16[1536,256]{1,0:T(8,128)(2,1)S(1)}, u32[]{:S(2)}, u32[]{:S(2)}) collective-permute-start(bf16[1536,256]{1,0:T(8,128)(2,1)S(1)} %copy-done.1), channel_id=1, source_target_pairs={{28,0},{13,2},{27,3},{9,5},{31,7},{4,8},{21,10},{3,11},{17,13},{7,... | collective-permute-start | bytes 2359304 | tf_op jit(solution)/shard_map/ppermute | solution.py:28
  16.3 0.0 collective-permute-done.refs_1_.refs_0_
  16.3 0.7 collective-permute-start.3
  17.0 6.2 %densify_rest.1 = (bf16[1,1536,1536]{2,1,0:T(8,128)(2,1)S(1)}, bf16[384,1536]{1,0:T(8,128)(2,1)S(1)}, bf16[384,1536]{1,0:T(8,128)(2,1)S(1)}) custom-call(s32[2,89]{1,0:T(2,128)S(1)} %pad_add_fusion.table, bf16[2,88,128,128]{3,2,1,0:T(8,128)(2,1)S(1)} %bitcast.33), custom_call_target="tpu_custom_call" | custom-call | bytes 21233664 | tf_op jit(solution)/shard_map/densify_rest/pallas_call | solution.py:158
  23.2 8.5 %collective-permute-done.1.refs_2_ = bf16[1536,256]{1,0:T(8,128)(2,1)S(1)} collective-permute-done((bf16[1536,256]{1,0:T(8,128)(2,1)S(1)}, bf16[1536,256]{1,0:T(8,128)(2,1)S(1)}, u32[]{:S(2)}, u32[]{:S(2)}) %collective-permute-start.1) | collective-permute-done | bytes 786464 | tf_op jit(solution)/shard_map/ppermute | solution.py:28
  31.7 5.5 %collective-permute-done.2.refs_3_ = bf16[1536,256]{1,0:T(8,128)(2,1)S(1)} collective-permute-done((bf16[1536,256]{1,0:T(8,128)(2,1)S(1)}, bf16[1536,256]{1,0:T(8,128)(2,1)S(1)}, u32[]{:S(2)}, u32[]{:S(2)}) %collective-permute-start.2) | collective-permute-done | bytes 786464 | tf_op jit(solution)/shard_map/ppermute | solution.py:28
  37.2 1.4 %early_rows.1 = (f32[384,256]{1,0:T(8,128)S(1)}, f32[384,256]{1,0:T(8,128)S(1)}, f32[384,256]{1,0:T(8,128)S(1)}, f32[384,256]{1,0:T(8,128)S(1)}) custom-call(bf16[1,1536,1536]{2,1,0:T(8,128)(2,1)S(1)} %get-tuple-element.20.dense, bf16[1536,256]{1,0:T(8,128)(2,1)S(1)} %copy-done.1, bf16[1536,256]{1,0:T(8,128)(2,1)S(1)} %collective-permute-done.refs_1_.refs_0_, ...), custom_call_target="tpu_custom_call" | custom-call | flops 1207959552 | bytes 9437184 | tf_op jit(solution)/shard_map/early_rows/pallas_call | solution.py:255
  38.6 0.0 collective-permute-done.3.refs_1_
  38.6 0.5 send_other_side.1
  39.1 0.1 collective-permute-start.5
  39.2 0.5 send_this_side.1
  39.7 0.5 collective-permute-start.4
  40.2 0.7 collective-permute-done.5.received
  40.9 0.0 copy-start.3
  40.9 0.5 mid_rows.1
  41.4 2.6 %collective-permute-start.6 = (bf16[384,256]{1,0:T(8,128)(2,1)S(1)}, bf16[384,256]{1,0:T(8,128)(2,1)S(1)}, u32[]{:S(2)}, u32[]{:S(2)}) collective-permute-start(bf16[384,256]{1,0:T(8,128)(2,1)S(1)} %mid_rows.1), channel_id=1, source_target_pairs={{0,2},{1,3},{2,0},{3,1},{4,6},{5,7},{6,4},{7,5},{8,10},{9,11},{10,... | collective-permute-start | bytes 589832 | tf_op jit(solution)/shard_map/ppermute | solution.py:33
  44.0 0.0 collective-permute-done.4.received
  44.0 0.0 copy-done.3
  44.0 0.0 copy-start.2
  44.0 0.0 copy-start.4
  44.0 0.7 own_rows.1
  44.7 4.5 %collective-permute-done.6.side = bf16[384,256]{1,0:T(8,128)(2,1)S(1)} collective-permute-done((bf16[384,256]{1,0:T(8,128)(2,1)S(1)}, bf16[384,256]{1,0:T(8,128)(2,1)S(1)}, u32[]{:S(2)}, u32[]{:S(2)}) %collective-permute-start.6) | collective-permute-done | bytes 196640 | tf_op jit(solution)/shard_map/ppermute | solution.py:33
  49.2 0.0 copy-done.2
  49.2 0.0 copy-done.4
  49.2 1.0 %layer.1 = (bf16[384,256]{1,0:T(8,128)(2,1)}, f32[256,256]{1,0:T(8,128)S(1)}, f32[256,256]{1,0:T(8,128)S(1)}) custom-call(bf16[1536,256]{1,0:T(8,128)(2,1)S(1)} %copy-done.1, f32[384,256]{1,0:T(8,128)S(1)} %get-tuple-element.28.own, bf16[384,256]{1,0:T(8,128)(2,1)S(1)} %collective-permute-done.6.side, f32[384,256]{1,0:T(8,128)S(1)} %get-tuple-element.33.projected, ...), custom_call_target="tpu_custom_call" | custom-call | flops 150994944 | bytes 2818048 | tf_op jit(solution)/shard_map/layer/pallas_call | solution.py:255
  50.2 0.0 collective-permute-start.7
  50.2 1.5 %collective-permute-done.7 = f32[256,256]{1,0:T(8,128)S(1)} collective-permute-done((f32[256,256]{1,0:T(8,128)S(1)}, f32[256,256]{1,0:T(8,128)S(1)}, u32[]{:S(2)}, u32[]{:S(2)}) %collective-permute-start.7) | collective-permute-done | bytes 262176 | tf_op jit(solution)/shard_map/ppermute | solution.py:33
  51.8 11.4 %all_to_all.21 = bf16[32,8,256]{2,1,0:T(8,128)(2,1)S(1)} all-to-all(bf16[32,8,256]{2,1,0:T(8,128)(2,1)S(1)} %fusion), channel_id=1, replica_groups=mesh['dom'=8,'rep'=4] {'dom','rep'}, dimensions={0} | all-to-all | bytes 262144 | tf_op jit(solution)/shard_map/all_to_all | solution.py:289
  63.2 10.0 %all_to_all.22 = bf16[32,8,256]{2,1,0:T(8,128)(2,1)S(1)} all-to-all(bf16[32,8,256]{2,1,0:T(8,128)(2,1)S(1)} %bitcast.35), channel_id=1, replica_groups=mesh['dom'=8,'rep'=4] {'dom','rep'}, dimensions={0} | all-to-all | bytes 262144 | tf_op jit(solution)/shard_map/all_to_all | solution.py:292
  73.2 0.2 collective-permute-start.8
  73.4 1.1 %collective-permute-done.8 = bf16[256,256]{1,0:T(8,128)(2,1)S(1)} collective-permute-done((bf16[256,256]{1,0:T(8,128)(2,1)S(1)}, bf16[256,256]{1,0:T(8,128)(2,1)S(1)}, u32[]{:S(2)}, u32[]{:S(2)}) %collective-permute-start.8) | collective-permute-done | bytes 131104 | tf_op jit(solution)/shard_map/ppermute | solution.py:33
  74.6 0.8 %select_convert_fusion = (f32[256,256]{1,0:T(8,128)}, f32[256,256]{1,0:T(8,128)}) fusion(bf16[256,256]{1,0:T(8,128)(2,1)S(1)} %collective-permute-done.8, pred[]{:T(512)S(6)} %eq.40, bf16[32,8,256]{2,1,0:T(8,128)(2,1)S(1)} %all_to_all.22), kind=kLoop, calls=%fused_computation.2 | loop fusion | flops 262144 | bytes 786433 | tf_op jit(solution)/shard_map/convert_element_type | solution.py:296
  (3 shorter events, 0.1 us)
Async XLA Ops:
  0.6 15.7 %collective-permute-start = (bf16[1536,256]{1,0:T(8,128)(2,1)}, bf16[1536,256]{1,0:T(8,128)(2,1)S(1)}, u32[]{:S(2)}, u32[]{:S(2)}) collective-permute-start(bf16[1536,256]{1,0:T(8,128)(2,1)} %features.3), channel_id=1, source_target_pairs={{5,1},{18,2},{1,4},{22,6},{13,9},{24,10},{9,12},{28,14},{21,17},{2... | collective-permute-start | bytes 2359304 | tf_op jit(solution)/shard_map/ppermute | solution.py:28
  2.9 2.6 %copy-start = (bf16[1,1,2,88,128,128]{5,4,3,2,1,0:T(8,128)(2,1)S(1)}, bf16[1,1,2,88,128,128]{5,4,3,2,1,0:T(8,128)(2,1)}, u32[]{:S(2)}) copy-start(bf16[1,1,2,88,128,128]{5,4,3,2,1,0:T(8,128)(2,1)} %param.9) | copy-start | bytes 17301508
  5.6 3.1 %copy-start.1 = (bf16[1536,256]{1,0:T(8,128)(2,1)S(1)}, bf16[1536,256]{1,0:T(8,128)(2,1)}, u32[]{:S(2)}) copy-start(bf16[1536,256]{1,0:T(8,128)(2,1)} %features.3) | copy-start | bytes 2359300
  8.7 23.0 %collective-permute-start.1 = (bf16[1536,256]{1,0:T(8,128)(2,1)S(1)}, bf16[1536,256]{1,0:T(8,128)(2,1)S(1)}, u32[]{:S(2)}, u32[]{:S(2)}) collective-permute-start(bf16[1536,256]{1,0:T(8,128)(2,1)S(1)} %copy-done.1), channel_id=1, source_target_pairs={{11,1},{15,5},{24,7},{19,9},{23,13},{0,15},{27,17},{31,21},{8,23},... | collective-permute-start | bytes 2359304 | tf_op jit(solution)/shard_map/ppermute | solution.py:28
  15.0 22.2 %collective-permute-start.2 = (bf16[1536,256]{1,0:T(8,128)(2,1)S(1)}, bf16[1536,256]{1,0:T(8,128)(2,1)S(1)}, u32[]{:S(2)}, u32[]{:S(2)}) collective-permute-start(bf16[1536,256]{1,0:T(8,128)(2,1)S(1)} %copy-done.1), channel_id=1, source_target_pairs={{28,0},{13,2},{27,3},{9,5},{31,7},{4,8},{21,10},{3,11},{17,13},{7,... | collective-permute-start | bytes 2359304 | tf_op jit(solution)/shard_map/ppermute | solution.py:28
  16.3 22.3 %collective-permute-start.3 = (bf16[1536,256]{1,0:T(8,128)(2,1)S(1)}, bf16[1536,256]{1,0:T(8,128)(2,1)S(1)}, u32[]{:S(2)}, u32[]{:S(2)}) collective-permute-start(bf16[1536,256]{1,0:T(8,128)(2,1)S(1)} %collective-permute-done.refs_1_.refs_0_), channel_id=1, source_target_pairs={{6,3},{2,6},{14,11},{10,14},{22,19},{18,22},{30,27},{26,30}} | collective-permute-start | bytes 2359304 | tf_op jit(solution)/shard_map/ppermute | solution.py:28
  39.1 1.8 %collective-permute-start.5 = (f32[384,256]{1,0:T(8,128)S(1)}, f32[384,256]{1,0:T(8,128)S(1)}, u32[]{:S(2)}, u32[]{:S(2)}) collective-permute-start(f32[384,256]{1,0:T(8,128)S(1)} %send_other_side.1), channel_id=1, source_target_pairs={{0,1},{1,0},{2,3},{3,2},{4,5},{5,4},{6,7},{7,6},{8,9},{9,8},{10,11... | collective-permute-start | bytes 1179656 | tf_op jit(solution)/shard_map/ppermute | solution.py:33
  39.7 4.3 %collective-permute-start.4 = (f32[384,256]{1,0:T(8,128)S(1)}, f32[384,256]{1,0:T(8,128)S(1)}, u32[]{:S(2)}, u32[]{:S(2)}) collective-permute-start(f32[384,256]{1,0:T(8,128)S(1)} %send_this_side.1), channel_id=1, source_target_pairs={{0,1},{1,0},{2,3},{3,2},{4,5},{5,4},{6,7},{7,6},{8,9},{9,8},{10,11... | collective-permute-start | bytes 1179656 | tf_op jit(solution)/shard_map/ppermute | solution.py:33
  40.9 3.1 %copy-start.3 = (bf16[256,256]{1,0:T(8,128)(2,1)S(1)}, bf16[256,256]{1,0:T(8,128)(2,1)}, u32[]{:S(2)}) copy-start(bf16[256,256]{1,0:T(8,128)(2,1)} %weight_self.1) | copy-start | bytes 393220
  41.4 7.8 %collective-permute-start.6 = (bf16[384,256]{1,0:T(8,128)(2,1)S(1)}, bf16[384,256]{1,0:T(8,128)(2,1)S(1)}, u32[]{:S(2)}, u32[]{:S(2)}) collective-permute-start(bf16[384,256]{1,0:T(8,128)(2,1)S(1)} %mid_rows.1), channel_id=1, source_target_pairs={{0,2},{1,3},{2,0},{3,1},{4,6},{5,7},{6,4},{7,5},{8,10},{9,11},{10,... | collective-permute-start | bytes 589832 | tf_op jit(solution)/shard_map/ppermute | solution.py:33
  44.0 5.2 %copy-start.2 = (bf16[384,256]{1,0:T(8,128)(2,1)S(1)}, bf16[384,256]{1,0:T(8,128)(2,1)}, u32[]{:S(2)}) copy-start(bf16[384,256]{1,0:T(8,128)(2,1)} %cotangent.1) | copy-start | bytes 589828
  44.0 5.2 %copy-start.4 = (bf16[256,256]{1,0:T(8,128)(2,1)S(1)}, bf16[256,256]{1,0:T(8,128)(2,1)}, u32[]{:S(2)}) copy-start(bf16[256,256]{1,0:T(8,128)(2,1)} %weight_neigh.1) | copy-start | bytes 393220
  50.2 1.5 %collective-permute-start.7 = (f32[256,256]{1,0:T(8,128)S(1)}, f32[256,256]{1,0:T(8,128)S(1)}, u32[]{:S(2)}, u32[]{:S(2)}) collective-permute-start(f32[256,256]{1,0:T(8,128)S(1)} %get-tuple-element.36), channel_id=1, source_target_pairs={{0,1},{1,0},{2,3},{3,2},{4,5},{5,4},{6,7},{7,6},{8,9},{9,8},{10,11... | collective-permute-start | bytes 786440 | tf_op jit(solution)/shard_map/ppermute | solution.py:33
  73.2 1.3 %collective-permute-start.8 = (bf16[256,256]{1,0:T(8,128)(2,1)S(1)}, bf16[256,256]{1,0:T(8,128)(2,1)S(1)}, u32[]{:S(2)}, u32[]{:S(2)}) collective-permute-start(bf16[256,256]{1,0:T(8,128)(2,1)S(1)} %bitcast.36), channel_id=1, source_target_pairs={{0,1},{1,0},{2,3},{3,2},{4,5},{5,4},{6,7},{7,6},{8,9},{9,8},{10,11... | collective-permute-start | bytes 393224 | tf_op jit(solution)/shard_map/ppermute | solution.py:33

commit v7 on v6

--- a/solution.py
+++ b/solution.py
@@ -225,14 +225,8 @@
     either(pick_late(), found, run)
 
 
-def mid_kernel(received, begun, dense, *refs):
-    found, out = refs[:-1], refs[-1]
-
-    def run(block):
-        total = begun[...] + jnp.dot(dense[...], block[...], preferred_element_type=F32)
-        out[...] = (total + received[...]).astype(out.dtype)
-
-    either(pick_late(), found, run)
+def across_kernel(mid, received, out):
+    out[...] = (mid[...] + received[...]).astype(out.dtype)
 
 
 def own_kernel(features, received, weight_self, begun, dense, *refs):
@@ -350,25 +344,21 @@
         "early_rows",
         (steps - 1) * nodes * per_row,
     )
-    send = [
-        vmem_call(limit, rows_kernel, quarter, (begun, dense, *late_found), name, part * per_row)
-        for begun, dense, name in zip(begun_send, dense_send, ("send_other_side", "send_this_side"))
-    ]
-    received = [rep_exchange(rows, groups, 0) for rows in send]
-    across = vmem_call(
-        limit,
-        mid_kernel,
-        jax.ShapeDtypeStruct((part, width), BF16),
-        (received[0], begun_mid, dense_mid, *late_found),
-        "mid_rows",
-        part * per_row,
-    )
+    def late_rows(begun, dense, name):
+        operands = (begun, dense, *late_found)
+        return vmem_call(limit, rows_kernel, quarter, operands, name, part * per_row)
+
+    other_side = rep_exchange(late_rows(begun_send[0], dense_send[0], "send_other_side"), groups, 0)
+    mid = late_rows(begun_mid, dense_mid, "mid_rows")
+    across_shape = jax.ShapeDtypeStruct((part, width), BF16)
+    across = vmem_call(limit, across_kernel, across_shape, (mid, other_side), "across")
     side = rep_exchange(across, groups, 1)
+    this_side = rep_exchange(late_rows(begun_send[1], dense_send[1], "send_this_side"), groups, 0)
     own, projected = vmem_call(
         limit,
         own_kernel,
         (quarter, quarter),
-        (features, received[1], weight_self, begun_own, dense_own, *late_found),
+        (features, this_side, weight_self, begun_own, dense_own, *late_found),
         "own_rows",
         part * per_row,
     )

time: 76.2 us -> 76.1 us (level)
  waiting for transfers between devices: 21.8 us -> 25.4 us
  starting transfers between devices: 12.5 us -> 9.53 us
  blocking collectives: 21.4 us -> 19.9 us
    ppermute x5, starting transfers between devices: 3.45 us -> 0.9 us  [rep_exchange(): return lax.ppermute(value, 'rep', route)]
    ppermute x4, waiting for transfers between devices: 14 us -> 16.4 us  [flat_permute(): return lax.ppermute(value, AXES, route)]
    all_to_all x1, blocking collectives: 11.4 us -> 9.93 us  [all_reduce_grads(): terms = lax.all_to_all(chip, AXES, 0, 0, tiled=True)]
    ppermute x5, waiting for transfers between devices: 7.8 us -> 9.08 us  [rep_exchange(): return lax.ppermute(value, 'rep', route)]
    pallas_call x6 -> x7, Pallas kernels: 4.6 us -> 4.59 us  [vmem_call(): pl.pallas_call(kernel, out_shape=out_shape, in_specs=[vmem] * len(operand...]
  transfers between devices with their start and end apart: 9 -> 9, of which waited for: 6 -> 7; matrix products, arithmetic and copies ran while one was open for 2% -> 2% of each run, Pallas kernels for 16% -> 17%
where the time goes in v7:
time: 76.1 us; the launch traced here: 74.8 us
  waiting for transfers between devices  25.4 us (33%)
  blocking collectives  19.9 us (26%)
  Pallas kernels  14.1 us (19%)
  starting transfers between devices  9.53 us (13%)
  local copies, waits for them, and re-layouts  3.4 us (4%)
  other arithmetic  1.68 us (2%)
  between operations  0.83 us (1%)
    ppermute x4, waiting for transfers between devices, flat_permute(): return lax.ppermute(value, AXES, route)  16.4 us
    all_to_all x1, blocking collectives, all_reduce_grads(): terms = lax.all_to_all(chip, AXES, 0, 0, tiled=True)  9.93 us
    all_to_all x1, blocking collectives, all_reduce_grads(): mine = lax.all_to_all(spread, AXES, 0, 0, tiled=True)  9.93 us
    pallas_call x2, Pallas kernels, densify(): pl.pallas_call(functools.partial(densify_kernel, pieces), out_shape=out_s...  9.51 us
    ppermute x5, waiting for transfers between devices, rep_exchange(): return lax.ppermute(value, 'rep', route)  9.08 us
    ppermute x4, starting transfers between devices, flat_permute(): return lax.ppermute(value, AXES, route)  8.63 us
    pallas_call x7, Pallas kernels, vmem_call(): pl.pallas_call(kernel, out_shape=out_shape, in_specs=[vmem] * len(operand...  4.59 us
    unnamed x10, local copies, waits for them, and re-layouts  2.65 us
  transfers between devices with their start and end apart: 9, of which 7 were waited for; matrix products, arithmetic and copies ran while one was open for 2% of the time, Pallas kernels for 17%

profile of v7, /device:TPU:0, one launch (start us, length us, event | category | flops | bytes accessed | tf_op | source)
XLA Modules:
  0.0 74.8 jit_solution(17155794526491927896)
XLA Ops:
  0.6 0.7 collective-permute-start
  1.4 0.7 copy.11
  2.1 0.7 fusion.7
  2.9 0.1 pad_add_fusion.table
  2.9 0.0 copy-start
  2.9 2.6 %copy-done = bf16[1,1,2,88,128,128]{5,4,3,2,1,0:T(8,128)(2,1)S(1)} copy-done((bf16[1,1,2,88,128,128]{5,4,3,2,1,0:T(8,128)(2,1)S(1)}, bf16[1,1,2,88,128,128]{5,4,3,2,1,0:T(8,128)(2,1)}, u32[]{:S(2)}) %copy-start) | copy-done | bytes 5767192
  5.6 0.0 copy-start.1
  5.6 3.1 %densify_send.1 = (bf16[384,1536]{1,0:T(8,128)(2,1)S(1)}, bf16[384,1536]{1,0:T(8,128)(2,1)S(1)}) custom-call(s32[2,89]{1,0:T(2,128)S(1)} %pad_add_fusion.table, bf16[2,88,128,128]{3,2,1,0:T(8,128)(2,1)S(1)} %bitcast.32), custom_call_target="tpu_custom_call" | custom-call | bytes 7077888 | tf_op jit(solution)/shard_map/densify_send/pallas_call | solution.py:158
  8.7 0.0 copy-done.1
  8.7 5.9 %collective-permute-start.1 = (bf16[1536,256]{1,0:T(8,128)(2,1)S(1)}, bf16[1536,256]{1,0:T(8,128)(2,1)S(1)}, u32[]{:S(2)}, u32[]{:S(2)}) collective-permute-start(bf16[1536,256]{1,0:T(8,128)(2,1)S(1)} %copy-done.1), channel_id=1, source_target_pairs={{11,1},{15,5},{24,7},{19,9},{23,13},{0,15},{27,17},{31,21},{8,23},... | collective-permute-start | bytes 2359304 | tf_op jit(solution)/shard_map/ppermute | solution.py:28
  14.6 1.3 %collective-permute-start.2 = (bf16[1536,256]{1,0:T(8,128)(2,1)S(1)}, bf16[1536,256]{1,0:T(8,128)(2,1)S(1)}, u32[]{:S(2)}, u32[]{:S(2)}) collective-permute-start(bf16[1536,256]{1,0:T(8,128)(2,1)S(1)} %copy-done.1), channel_id=1, source_target_pairs={{28,0},{13,2},{27,3},{9,5},{31,7},{4,8},{21,10},{3,11},{17,13},{7,... | collective-permute-start | bytes 2359304 | tf_op jit(solution)/shard_map/ppermute | solution.py:28
  15.9 0.0 collective-permute-done.refs_1_.refs_0_
  15.9 0.7 collective-permute-start.3
  16.7 6.4 %densify_rest.1 = (bf16[1,1536,1536]{2,1,0:T(8,128)(2,1)S(1)}, bf16[384,1536]{1,0:T(8,128)(2,1)S(1)}, bf16[384,1536]{1,0:T(8,128)(2,1)S(1)}) custom-call(s32[2,89]{1,0:T(2,128)S(1)} %pad_add_fusion.table, bf16[2,88,128,128]{3,2,1,0:T(8,128)(2,1)S(1)} %bitcast.33), custom_call_target="tpu_custom_call" | custom-call | bytes 21233664 | tf_op jit(solution)/shard_map/densify_rest/pallas_call | solution.py:158
  23.1 8.5 %collective-permute-done.1.refs_2_ = bf16[1536,256]{1,0:T(8,128)(2,1)S(1)} collective-permute-done((bf16[1536,256]{1,0:T(8,128)(2,1)S(1)}, bf16[1536,256]{1,0:T(8,128)(2,1)S(1)}, u32[]{:S(2)}, u32[]{:S(2)}) %collective-permute-start.1) | collective-permute-done | bytes 786464 | tf_op jit(solution)/shard_map/ppermute | solution.py:28
  31.6 7.8 %collective-permute-done.2.refs_3_ = bf16[1536,256]{1,0:T(8,128)(2,1)S(1)} collective-permute-done((bf16[1536,256]{1,0:T(8,128)(2,1)S(1)}, bf16[1536,256]{1,0:T(8,128)(2,1)S(1)}, u32[]{:S(2)}, u32[]{:S(2)}) %collective-permute-start.2) | collective-permute-done | bytes 786464 | tf_op jit(solution)/shard_map/ppermute | solution.py:28
  39.4 1.4 %early_rows.1 = (f32[384,256]{1,0:T(8,128)S(1)}, f32[384,256]{1,0:T(8,128)S(1)}, f32[384,256]{1,0:T(8,128)S(1)}, f32[384,256]{1,0:T(8,128)S(1)}) custom-call(bf16[1,1536,1536]{2,1,0:T(8,128)(2,1)S(1)} %get-tuple-element.20.dense, bf16[1536,256]{1,0:T(8,128)(2,1)S(1)} %copy-done.1, bf16[1536,256]{1,0:T(8,128)(2,1)S(1)} %collective-permute-done.refs_1_.refs_0_, ...), custom_call_target="tpu_custom_call" | custom-call | flops 1207959552 | bytes 9437184 | tf_op jit(solution)/shard_map/early_rows/pallas_call | solution.py:249
  40.8 0.0 collective-permute-done.3.refs_1_
  40.8 0.5 send_other_side.1
  41.3 0.1 collective-permute-start.5
  41.4 0.5 send_this_side.1
  41.9 0.5 collective-permute-start.4
  42.5 0.0 copy-start.3
  42.5 0.5 mid_rows.1.mid
  42.9 0.2 collective-permute-done.5.received
  43.2 0.1 collective-permute-start.6
  43.2 0.6 collective-permute-done.4.received
  43.8 0.0 copy-done.3
  43.8 0.0 copy-start.2
  43.8 0.0 copy-start.4
  43.8 0.7 own_rows.1
  44.5 5.7 %collective-permute-done.6.side = bf16[384,256]{1,0:T(8,128)(2,1)S(1)} collective-permute-done((bf16[384,256]{1,0:T(8,128)(2,1)S(1)}, bf16[384,256]{1,0:T(8,128)(2,1)S(1)}, u32[]{:S(2)}, u32[]{:S(2)}) %collective-permute-start.6) | collective-permute-done | bytes 196640 | tf_op jit(solution)/shard_map/ppermute | solution.py:33
  50.2 0.0 copy-done.2
  50.2 0.0 copy-done.4
  50.2 1.0 %layer.1 = (bf16[384,256]{1,0:T(8,128)(2,1)}, f32[256,256]{1,0:T(8,128)S(1)}, f32[256,256]{1,0:T(8,128)S(1)}) custom-call(bf16[1536,256]{1,0:T(8,128)(2,1)S(1)} %copy-done.1, f32[384,256]{1,0:T(8,128)S(1)} %get-tuple-element.28.own, bf16[384,256]{1,0:T(8,128)(2,1)S(1)} %collective-permute-done.6.side, f32[384,256]{1,0:T(8,128)S(1)} %get-tuple-element.33.projected, ...), custom_call_target="tpu_custom_call" | custom-call | flops 150994944 | bytes 2818048 | tf_op jit(solution)/shard_map/layer/pallas_call | solution.py:249
  51.2 0.0 collective-permute-start.7
  51.2 1.5 %collective-permute-done.7 = f32[256,256]{1,0:T(8,128)S(1)} collective-permute-done((f32[256,256]{1,0:T(8,128)S(1)}, f32[256,256]{1,0:T(8,128)S(1)}, u32[]{:S(2)}, u32[]{:S(2)}) %collective-permute-start.7) | collective-permute-done | bytes 262176 | tf_op jit(solution)/shard_map/ppermute | solution.py:33
  52.8 9.9 %all_to_all.21 = bf16[32,8,256]{2,1,0:T(8,128)(2,1)S(1)} all-to-all(bf16[32,8,256]{2,1,0:T(8,128)(2,1)S(1)} %fusion), channel_id=1, replica_groups=mesh['dom'=8,'rep'=4] {'dom','rep'}, dimensions={0} | all-to-all | bytes 262144 | tf_op jit(solution)/shard_map/all_to_all | solution.py:283
  62.7 9.9 %all_to_all.22 = bf16[32,8,256]{2,1,0:T(8,128)(2,1)S(1)} all-to-all(bf16[32,8,256]{2,1,0:T(8,128)(2,1)S(1)} %bitcast.35), channel_id=1, replica_groups=mesh['dom'=8,'rep'=4] {'dom','rep'}, dimensions={0} | all-to-all | bytes 262144 | tf_op jit(solution)/shard_map/all_to_all | solution.py:286
  72.7 0.2 collective-permute-start.8
  72.9 1.1 %collective-permute-done.8 = bf16[256,256]{1,0:T(8,128)(2,1)S(1)} collective-permute-done((bf16[256,256]{1,0:T(8,128)(2,1)S(1)}, bf16[256,256]{1,0:T(8,128)(2,1)S(1)}, u32[]{:S(2)}, u32[]{:S(2)}) %collective-permute-start.8) | collective-permute-done | bytes 131104 | tf_op jit(solution)/shard_map/ppermute | solution.py:33
  74.0 0.8 %select_convert_fusion = (f32[256,256]{1,0:T(8,128)}, f32[256,256]{1,0:T(8,128)}) fusion(bf16[256,256]{1,0:T(8,128)(2,1)S(1)} %collective-permute-done.8, pred[]{:T(512)S(6)} %eq.40, bf16[32,8,256]{2,1,0:T(8,128)(2,1)S(1)} %all_to_all.22), kind=kLoop, calls=%fused_computation.2 | loop fusion | flops 262144 | bytes 786433 | tf_op jit(solution)/shard_map/convert_element_type | solution.py:290
  (4 shorter events, 0.1 us)
Async XLA Ops:
  0.6 15.3 %collective-permute-start = (bf16[1536,256]{1,0:T(8,128)(2,1)}, bf16[1536,256]{1,0:T(8,128)(2,1)S(1)}, u32[]{:S(2)}, u32[]{:S(2)}) collective-permute-start(bf16[1536,256]{1,0:T(8,128)(2,1)} %features.3), channel_id=1, source_target_pairs={{5,1},{18,2},{1,4},{22,6},{13,9},{24,10},{9,12},{28,14},{21,17},{2... | collective-permute-start | bytes 2359304 | tf_op jit(solution)/shard_map/ppermute | solution.py:28
  2.9 2.6 %copy-start = (bf16[1,1,2,88,128,128]{5,4,3,2,1,0:T(8,128)(2,1)S(1)}, bf16[1,1,2,88,128,128]{5,4,3,2,1,0:T(8,128)(2,1)}, u32[]{:S(2)}) copy-start(bf16[1,1,2,88,128,128]{5,4,3,2,1,0:T(8,128)(2,1)} %param.9) | copy-start | bytes 17301508
  5.6 3.1 %copy-start.1 = (bf16[1536,256]{1,0:T(8,128)(2,1)S(1)}, bf16[1536,256]{1,0:T(8,128)(2,1)}, u32[]{:S(2)}) copy-start(bf16[1536,256]{1,0:T(8,128)(2,1)} %features.3) | copy-start | bytes 2359300
  8.7 22.9 %collective-permute-start.1 = (bf16[1536,256]{1,0:T(8,128)(2,1)S(1)}, bf16[1536,256]{1,0:T(8,128)(2,1)S(1)}, u32[]{:S(2)}, u32[]{:S(2)}) collective-permute-start(bf16[1536,256]{1,0:T(8,128)(2,1)S(1)} %copy-done.1), channel_id=1, source_target_pairs={{11,1},{15,5},{24,7},{19,9},{23,13},{0,15},{27,17},{31,21},{8,23},... | collective-permute-start | bytes 2359304 | tf_op jit(solution)/shard_map/ppermute | solution.py:28
  14.6 24.8 %collective-permute-start.2 = (bf16[1536,256]{1,0:T(8,128)(2,1)S(1)}, bf16[1536,256]{1,0:T(8,128)(2,1)S(1)}, u32[]{:S(2)}, u32[]{:S(2)}) collective-permute-start(bf16[1536,256]{1,0:T(8,128)(2,1)S(1)} %copy-done.1), channel_id=1, source_target_pairs={{28,0},{13,2},{27,3},{9,5},{31,7},{4,8},{21,10},{3,11},{17,13},{7,... | collective-permute-start | bytes 2359304 | tf_op jit(solution)/shard_map/ppermute | solution.py:28
  15.9 24.9 %collective-permute-start.3 = (bf16[1536,256]{1,0:T(8,128)(2,1)S(1)}, bf16[1536,256]{1,0:T(8,128)(2,1)S(1)}, u32[]{:S(2)}, u32[]{:S(2)}) collective-permute-start(bf16[1536,256]{1,0:T(8,128)(2,1)S(1)} %collective-permute-done.refs_1_.refs_0_), channel_id=1, source_target_pairs={{6,3},{2,6},{14,11},{10,14},{22,19},{18,22},{30,27},{26,30}} | collective-permute-start | bytes 2359304 | tf_op jit(solution)/shard_map/ppermute | solution.py:28
  41.3 1.8 %collective-permute-start.5 = (f32[384,256]{1,0:T(8,128)S(1)}, f32[384,256]{1,0:T(8,128)S(1)}, u32[]{:S(2)}, u32[]{:S(2)}) collective-permute-start(f32[384,256]{1,0:T(8,128)S(1)} %send_other_side.1), channel_id=1, source_target_pairs={{0,1},{1,0},{2,3},{3,2},{4,5},{5,4},{6,7},{7,6},{8,9},{9,8},{10,11... | collective-permute-start | bytes 1179656 | tf_op jit(solution)/shard_map/ppermute | solution.py:33
  41.9 1.9 %collective-permute-start.4 = (f32[384,256]{1,0:T(8,128)S(1)}, f32[384,256]{1,0:T(8,128)S(1)}, u32[]{:S(2)}, u32[]{:S(2)}) collective-permute-start(f32[384,256]{1,0:T(8,128)S(1)} %send_this_side.1), channel_id=1, source_target_pairs={{0,1},{1,0},{2,3},{3,2},{4,5},{5,4},{6,7},{7,6},{8,9},{9,8},{10,11... | collective-permute-start | bytes 1179656 | tf_op jit(solution)/shard_map/ppermute | solution.py:33
  42.5 1.4 %copy-start.3 = (bf16[256,256]{1,0:T(8,128)(2,1)S(1)}, bf16[256,256]{1,0:T(8,128)(2,1)}, u32[]{:S(2)}) copy-start(bf16[256,256]{1,0:T(8,128)(2,1)} %weight_self.1) | copy-start | bytes 393220
  43.2 7.0 %collective-permute-start.6 = (bf16[384,256]{1,0:T(8,128)(2,1)S(1)}, bf16[384,256]{1,0:T(8,128)(2,1)S(1)}, u32[]{:S(2)}, u32[]{:S(2)}) collective-permute-start(bf16[384,256]{1,0:T(8,128)(2,1)S(1)} %across.1), channel_id=1, source_target_pairs={{0,2},{1,3},{2,0},{3,1},{4,6},{5,7},{6,4},{7,5},{8,10},{9,11},{10,... | collective-permute-start | bytes 589832 | tf_op jit(solution)/shard_map/ppermute | solution.py:33
  43.8 6.4 %copy-start.2 = (bf16[384,256]{1,0:T(8,128)(2,1)S(1)}, bf16[384,256]{1,0:T(8,128)(2,1)}, u32[]{:S(2)}) copy-start(bf16[384,256]{1,0:T(8,128)(2,1)} %cotangent.1) | copy-start | bytes 589828
  43.8 6.4 %copy-start.4 = (bf16[256,256]{1,0:T(8,128)(2,1)S(1)}, bf16[256,256]{1,0:T(8,128)(2,1)}, u32[]{:S(2)}) copy-start(bf16[256,256]{1,0:T(8,128)(2,1)} %weight_neigh.1) | copy-start | bytes 393220
  51.2 1.5 %collective-permute-start.7 = (f32[256,256]{1,0:T(8,128)S(1)}, f32[256,256]{1,0:T(8,128)S(1)}, u32[]{:S(2)}, u32[]{:S(2)}) collective-permute-start(f32[256,256]{1,0:T(8,128)S(1)} %get-tuple-element.36), channel_id=1, source_target_pairs={{0,1},{1,0},{2,3},{3,2},{4,5},{5,4},{6,7},{7,6},{8,9},{9,8},{10,11... | collective-permute-start | bytes 786440 | tf_op jit(solution)/shard_map/ppermute | solution.py:33
  72.7 1.3 %collective-permute-start.8 = (bf16[256,256]{1,0:T(8,128)(2,1)S(1)}, bf16[256,256]{1,0:T(8,128)(2,1)S(1)}, u32[]{:S(2)}, u32[]{:S(2)}) collective-permute-start(bf16[256,256]{1,0:T(8,128)(2,1)S(1)} %bitcast.36), channel_id=1, source_target_pairs={{0,1},{1,0},{2,3},{3,2},{4,5},{5,4},{6,7},{7,6},{8,9},{9,8},{10,11... | collective-permute-start | bytes 393224 | tf_op jit(solution)/shard_map/ppermute | solution.py:33

commit v8 on v7

--- a/solution.py
+++ b/solution.py
@@ -69,9 +69,9 @@
 
     def third(self, p, r):
         if r == self.last:
-            return p + 2 * r, self.last
+            return p + 2 * r, self.last if p % 2 else 1
         if p % 2:
-            return (p + 2 * r - 1, 1) if r == 1 else None
+            return (p + 2 * r - 1, self.last) if r == 1 else None
         return None if r == 1 else (p + 2 * r - 1, 1 if r else 0)
 
 

time: 76.1 us -> 76.2 us (level); the launches traced: 74.8 us -> 76.9 us
  waiting for transfers between devices: 25.4 us -> 22 us
  blocking collectives: 19.9 us -> 23.2 us
  starting transfers between devices: 9.53 us -> 11.4 us
    all_to_all x1, blocking collectives: 9.93 us -> 13.2 us  [all_reduce_grads(): terms = lax.all_to_all(chip, AXES, 0, 0, tiled=True)]
    ppermute x5, starting transfers between devices: 0.9 us -> 3.02 us  [rep_exchange(): return lax.ppermute(value, 'rep', route)]
    ppermute x4, waiting for transfers between devices: 16.4 us -> 14.5 us  [flat_permute(): return lax.ppermute(value, AXES, route)]
    ppermute x5, waiting for transfers between devices: 9.08 us -> 7.53 us  [rep_exchange(): return lax.ppermute(value, 'rep', route)]
  transfers between devices with their start and end apart: 9 -> 9, of which waited for: 7 -> 6; matrix products, arithmetic and copies ran while one was open for 2% -> 2% of each run, Pallas kernels for 17% -> 17%
where the time goes in v8:
time: 76.2 us; the launch traced here: 76.9 us
  blocking collectives  23.2 us (30%)
  waiting for transfers between devices  22 us (29%)
  Pallas kernels  14.4 us (19%)
  starting transfers between devices  11.4 us (15%)
  local copies, waits for them, and re-layouts  3.4 us (4%)
  other arithmetic  1.68 us (2%)
  between operations  0.82 us (1%)
    ppermute x4, waiting for transfers between devices, flat_permute(): return lax.ppermute(value, AXES, route)  14.5 us
    all_to_all x1, blocking collectives, all_reduce_grads(): terms = lax.all_to_all(chip, AXES, 0, 0, tiled=True)  13.2 us
    all_to_all x1, blocking collectives, all_reduce_grads(): mine = lax.all_to_all(spread, AXES, 0, 0, tiled=True)  10 us
    pallas_call x2, Pallas kernels, densify(): pl.pallas_call(functools.partial(densify_kernel, pieces), out_shape=out_s...  9.77 us
    ppermute x4, starting transfers between devices, flat_permute(): return lax.ppermute(value, AXES, route)  8.42 us
    ppermute x5, waiting for transfers between devices, rep_exchange(): return lax.ppermute(value, 'rep', route)  7.53 us
    pallas_call x7, Pallas kernels, vmem_call(): pl.pallas_call(kernel, out_shape=out_shape, in_specs=[vmem] * len(operand...  4.63 us
    ppermute x5, starting transfers between devices, rep_exchange(): return lax.ppermute(value, 'rep', route)  3.02 us
  transfers between devices with their start and end apart: 9, of which 6 were waited for; matrix products, arithmetic and copies ran while one was open for 2% of the time, Pallas kernels for 17%

profile of v8, /device:TPU:0, one launch (start us, length us, event | category | flops | bytes accessed | tf_op | source)
XLA Modules:
  0.0 76.9 jit_solution(8718150452305268084)
XLA Ops:
  0.6 0.7 collective-permute-start
  1.4 0.7 copy.11
  2.1 0.7 fusion.7
  2.9 0.1 pad_add_fusion.table
  2.9 0.0 copy-start
  2.9 2.6 %copy-done = bf16[1,1,2,88,128,128]{5,4,3,2,1,0:T(8,128)(2,1)S(1)} copy-done((bf16[1,1,2,88,128,128]{5,4,3,2,1,0:T(8,128)(2,1)S(1)}, bf16[1,1,2,88,128,128]{5,4,3,2,1,0:T(8,128)(2,1)}, u32[]{:S(2)}) %copy-start) | copy-done | bytes 5767192
  5.6 0.0 copy-start.1
  5.6 3.3 %densify_send.1 = (bf16[384,1536]{1,0:T(8,128)(2,1)S(1)}, bf16[384,1536]{1,0:T(8,128)(2,1)S(1)}) custom-call(s32[2,89]{1,0:T(2,128)S(1)} %pad_add_fusion.table, bf16[2,88,128,128]{3,2,1,0:T(8,128)(2,1)S(1)} %bitcast.32), custom_call_target="tpu_custom_call" | custom-call | bytes 7077888 | tf_op jit(solution)/shard_map/densify_send/pallas_call | solution.py:158
  8.9 0.0 copy-done.1
  8.9 5.7 %collective-permute-start.1 = (bf16[1536,256]{1,0:T(8,128)(2,1)S(1)}, bf16[1536,256]{1,0:T(8,128)(2,1)S(1)}, u32[]{:S(2)}, u32[]{:S(2)}) collective-permute-start(bf16[1536,256]{1,0:T(8,128)(2,1)S(1)} %copy-done.1), channel_id=1, source_target_pairs={{11,1},{15,5},{24,7},{19,9},{23,13},{0,15},{27,17},{31,21},{8,23},... | collective-permute-start | bytes 2359304 | tf_op jit(solution)/shard_map/ppermute | solution.py:28
  14.6 1.3 %collective-permute-start.2 = (bf16[1536,256]{1,0:T(8,128)(2,1)S(1)}, bf16[1536,256]{1,0:T(8,128)(2,1)S(1)}, u32[]{:S(2)}, u32[]{:S(2)}) collective-permute-start(bf16[1536,256]{1,0:T(8,128)(2,1)S(1)} %copy-done.1), channel_id=1, source_target_pairs={{28,0},{13,2},{25,3},{11,5},{31,7},{4,8},{21,10},{1,11},{19,13},{7... | collective-permute-start | bytes 2359304 | tf_op jit(solution)/shard_map/ppermute | solution.py:28
  15.9 0.0 collective-permute-done.refs_1_.refs_0_
  15.9 0.7 collective-permute-start.3
  16.6 6.5 %densify_rest.1 = (bf16[1,1536,1536]{2,1,0:T(8,128)(2,1)S(1)}, bf16[384,1536]{1,0:T(8,128)(2,1)S(1)}, bf16[384,1536]{1,0:T(8,128)(2,1)S(1)}) custom-call(s32[2,89]{1,0:T(2,128)S(1)} %pad_add_fusion.table, bf16[2,88,128,128]{3,2,1,0:T(8,128)(2,1)S(1)} %bitcast.33), custom_call_target="tpu_custom_call" | custom-call | bytes 21233664 | tf_op jit(solution)/shard_map/densify_rest/pallas_call | solution.py:158
  23.1 8.6 %collective-permute-done.1.refs_2_ = bf16[1536,256]{1,0:T(8,128)(2,1)S(1)} collective-permute-done((bf16[1536,256]{1,0:T(8,128)(2,1)S(1)}, bf16[1536,256]{1,0:T(8,128)(2,1)S(1)}, u32[]{:S(2)}, u32[]{:S(2)}) %collective-permute-start.1) | collective-permute-done | bytes 786464 | tf_op jit(solution)/shard_map/ppermute | solution.py:28
  31.7 5.9 %collective-permute-done.2.refs_3_ = bf16[1536,256]{1,0:T(8,128)(2,1)S(1)} collective-permute-done((bf16[1536,256]{1,0:T(8,128)(2,1)S(1)}, bf16[1536,256]{1,0:T(8,128)(2,1)S(1)}, u32[]{:S(2)}, u32[]{:S(2)}) %collective-permute-start.2) | collective-permute-done | bytes 786464 | tf_op jit(solution)/shard_map/ppermute | solution.py:28
  37.5 1.4 %early_rows.1 = (f32[384,256]{1,0:T(8,128)S(1)}, f32[384,256]{1,0:T(8,128)S(1)}, f32[384,256]{1,0:T(8,128)S(1)}, f32[384,256]{1,0:T(8,128)S(1)}) custom-call(bf16[1,1536,1536]{2,1,0:T(8,128)(2,1)S(1)} %get-tuple-element.20.dense, bf16[1536,256]{1,0:T(8,128)(2,1)S(1)} %copy-done.1, bf16[1536,256]{1,0:T(8,128)(2,1)S(1)} %collective-permute-done.refs_1_.refs_0_, ...), custom_call_target="tpu_custom_call" | custom-call | flops 1207959552 | bytes 9437184 | tf_op jit(solution)/shard_map/early_rows/pallas_call | solution.py:249
  38.9 0.0 collective-permute-done.3.refs_1_
  39.0 0.5 send_other_side.1
  39.5 0.1 collective-permute-start.5
  39.5 0.5 send_this_side.1
  40.1 0.5 collective-permute-start.4
  40.6 0.0 copy-start.3
  40.6 0.5 mid_rows.1.mid
  41.1 0.2 collective-permute-done.5.received
  41.3 2.2 %collective-permute-start.6 = (bf16[384,256]{1,0:T(8,128)(2,1)S(1)}, bf16[384,256]{1,0:T(8,128)(2,1)S(1)}, u32[]{:S(2)}, u32[]{:S(2)}) collective-permute-start(bf16[384,256]{1,0:T(8,128)(2,1)S(1)} %across.1), channel_id=1, source_target_pairs={{0,2},{1,3},{2,0},{3,1},{4,6},{5,7},{6,4},{7,5},{8,10},{9,11},{10,... | collective-permute-start | bytes 589832 | tf_op jit(solution)/shard_map/ppermute | solution.py:33
  43.5 0.0 collective-permute-done.4.received
  43.5 0.0 copy-done.3
  43.5 0.0 copy-start.2
  43.5 0.0 copy-start.4
  43.5 0.7 own_rows.1
  44.2 4.7 %collective-permute-done.6.side = bf16[384,256]{1,0:T(8,128)(2,1)S(1)} collective-permute-done((bf16[384,256]{1,0:T(8,128)(2,1)S(1)}, bf16[384,256]{1,0:T(8,128)(2,1)S(1)}, u32[]{:S(2)}, u32[]{:S(2)}) %collective-permute-start.6) | collective-permute-done | bytes 196640 | tf_op jit(solution)/shard_map/ppermute | solution.py:33
  48.9 0.0 copy-done.2
  48.9 0.0 copy-done.4
  48.9 1.0 %layer.1 = (bf16[384,256]{1,0:T(8,128)(2,1)}, f32[256,256]{1,0:T(8,128)S(1)}, f32[256,256]{1,0:T(8,128)S(1)}) custom-call(bf16[1536,256]{1,0:T(8,128)(2,1)S(1)} %copy-done.1, f32[384,256]{1,0:T(8,128)S(1)} %get-tuple-element.28.own, bf16[384,256]{1,0:T(8,128)(2,1)S(1)} %collective-permute-done.6.side, f32[384,256]{1,0:T(8,128)S(1)} %get-tuple-element.33.projected, ...), custom_call_target="tpu_custom_call" | custom-call | flops 150994944 | bytes 2818048 | tf_op jit(solution)/shard_map/layer/pallas_call | solution.py:249
  49.9 0.0 collective-permute-start.7
  49.9 1.5 %collective-permute-done.7 = f32[256,256]{1,0:T(8,128)S(1)} collective-permute-done((f32[256,256]{1,0:T(8,128)S(1)}, f32[256,256]{1,0:T(8,128)S(1)}, u32[]{:S(2)}, u32[]{:S(2)}) %collective-permute-start.7) | collective-permute-done | bytes 262176 | tf_op jit(solution)/shard_map/ppermute | solution.py:33
  51.5 13.2 %all_to_all.21 = bf16[32,8,256]{2,1,0:T(8,128)(2,1)S(1)} all-to-all(bf16[32,8,256]{2,1,0:T(8,128)(2,1)S(1)} %fusion), channel_id=1, replica_groups=mesh['dom'=8,'rep'=4] {'dom','rep'}, dimensions={0} | all-to-all | bytes 262144 | tf_op jit(solution)/shard_map/all_to_all | solution.py:283
  64.7 10.0 %all_to_all.22 = bf16[32,8,256]{2,1,0:T(8,128)(2,1)S(1)} all-to-all(bf16[32,8,256]{2,1,0:T(8,128)(2,1)S(1)} %bitcast.35), channel_id=1, replica_groups=mesh['dom'=8,'rep'=4] {'dom','rep'}, dimensions={0} | all-to-all | bytes 262144 | tf_op jit(solution)/shard_map/all_to_all | solution.py:286
  74.7 0.2 collective-permute-start.8
  74.9 1.1 %collective-permute-done.8 = bf16[256,256]{1,0:T(8,128)(2,1)S(1)} collective-permute-done((bf16[256,256]{1,0:T(8,128)(2,1)S(1)}, bf16[256,256]{1,0:T(8,128)(2,1)S(1)}, u32[]{:S(2)}, u32[]{:S(2)}) %collective-permute-start.8) | collective-permute-done | bytes 131104 | tf_op jit(solution)/shard_map/ppermute | solution.py:33
  76.1 0.8 %select_convert_fusion = (f32[256,256]{1,0:T(8,128)}, f32[256,256]{1,0:T(8,128)}) fusion(bf16[256,256]{1,0:T(8,128)(2,1)S(1)} %collective-permute-done.8, pred[]{:T(512)S(6)} %eq.40, bf16[32,8,256]{2,1,0:T(8,128)(2,1)S(1)} %all_to_all.22), kind=kLoop, calls=%fused_computation.2 | loop fusion | flops 262144 | bytes 786433 | tf_op jit(solution)/shard_map/convert_element_type | solution.py:290
  (4 shorter events, 0.1 us)
Async XLA Ops:
  0.6 15.3 %collective-permute-start = (bf16[1536,256]{1,0:T(8,128)(2,1)}, bf16[1536,256]{1,0:T(8,128)(2,1)S(1)}, u32[]{:S(2)}, u32[]{:S(2)}) collective-permute-start(bf16[1536,256]{1,0:T(8,128)(2,1)} %features.3), channel_id=1, source_target_pairs={{5,1},{18,2},{1,4},{22,6},{13,9},{24,10},{9,12},{28,14},{21,17},{2... | collective-permute-start | bytes 2359304 | tf_op jit(solution)/shard_map/ppermute | solution.py:28
  2.9 2.6 %copy-start = (bf16[1,1,2,88,128,128]{5,4,3,2,1,0:T(8,128)(2,1)S(1)}, bf16[1,1,2,88,128,128]{5,4,3,2,1,0:T(8,128)(2,1)}, u32[]{:S(2)}) copy-start(bf16[1,1,2,88,128,128]{5,4,3,2,1,0:T(8,128)(2,1)} %param.9) | copy-start | bytes 17301508
  5.6 3.3 %copy-start.1 = (bf16[1536,256]{1,0:T(8,128)(2,1)S(1)}, bf16[1536,256]{1,0:T(8,128)(2,1)}, u32[]{:S(2)}) copy-start(bf16[1536,256]{1,0:T(8,128)(2,1)} %features.3) | copy-start | bytes 2359300
  8.9 22.8 %collective-permute-start.1 = (bf16[1536,256]{1,0:T(8,128)(2,1)S(1)}, bf16[1536,256]{1,0:T(8,128)(2,1)S(1)}, u32[]{:S(2)}, u32[]{:S(2)}) collective-permute-start(bf16[1536,256]{1,0:T(8,128)(2,1)S(1)} %copy-done.1), channel_id=1, source_target_pairs={{11,1},{15,5},{24,7},{19,9},{23,13},{0,15},{27,17},{31,21},{8,23},... | collective-permute-start | bytes 2359304 | tf_op jit(solution)/shard_map/ppermute | solution.py:28
  14.6 22.9 %collective-permute-start.2 = (bf16[1536,256]{1,0:T(8,128)(2,1)S(1)}, bf16[1536,256]{1,0:T(8,128)(2,1)S(1)}, u32[]{:S(2)}, u32[]{:S(2)}) collective-permute-start(bf16[1536,256]{1,0:T(8,128)(2,1)S(1)} %copy-done.1), channel_id=1, source_target_pairs={{28,0},{13,2},{25,3},{11,5},{31,7},{4,8},{21,10},{1,11},{19,13},{7... | collective-permute-start | bytes 2359304 | tf_op jit(solution)/shard_map/ppermute | solution.py:28
  15.9 23.0 %collective-permute-start.3 = (bf16[1536,256]{1,0:T(8,128)(2,1)S(1)}, bf16[1536,256]{1,0:T(8,128)(2,1)S(1)}, u32[]{:S(2)}, u32[]{:S(2)}) collective-permute-start(bf16[1536,256]{1,0:T(8,128)(2,1)S(1)} %collective-permute-done.refs_1_.refs_0_), channel_id=1, source_target_pairs={{6,3},{2,6},{14,11},{10,14},{22,19},{18,22},{30,27},{26,30}} | collective-permute-start | bytes 2359304 | tf_op jit(solution)/shard_map/ppermute | solution.py:28
  39.5 1.8 %collective-permute-start.5 = (f32[384,256]{1,0:T(8,128)S(1)}, f32[384,256]{1,0:T(8,128)S(1)}, u32[]{:S(2)}, u32[]{:S(2)}) collective-permute-start(f32[384,256]{1,0:T(8,128)S(1)} %send_other_side.1), channel_id=1, source_target_pairs={{0,1},{1,0},{2,3},{3,2},{4,5},{5,4},{6,7},{7,6},{8,9},{9,8},{10,11... | collective-permute-start | bytes 1179656 | tf_op jit(solution)/shard_map/ppermute | solution.py:33
  40.1 3.4 %collective-permute-start.4 = (f32[384,256]{1,0:T(8,128)S(1)}, f32[384,256]{1,0:T(8,128)S(1)}, u32[]{:S(2)}, u32[]{:S(2)}) collective-permute-start(f32[384,256]{1,0:T(8,128)S(1)} %send_this_side.1), channel_id=1, source_target_pairs={{0,1},{1,0},{2,3},{3,2},{4,5},{5,4},{6,7},{7,6},{8,9},{9,8},{10,11... | collective-permute-start | bytes 1179656 | tf_op jit(solution)/shard_map/ppermute | solution.py:33
  40.6 2.9 %copy-start.3 = (bf16[256,256]{1,0:T(8,128)(2,1)S(1)}, bf16[256,256]{1,0:T(8,128)(2,1)}, u32[]{:S(2)}) copy-start(bf16[256,256]{1,0:T(8,128)(2,1)} %weight_self.1) | copy-start | bytes 393220
  41.3 7.6 %collective-permute-start.6 = (bf16[384,256]{1,0:T(8,128)(2,1)S(1)}, bf16[384,256]{1,0:T(8,128)(2,1)S(1)}, u32[]{:S(2)}, u32[]{:S(2)}) collective-permute-start(bf16[384,256]{1,0:T(8,128)(2,1)S(1)} %across.1), channel_id=1, source_target_pairs={{0,2},{1,3},{2,0},{3,1},{4,6},{5,7},{6,4},{7,5},{8,10},{9,11},{10,... | collective-permute-start | bytes 589832 | tf_op jit(solution)/shard_map/ppermute | solution.py:33
  43.5 5.4 %copy-start.2 = (bf16[384,256]{1,0:T(8,128)(2,1)S(1)}, bf16[384,256]{1,0:T(8,128)(2,1)}, u32[]{:S(2)}) copy-start(bf16[384,256]{1,0:T(8,128)(2,1)} %cotangent.1) | copy-start | bytes 589828
  43.5 5.4 %copy-start.4 = (bf16[256,256]{1,0:T(8,128)(2,1)S(1)}, bf16[256,256]{1,0:T(8,128)(2,1)}, u32[]{:S(2)}) copy-start(bf16[256,256]{1,0:T(8,128)(2,1)} %weight_neigh.1) | copy-start | bytes 393220
  49.9 1.5 %collective-permute-start.7 = (f32[256,256]{1,0:T(8,128)S(1)}, f32[256,256]{1,0:T(8,128)S(1)}, u32[]{:S(2)}, u32[]{:S(2)}) collective-permute-start(f32[256,256]{1,0:T(8,128)S(1)} %get-tuple-element.36), channel_id=1, source_target_pairs={{0,1},{1,0},{2,3},{3,2},{4,5},{5,4},{6,7},{7,6},{8,9},{9,8},{10,11... | collective-permute-start | bytes 786440 | tf_op jit(solution)/shard_map/ppermute | solution.py:33
  74.7 1.3 %collective-permute-start.8 = (bf16[256,256]{1,0:T(8,128)(2,1)S(1)}, bf16[256,256]{1,0:T(8,128)(2,1)S(1)}, u32[]{:S(2)}, u32[]{:S(2)}) collective-permute-start(bf16[256,256]{1,0:T(8,128)(2,1)S(1)} %bitcast.36), channel_id=1, source_target_pairs={{0,1},{1,0},{2,3},{3,2},{4,5},{5,4},{6,7},{7,6},{8,9},{9,8},{10,11... | collective-permute-start | bytes 393224 | tf_op jit(solution)/shard_map/ppermute | solution.py:33
